TPU v7x, 32 devices: a whole 2x2x4 slice. The times are simulated.
32 devices in a mesh: box: 16 (over z, y, x), samp: 2 (over core).
Axes of the slice: x: 2, y: 2, z: 4, core: 2. Of those that a mesh axis runs over, the one named last changes fastest.
Arguments:
- child_pattern: bfloat16 [2, 2, 512, 2048], P(None, 'samp', None, 'box'), may hold values from -6 to 6
- child_parent: int32 [2048], P('box'), may hold values from 0 to 511, as said below
- child_octant: int32 [2048], P('box'), may hold values from 0 to 7, as said below
- child_sources: int32 [2048, 8], P('box'), may hold values from 0 to 2047, as said below
- child_offsets: int32 [2048, 8], P('box'), may hold values from 0 to 315
- child_counts: int32 [2048], P('box'), may hold values from 1 to 8, as said below
- parent_sources: int32 [512, 8], replicated, may hold values from 0 to 511
- parent_offsets: int32 [512, 8], replicated, may hold values from 0 to 315
- parent_counts: int32 [512], replicated, may hold values from 1 to 8, as said below
- interp_weights: bfloat16 [640, 2048], replicated, may hold values from -0.25 to 0.25
- shift_phase: float32 [8, 2, 2048], P(None, 'samp'), may hold values from -3.140625 to 3.140625
- child_table: bfloat16 [2, 316, 2, 512], P(None, None, 'samp'), may hold values from -4 to 4
- parent_table: bfloat16 [2, 316, 2, 2048], P(None, None, 'samp', 'box'), may hold values from -1.25 to 1.25
Outputs:
- child_field: bfloat16 [2, 2, 512, 2048], P(None, 'samp', None, 'box')
Inputs may be any that keep to these rules, and one draw needn't show every extreme that they name: `child_parent`: child boxes on one index d of box have their parents among the boxes d * 32 to d * 32 + 31; children of one parent stand next to each other, parents in rising order; every parent has 2 to 8 children, and each index has parents with 8 and with 2. `child_octant`: children of one parent have different octants. `child_sources`: an entry of a child box's list names a child box of the same index of box, one of the last 32 boxes of the index before it, or one of the first 32 boxes of the index after it. Entries of child_sources and child_offsets at positions child_counts[c] and beyond are unused; on every index of box some child list is full. Entries of parent_sources and parent_offsets at positions parent_counts[p] and beyond are unused; some parent list is full.
All inputs are finite; a program needn't handle non-finite values.
Results may differ from a plain program's by a relative error of at most 0.0061.
Values may be sent and summed in bfloat16 or wider, within the bound.
No kernel may reach another device: no remote copies, remote signals or barrier semaphores. Data moves between devices by JAX's collectives and lax.ppermute only.
A program may use at most 128 MiB of HBM per device.

v0:
```python
import jax
import jax.numpy as jnp
from jax import lax
from jax.sharding import PartitionSpec as P

PAR_DEV = 32
KCG = 512
RIM = 64
NEARB = 32


def padded(value, sides, width, wrap):
    for axis, dim in sides:
        peers, length = (lax.axis_size(axis), value.shape[dim])
        up = [(i, (i + 1) % peers) for i in range(peers if wrap else peers - 1)]
        down = [(j, i) for i, j in up]
        last = lax.slice_in_dim(value, length - width, length, axis=dim)
        initial = lax.slice_in_dim(value, 0, width, axis=dim)
        before = lax.ppermute(last, axis, up)
        after = lax.ppermute(initial, axis, down)
        value = jnp.concatenate([before, value, after], axis=dim)
    return value


def translate(pattern, table, sources, offsets, counts, block_width):
    box_total = sources.shape[0]
    sample_count = pattern.shape[1]
    turn_count = sources.shape[1] // block_width

    def advance(step_index, summed):
        begin_at = step_index * block_width
        source_block = sources.T
        offset_block = offsets.T
        alive_mask = (begin_at + jnp.arange(block_width)[:, None] < counts[None, :]).astype(
            jnp.float32
        )
        picked = pattern[:, :, source_block].astype(jnp.float32)
        coefficient = table[:, :, offset_block].astype(jnp.float32)
        real_part = jnp.sum(
            (coefficient[0] * picked[0] - coefficient[1] * picked[1]) * alive_mask, axis=1
        )
        imag_part = jnp.sum(
            (coefficient[0] * picked[1] + coefficient[1] * picked[0]) * alive_mask, axis=1
        )
        return summed + jnp.stack([real_part, imag_part])

    return lax.fori_loop(
        0, turn_count, advance, jnp.zeros((2, sample_count, box_total), jnp.float32)
    )


def local(
    child_pattern,
    child_parent,
    child_octant,
    child_sources,
    child_offsets,
    child_counts,
    parent_sources,
    parent_offsets,
    parent_counts,
    interp_weights,
    shift_phase,
    child_table,
    parent_table,
):
    highest = lax.Precision.HIGHEST
    box_count = child_pattern.shape[3]
    own_pattern = child_pattern[:, 0]
    extended = padded(own_pattern, (("samp", 1),), RIM, True)
    interp = jnp.einsum("jk,rjc->rkc", interp_weights, extended, preferred_element_type=jnp.float32)
    octant_table = (child_octant[None, :] == jnp.arange(8, dtype=jnp.int32)[:, None]).astype(
        jnp.float32
    )
    angles = shift_phase[:, 0, :]
    cosine = jnp.dot(jnp.cos(angles).T, octant_table, precision=highest)
    sine_part = jnp.dot(jnp.sin(angles).T, octant_table, precision=highest)
    shifted = jnp.stack(
        [interp[0] * cosine - interp[1] * sine_part, interp[0] * sine_part + interp[1] * cosine]
    )
    my_box = lax.axis_index("box")
    local_parent = child_parent - my_box * PAR_DEV
    parent_onehot = (local_parent[:, None] == jnp.arange(PAR_DEV, dtype=jnp.int32)[None, :]).astype(
        jnp.float32
    )
    aggregated = jnp.dot(shifted.reshape(-1, box_count), parent_onehot, precision=highest)
    aggregated = aggregated.reshape(2, 1, -1, PAR_DEV).astype(jnp.bfloat16)
    regrouped = lax.all_to_all(aggregated, "box", split_axis=2, concat_axis=3, tiled=True)
    parent_coeff = jnp.transpose(parent_table[:, :, 0, :], (0, 2, 1))
    parent_far = translate(
        regrouped[:, 0], parent_coeff, parent_sources, parent_offsets, parent_counts, 8
    ).astype(jnp.bfloat16)
    returned = lax.all_to_all(parent_far[:, None], "box", split_axis=3, concat_axis=2, tiled=True)
    spread = jnp.dot(
        returned.reshape(-1, PAR_DEV),
        parent_onehot.T.astype(jnp.bfloat16),
        preferred_element_type=jnp.float32,
    )
    spread = spread.reshape(2, -1, box_count)
    lowered = jnp.stack(
        [spread[0] * cosine + spread[1] * sine_part, spread[1] * cosine - spread[0] * sine_part]
    ).astype(jnp.bfloat16)
    child_terms = jnp.einsum(
        "jk,rkc->rjc", interp_weights, lowered, preferred_element_type=jnp.float32
    ).astype(jnp.bfloat16)
    rimmed = padded(child_terms, (("samp", 1),), RIM, True)
    incoming = child_terms[:, RIM : RIM + KCG].astype(jnp.float32)
    incoming = incoming.at[:, :RIM].add(rimmed[:, :RIM].astype(jnp.float32))
    incoming = incoming.at[:, KCG - RIM :].add(
        rimmed[:, rimmed.shape[1] - RIM :].astype(jnp.float32)
    )
    reach_boxes = NEARB
    near_pattern = padded(own_pattern, (("box", 2),), NEARB, False)
    near_sources = child_sources - (my_box * box_count - reach_boxes)
    child_coeff = jnp.transpose(child_table[:, :, 0, :], (0, 2, 1))
    nearby = translate(near_pattern, child_coeff, near_sources, child_offsets, child_counts, 8)
    return (nearby + incoming).astype(jnp.bfloat16)[:, None]


def solution(mesh):
    return jax.shard_map(
        local,
        mesh=mesh,
        in_specs=(
            P(None, "samp", None, "box"),
            P("box"),
            P("box"),
            P("box", None),
            P("box", None),
            P("box"),
            P(),
            P(),
            P(),
            P(),
            P(None, "samp", None),
            P(None, None, "samp", None),
            P(None, None, "samp", "box"),
        ),
        out_specs=P(None, "samp", None, "box"),
        check_vma=False,
    )
```

profile of v0, /device:TPU:0, one launch (start us, length us, event | category | flops | bytes accessed | tf_op | source)
XLA Modules:
  0.0 162.1 jit_solution(11176833794705295781)
XLA Ops:
  0.0 1.2 copy.128
  2.6 5.4 %collective-permute-start = (bf16[2,512,32]{1,2,0:T(8,128)(2,1)}, bf16[2,512,32]{1,2,0:T(8,128)(2,1)}, u32[]{:S(2)}, u32[]{:S(2)}) collective-permute-start(bf16[2,512,32]{1,2,0:T(8,128)(2,1)} %get-tuple-element.87), channel_id=1, source_target_pairs={{0,2},{2,4},{4,6},{6,8},{8,10},{10,12},{12,14},{14,16},{16,18},{18... | collective-permute-start | bytes 196616 | tf_op jit(solution)/shard_map/ppermute | solution.py:19
  8.1 1.3 collective-permute-start.1
  9.4 1.1 fusion.54
  10.4 2.3 %convolution_bitcast_fusion.1 = f32[2048,128]{0,1:T(8,128)} fusion(f32[8,1,2048]{2,1,0:T(1,128)S(1)} %bitcast.152, s32[128]{0:T(128)} %param.19), kind=kOutput, calls=%fused_computation.10 | convolution fusion | flops 25166848 | bytes 1114624 | tf_op jit(solution)/shard_map/dot_general | solution.py:77
  12.7 1.6 convolution_bitcast_fusion.2
  15.1 1.0 convolution_bitcast_fusion
  17.1 0.9 fusion.3
  17.9 2.0 %copy.135 = bf16[2,1,2048,32]{3,0,1,2:T(2,128)(2,1)} copy(bf16[2,1,2048,32]{2,3,0,1:T(8,128)(2,1)S(1)} %fusion.3) | data formatting | bytes 524288 | tf_op jit(solution)/shard_map/convert_element_type | solution.py:87
  19.9 3.8 %reshape.216 = bf16[16,2,4096]{2,1,0:T(2,128)(2,1)} reshape(bf16[2048,1,2,32]{3,2,1,0:T(2,128)(2,1)} %bitcast.139) | data formatting | bytes 524288
  23.7 8.1 %all-to-all-start = ((bf16[16,2,4096]{2,1,0:T(2,128)(2,1)}), bf16[16,2,4096]{2,1,0:T(2,128)(2,1)}, u32[]{:S(2)}, u32[]{:S(2)}) async-start(bf16[16,2,4096]{2,1,0:T(2,128)(2,1)} %reshape.216), calls=%async_computation | async-start | bytes 524288 | tf_op jit(solution)/shard_map/all_to_all | solution.py:88
  31.9 27.0 %gather_fusion.2 = bf16[4096,2,128]{2,1,0:T(2,128)(2,1)} fusion(bf16[2,128,316]{1,0,2:T(2,128)(2,1)S(1)} %bitcast.131, s32[4096]{0:T(1024)S(1)} %broadcast_clamp_fusion.1), kind=kCustom, calls=%fused_computation.2 | custom fusion | bytes 4210688 | tf_op jit(solution)/shard_map/while/body/eval_jaxpr/gather | solution.py:38
  58.8 5.1 %convert.22 = f32[8,512,2,128]{3,2,1,0:T(2,128)} convert(bf16[8,512,2,128]{3,2,1,0:T(2,128)(2,1)} %bitcast.137) | non-fusion elementwise | flops 1048576 | bytes 6291456 | tf_op jit(solution)/shard_map/while/body/eval_jaxpr/convert_element_type | solution.py:38
  63.9 11.1 %gather_fusion = bf16[1024,2,512]{2,1,0:T(2,128)(2,1)} fusion(bf16[2,512,316]{1,0,2:T(2,128)(2,1)S(1)} %bitcast.138, s32[1024]{0:T(1024)} %fusion.42), kind=kCustom, calls=%fused_computation | custom fusion | bytes 4198400 | tf_op jit(solution)/shard_map/while/body/eval_jaxpr/gather | solution.py:38
  75.0 4.8 %copy.150 = f32[8,128,2,512]{1,0,3,2:T(8,128)} copy(bf16[8,128,2,512]{3,2,1,0:T(2,128)(2,1)} %bitcast.135) | data formatting | bytes 6291456 | tf_op jit(solution)/shard_map/while/body/eval_jaxpr/convert_element_type | solution.py:38
  79.8 3.7 %reshape.217 = bf16[2048,1,2,32]{3,2,1,0:T(2,128)(2,1)} reshape(bf16[16,2,4096]{2,1,0:T(2,128)(2,1)} %all-to-all-done) | data formatting | bytes 524288
  83.5 2.4 %copy.153 = bf16[2,1,16,128,32]{3,4,2,0,1:T(8,128)(2,1)S(1)} copy(bf16[2,1,16,128,32]{4,0,3,2,1:T(2,128)(2,1)} %bitcast.140) | data formatting | bytes 524288 | tf_op jit(solution)/shard_map/all_to_all | solution.py:88
  86.2 27.0 %gather_fusion.3 = bf16[4096,2,128]{2,1,0:T(2,128)(2,1)} fusion(bf16[2,128,512]{1,0,2:T(2,128)(2,1)S(1)} %copy.138, s32[4096]{0:T(1024)S(1)} %broadcast_clamp_fusion), kind=kCustom, calls=%fused_computation.3 | custom fusion | bytes 4210688 | tf_op jit(solution)/shard_map/while/body/eval_jaxpr/gather | solution.py:37
  113.2 3.2 %convert.23 = f32[8,512,2,128]{3,2,1,0:T(2,128)S(1)} convert(bf16[8,512,2,128]{3,2,1,0:T(2,128)(2,1)} %bitcast.136) | non-fusion elementwise | flops 1048576 | bytes 6291456 | tf_op jit(solution)/shard_map/while/body/eval_jaxpr/convert_element_type | solution.py:37
  116.4 1.0 copy_bitcast_fusion
  117.4 1.2 fusion.8
  118.9 0.9 copy.142
  119.7 6.9 %all-to-all-start.1 = ((bf16[2,1,128,512]{2,0,1,3:T(2,128)(2,1)}), bf16[2,1,128,512]{2,0,1,3:T(2,128)(2,1)}, u32[]{:S(2)}, u32[]{:S(2)}) async-start(bf16[2,1,128,512]{2,0,1,3:T(2,128)(2,1)} %copy.142), calls=%async_computation.1 | async-start | bytes 524288 | tf_op jit(solution)/shard_map/all_to_all | solution.py:93
  126.7 0.9 pad_maximum_fusion
  128.0 11.0 %gather_fusion.1 = bf16[1024,2,512]{2,1,0:T(2,128)(2,1)} fusion(bf16[2,512,192]{1,0,2:T(2,128)(2,1)S(1)} %copy.129, s32[1024]{0:T(1024)S(1)} %fusion.44), kind=kCustom, calls=%fused_computation.1 | custom fusion | bytes 4198400 | tf_op jit(solution)/shard_map/while/body/eval_jaxpr/gather | solution.py:37
  139.0 4.8 %copy.151 = f32[8,128,2,512]{1,0,3,2:T(8,128)} copy(bf16[8,128,2,512]{3,2,1,0:T(2,128)(2,1)} %bitcast.134) | data formatting | bytes 6291456 | tf_op jit(solution)/shard_map/while/body/eval_jaxpr/convert_element_type | solution.py:37
  143.8 5.2 %fusion.10 = (f32[512,128]{1,0:T(8,128)S(1)}, f32[512,128]{1,0:T(8,128)S(1)}) fusion(f32[2,512,8,128]{3,2,1,0:T(8,128)} %bitcast.133, f32[2,512,8,128]{3,2,1,0:T(8,128)} %bitcast.132, f32[8,128]{1,0:T(8,128)S(1)} %fusion.45), kind=kLoop, calls=%fused_computation.24 | loop fusion | flops 5111808 | bytes 8916992 | tf_op jit(solution)/shard_map/while/body/eval_jaxpr/reduce_sum | solution.py:39
  150.0 1.0 copy.143
  153.2 1.0 fusion.14
  156.8 0.9 slice_add_fusion
  158.6 1.7 %fusion.28 = bf16[2,1,512,128]{2,3,0,1:T(8,128)(2,1)} fusion(f32[2,512,128]{1,2,0:T(8,128)S(1)} %scatter-add.9, f32[1,512,128]{1,2,0:T(8,128)} %bitcast.146, f32[1,512,128]{1,2,0:T(8,128)S(1)} %bitcast.145), kind=kLoop, calls=%fused_computation.46 | loop fusion | flops 393216 | bytes 1310720 | tf_op jit(solution)/shard_map/broadcast_in_dim | solution.py:117
  160.3 1.8 %copy.147 = bf16[2,1,512,128]{3,2,1,0:T(8,128)(2,1)} copy(bf16[2,1,512,128]{2,3,0,1:T(8,128)(2,1)} %fusion.28) | data formatting | bytes 524288 | tf_op jit(solution)/shard_map/broadcast_in_dim | solution.py:117
  (78 shorter events, 10.5 us)
Async XLA Ops:
  0.0 15.1 %copy-start = (bf16[640,2048]{1,0:T(8,128)(2,1)S(1)}, bf16[640,2048]{1,0:T(8,128)(2,1)}, u32[]{:S(2)}) copy-start(bf16[640,2048]{1,0:T(8,128)(2,1)} %param.26) | copy-start | bytes 7864324
  0.0 12.7 %copy-start.12 = (s32[128]{0:T(128)S(1)}, s32[128]{0:T(128)}, u32[]{:S(2)}) copy-start(s32[128]{0:T(128)} %param.19) | copy-start | bytes 1540
  0.0 14.3 %copy-start.8 = (s32[512,8]{0,1:T(8,128)S(1)}, s32[512,8]{0,1:T(8,128)}, u32[]{:S(2)}) copy-start(s32[512,8]{0,1:T(8,128)} %param.23) | copy-start | bytes 49156
  0.0 14.3 %copy-start.9 = (s32[512,8]{0,1:T(8,128)S(1)}, s32[512,8]{0,1:T(8,128)}, u32[]{:S(2)}) copy-start(s32[512,8]{0,1:T(8,128)} %param.24) | copy-start | bytes 49156
  0.0 14.4 %copy-start.10 = (s32[128,8]{0,1:T(8,128)S(1)}, s32[128,8]{0,1:T(8,128)}, u32[]{:S(2)}) copy-start(s32[128,8]{0,1:T(8,128)} %param.21) | copy-start | bytes 12292
  0.0 15.0 %copy-start.11 = (s32[128,8]{0,1:T(8,128)S(1)}, s32[128,8]{0,1:T(8,128)}, u32[]{:S(2)}) copy-start(s32[128,8]{0,1:T(8,128)} %param.20) | copy-start | bytes 12292
  0.0 15.0 %copy-start.17 = (s32[128]{0:T(128)S(1)}, s32[128]{0:T(128)}, u32[]{:S(2)}) copy-start(s32[128]{0:T(128)} %param.18) | copy-start | bytes 1540
  1.4 13.7 %collective-permute-start.2 = (bf16[2,64,128]{1,2,0:T(8,128)(2,1)S(1)}, bf16[2,64,128]{1,2,0:T(8,128)(2,1)S(1)}, u32[]{:S(2)}, u32[]{:S(2)}) collective-permute-start(bf16[2,64,128]{1,2,0:T(8,128)(2,1)S(1)} %get-tuple-element.89), channel_id=1, source_target_pairs={{0,1},{1,0},{2,3},{3,2},{4,5},{5,4},{6,7},{7,6},{8,9},{9,8},{10,11... | collective-permute-start | bytes 98312 | tf_op jit(solution)/shard_map/ppermute | solution.py:19
  1.9 13.1 %collective-permute-start.3 = (bf16[2,64,128]{1,2,0:T(8,128)(2,1)S(1)}, bf16[2,64,128]{1,2,0:T(8,128)(2,1)S(1)}, u32[]{:S(2)}, u32[]{:S(2)}) collective-permute-start(bf16[2,64,128]{1,2,0:T(8,128)(2,1)S(1)} %get-tuple-element.90), channel_id=1, source_target_pairs={{1,0},{0,1},{3,2},{2,3},{5,4},{4,5},{7,6},{6,7},{9,8},{8,9},{11,10... | collective-permute-start | bytes 98312 | tf_op jit(solution)/shard_map/ppermute | solution.py:20
  2.6 124.0 %collective-permute-start = (bf16[2,512,32]{1,2,0:T(8,128)(2,1)}, bf16[2,512,32]{1,2,0:T(8,128)(2,1)}, u32[]{:S(2)}, u32[]{:S(2)}) collective-permute-start(bf16[2,512,32]{1,2,0:T(8,128)(2,1)} %get-tuple-element.87), channel_id=1, source_target_pairs={{0,2},{2,4},{4,6},{6,8},{8,10},{10,12},{12,14},{14,16},{16,18},{18... | collective-permute-start | bytes 196616 | tf_op jit(solution)/shard_map/ppermute | solution.py:19
  8.1 118.6 %collective-permute-start.1 = (bf16[2,512,32]{1,2,0:T(8,128)(2,1)}, bf16[2,512,32]{1,2,0:T(8,128)(2,1)}, u32[]{:S(2)}, u32[]{:S(2)}) collective-permute-start(bf16[2,512,32]{1,2,0:T(8,128)(2,1)} %get-tuple-element.88), channel_id=1, source_target_pairs={{2,0},{4,2},{6,4},{8,6},{10,8},{12,10},{14,12},{16,14},{18,16},{20... | collective-permute-start | bytes 196616 | tf_op jit(solution)/shard_map/ppermute | solution.py:20
  15.0 2.0 %copy-start.13 = (s32[128]{0:T(128)}, s32[128]{0:T(128)S(1)}, u32[]{:S(2)}) copy-start(s32[128]{0:T(128)S(1)} %broadcast_subtract_fusion) | copy-start | bytes 1540
  15.0 1.2 copy-start.3
  15.0 1.5 copy-start.5
  17.9 13.9 %copy-start.16 = (s32[128]{0:T(128)S(1)}, s32[128]{0:T(128)}, u32[]{:S(2)}) copy-start(s32[128]{0:T(128)} %param.22) | copy-start | bytes 1540
  17.9 13.9 %copy-start.1 = (bf16[2,316,1,128]{3,0,2,1:T(2,128)(2,1)S(1)}, bf16[2,316,1,128]{3,0,2,1:T(2,128)(2,1)}, u32[]{:S(2)}) copy-start(bf16[2,316,1,128]{3,0,2,1:T(2,128)(2,1)} %param.29) | copy-start | bytes 485380
  23.7 56.1 %all-to-all-start = ((bf16[16,2,4096]{2,1,0:T(2,128)(2,1)}), bf16[16,2,4096]{2,1,0:T(2,128)(2,1)}, u32[]{:S(2)}, u32[]{:S(2)}) async-start(bf16[16,2,4096]{2,1,0:T(2,128)(2,1)} %reshape.216), calls=%async_computation | async-start | bytes 524288 | tf_op jit(solution)/shard_map/all_to_all | solution.py:88
  58.8 5.1 %copy-start.7 = (bf16[2,316,1,512]{3,0,2,1:T(2,128)(2,1)S(1)}, bf16[2,316,1,512]{3,0,2,1:T(2,128)(2,1)}, u32[]{:S(2)}) copy-start(bf16[2,316,1,512]{3,0,2,1:T(2,128)(2,1)} %param.28) | copy-start | bytes 1941508
  75.0 4.8 %copy-start.15 = (s32[512]{0:T(512)S(1)}, s32[512]{0:T(512)}, u32[]{:S(2)}) copy-start(s32[512]{0:T(512)} %param.25) | copy-start | bytes 6148
  113.2 3.2 %copy-start.2 = (f32[8,512,2,128]{3,2,1,0:T(2,128)S(1)}, f32[8,512,2,128]{3,2,1,0:T(2,128)}, u32[]{:S(2)}) copy-start(f32[8,512,2,128]{3,2,1,0:T(2,128)} %convert.22) | copy-start | bytes 12582916
  119.7 30.2 %all-to-all-start.1 = ((bf16[2,1,128,512]{2,0,1,3:T(2,128)(2,1)}), bf16[2,1,128,512]{2,0,1,3:T(2,128)(2,1)}, u32[]{:S(2)}, u32[]{:S(2)}) async-start(bf16[2,1,128,512]{2,0,1,3:T(2,128)(2,1)} %copy.142), calls=%async_computation.1 | async-start | bytes 524288 | tf_op jit(solution)/shard_map/all_to_all | solution.py:93
  149.0 2.2 %copy-start.14 = (s32[128]{0:T(128)S(1)}, s32[128]{0:T(128)}, u32[]{:S(2)}) copy-start(s32[128]{0:T(128)} %copy-done.13) | copy-start | bytes 1540
  151.2 1.2 copy-start.4
  151.2 1.5 copy-start.6
  154.8 1.3 collective-permute-start.4
  155.0 1.8 %collective-permute-start.5 = (bf16[2,64,128]{1,2,0:T(8,128)(2,1)}, bf16[2,64,128]{1,2,0:T(8,128)(2,1)}, u32[]{:S(2)}, u32[]{:S(2)}) collective-permute-start(bf16[2,64,128]{1,2,0:T(8,128)(2,1)} %get-tuple-element.85), channel_id=1, source_target_pairs={{1,0},{0,1},{3,2},{2,3},{5,4},{4,5},{7,6},{6,7},{9,8},{8,9},{11,10... | collective-permute-start | bytes 98312 | tf_op jit(solution)/shard_map/ppermute | solution.py:20
where the time goes:
time: 163 us; the launch traced here: 162 us
  local copies, waits for them, and re-layouts  111 us (68%)
  starting transfers between devices  22.9 us (14%)
  other arithmetic  19.9 us (12%)
  matrix products  7.27 us (4%)
    gather x2, local copies, waits for them, and re-layouts, advance(): coefficient = table[:, :, offset_block].astype(jnp.float32)  38 us
    gather x2, local copies, waits for them, and re-layouts, advance(): picked = pattern[:, :, source_block].astype(jnp.float32)  37.9 us
    unnamed x41, local copies, waits for them, and re-layouts  10.3 us
    all_to_all x1, starting transfers between devices, local(): lax.all_to_all(aggregated, 'box', split_axis=2, concat_axis=3, tiled=True)  8.09 us
    all_to_all x1, starting transfers between devices, local(): lax.all_to_all(parent_far[:, None], 'box', split_axis=3, concat_axis=2, t...  6.9 us
    reduce_sum x2, other arithmetic, advance(): jnp.sum((coefficient[0] * picked[0] - coefficient[1] * picked[1]) * alive...  6.33 us
    ppermute x3, starting transfers between devices, padded(): before = lax.ppermute(last, axis, up)  5.95 us
    convert_element_type x2, local copies, waits for them, and re-layouts, advance(): picked = pattern[:, :, source_block].astype(jnp.float32)  5.9 us
  transfers between devices with their start and end apart: 8, of which 1 were waited for; matrix products, arithmetic and copies ran while one was open for 78% of the time, Pallas kernels for 0%

commit v1 on v0

v1 whole, which is shorter than its diff:
```python
import jax
import jax.numpy as jnp
from jax import lax
from jax.experimental import pallas as pl
from jax.experimental.pallas import tpu as pltpu
from jax.sharding import PartitionSpec as P

NEARB = 32
OCTANTS = 8
LANES = 128
f32, bf16, i32 = jnp.float32, jnp.bfloat16, jnp.int32
VMEM = pl.BlockSpec(memory_space=pltpu.VMEM)


def call(body, outs, name, scratch=(), flops=1 << 20, moved=1 << 20, limit=24 << 20):
    def run(*args):
        return pl.pallas_call(
            body,
            out_shape=outs,
            in_specs=[VMEM] * len(args),
            out_specs=[VMEM] * len(outs) if isinstance(outs, list) else VMEM,
            scratch_shapes=list(scratch),
            name=name,
            cost_estimate=pl.CostEstimate(flops=flops, bytes_accessed=moved, transcendentals=0),
            compiler_params=pltpu.CompilerParams(vmem_limit_bytes=limit),
        )(*args)

    return run


def nt(a, b):
    return lax.dot_general(a, b, (((1,), (1,)), ((), ())), preferred_element_type=f32)


def tn(a, b, precision=None):
    return lax.dot_general(
        a, b, (((0,), (0,)), ((), ())), preferred_element_type=f32, precision=precision
    )


def nn(a, b):
    return lax.dot_general(a, b, (((1,), (0,)), ((), ())), preferred_element_type=f32)


def sincos(x):
    h = 0.5 * x
    q = h * h
    s = -2.50521083854417e-08 + q * 1.60590438368216e-10
    s = 2.75573192239859e-06 + q * s
    s = -1.98412698412698e-04 + q * s
    s = 8.33333333333333e-03 + q * s
    s = -1.66666666666667e-01 + q * s
    s = h + h * (q * s)
    c = 2.08767569878681e-09 + q * -1.14707455977297e-11
    c = -2.75573192239859e-07 + q * c
    c = 2.48015873015873e-05 + q * c
    c = -1.38888888888889e-03 + q * c
    c = 4.16666666666667e-02 + q * c
    c = -0.5 + q * c
    c = 1.0 + q * c
    return 2.0 * (s * c), 1.0 - 2.0 * (s * s)


def iota(shape, dim):
    return lax.broadcasted_iota(i32, shape, dim)


def slot_onehot(parent_ref, octant_ref, parents):
    base = lax.axis_index("box") * parents
    slot = octant_ref[...] * parents + (parent_ref[...] - base)
    shape = (OCTANTS * parents, slot.shape[1])
    return jnp.where(iota(shape, 0) == slot, 1.0, 0.0).astype(bf16)


def weighted(y, cosine, sine, begin, width, parents):
    slots = OCTANTS * parents
    real = imag = None
    for o in range(OCTANTS):
        yr = y[o * parents : (o + 1) * parents]
        yi = y[slots + o * parents : slots + (o + 1) * parents]
        c = cosine[o : o + 1, pl.ds(begin, width)]
        s = sine[o : o + 1, pl.ds(begin, width)]
        tr, ti = yr * c - yi * s, yr * s + yi * c
        real, imag = (tr, ti) if o == 0 else (real + tr, imag + ti)
    return real, imag


def interior(own, parent, octant, phase, weights, parents):
    _, kcg, boxes = own.shape
    kpg = weights.shape[1]
    rim = (weights.shape[0] - kcg) // 2
    slots = OCTANTS * parents
    width = 256

    def body(own_ref, par_ref, oct_ref, ph_ref, w_ref, acc_ref, cos_ref, sin_ref, e_ref):
        onehot = slot_onehot(par_ref, oct_ref, parents)
        for r in range(2):
            e_ref[r * slots : (r + 1) * slots] = nt(onehot, own_ref[r]).astype(bf16)
        sin_ref[...], cos_ref[...] = sincos(ph_ref[:, 0, :])

        @pl.loop(0, kpg // width)
        def _(step):
            begin = pl.multiple_of(step * width, width)
            y = nn(e_ref[...], w_ref[rim : rim + kcg, pl.ds(begin, width)])
            real, imag = weighted(y, cos_ref, sin_ref, begin, width, parents)
            acc_ref[0, :, pl.ds(begin, width)] = real
            acc_ref[1, :, pl.ds(begin, width)] = imag

    return call(
        body,
        [
            jax.ShapeDtypeStruct((2, parents, kpg), f32),
            jax.ShapeDtypeStruct((OCTANTS, kpg), f32),
            jax.ShapeDtypeStruct((OCTANTS, kpg), f32),
        ],
        "interior",
        [pltpu.VMEM((2 * slots, kcg), bf16)],
        flops=2 * 2 * slots * kcg * kpg,
    )(own, parent, octant, phase, weights)


def with_rims(before, after, parent, octant, cosine, sine, weights, acc, parents, spans, packed):
    kpg = weights.shape[1]
    rows = weights.shape[0]
    rim = spans[0][1] - spans[0][0]
    slots = OCTANTS * parents
    width = 256
    arrays = [before] if after is None else [before, after]

    def body(*refs):
        rims = refs[: len(arrays)]
        par_ref, oct_ref, cos_ref, sin_ref, w_ref, acc_ref, out_ref, e_ref, wr_ref = refs[len(arrays) :]
        onehot = slot_onehot(par_ref, oct_ref, parents)
        for r in range(2):
            for side, (low, high) in enumerate(spans):
                picked = nt(onehot, rims[min(side, len(arrays) - 1)][r, low:high, :])
                e_ref[r * slots : (r + 1) * slots, side * rim : (side + 1) * rim] = picked.astype(bf16)
        wr_ref[:rim] = w_ref[:rim]
        wr_ref[rim:] = w_ref[rows - rim :]

        @pl.loop(0, kpg // width)
        def _(step):
            begin = pl.multiple_of(step * width, width)
            y = nn(e_ref[...], wr_ref[:, pl.ds(begin, width)])
            sums = weighted(y, cos_ref, sin_ref, begin, width, parents)
            for r in range(2):
                total = (acc_ref[r, :, pl.ds(begin, width)] + sums[r]).astype(bf16)
                if packed:
                    for part in range(width // LANES):
                        row = pl.multiple_of((step * (width // LANES) + part) * parents, parents)
                        out_ref[pl.ds(row, parents), r * LANES : (r + 1) * LANES] = total[
                            :, part * LANES : (part + 1) * LANES
                        ]
                else:
                    out_ref[r, :, pl.ds(begin, width)] = total

    shape = (kpg // LANES * parents, 2 * LANES) if packed else (2, parents, kpg)
    return call(
        body,
        jax.ShapeDtypeStruct(shape, bf16),
        "with_rims",
        [pltpu.VMEM((2 * slots, 2 * rim), bf16), pltpu.VMEM((2 * rim, kpg), bf16)],
        flops=2 * 2 * slots * 2 * rim * kpg,
    )(*arrays, parent, octant, cosine, sine, weights, acc)


CHUNK = 128


def list_tables(sources, offsets, counts, table):
    slots, boxes = sources.shape
    total = boxes
    operators, lanes = table.shape

    def body(src_ref, off_ref, cnt_ref, tab_ref, hot_ref, coef_ref):
        alive = iota((slots, boxes), 0) < cnt_ref[...]
        src = src_ref[...].T
        off = jnp.where(alive, off_ref[...], -1).T
        for chunk in range(boxes // CHUNK):
            rows = slice(chunk * CHUNK, (chunk + 1) * CHUNK)
            for m in range(slots):
                at = (chunk * slots + m) * CHUNK
                hot = src[rows, m : m + 1] == iota((CHUNK, total), 1)
                hot_ref[at : at + CHUNK] = jnp.where(hot, 1.0, 0.0).astype(bf16)
                pick = off[rows, m : m + 1] == iota((CHUNK, operators), 1)
                coef_ref[at : at + CHUNK] = nn(
                    jnp.where(pick, 1.0, 0.0).astype(bf16), tab_ref[...]
                ).astype(bf16)

    return call(
        body,
        [
            jax.ShapeDtypeStruct((slots * boxes, total), bf16),
            jax.ShapeDtypeStruct((slots * boxes, lanes), bf16),
        ],
        "list_tables",
        flops=2 * slots * boxes * operators * lanes * 4,
        moved=8 << 20,
        limit=32 << 20,
    )(sources, offsets, counts, table)


def parent_sums(pattern, hot, coef, slots):
    total, lanes = pattern.shape
    half = lanes // 2

    def body(pat_ref, hot_ref, coef_ref, out_ref):
        for chunk in range(total // CHUNK):
            at = chunk * slots * CHUNK
            picked = nn(hot_ref[at : at + slots * CHUNK], pat_ref[...])
            real = imag = 0.0
            for m in range(slots):
                rows = slice(m * CHUNK, (m + 1) * CHUNK)
                pr, pi = picked[rows, :half], picked[rows, half:]
                c = coef_ref[at + m * CHUNK : at + (m + 1) * CHUNK].astype(f32)
                cr, ci = c[:, :half], c[:, half:]
                real += cr * pr - ci * pi
                imag += cr * pi + ci * pr
            out_ref[chunk * CHUNK : (chunk + 1) * CHUNK, :half] = real.astype(bf16)
            out_ref[chunk * CHUNK : (chunk + 1) * CHUNK, half:] = imag.astype(bf16)

    return call(
        body,
        jax.ShapeDtypeStruct((total, lanes), bf16),
        "parent_sums",
        flops=2 * slots * total * total * lanes,
        moved=8 << 20,
        limit=32 << 20,
    )(pattern, hot, coef)


def child_phases(octant, cosine, sine):
    boxes = octant.shape[1]
    kpg = cosine.shape[1]

    def body(oct_ref, cos_ref, sin_ref, c_ref, s_ref):
        onehot = jnp.where(iota((OCTANTS, boxes), 0) == oct_ref[...], 1.0, 0.0)
        c_ref[...] = tn(onehot, cos_ref[...], lax.Precision.HIGHEST)
        s_ref[...] = tn(onehot, sin_ref[...], lax.Precision.HIGHEST)

    shape = jax.ShapeDtypeStruct((boxes, kpg), f32)
    return call(body, [shape, shape], "child_phases", flops=1 << 28)(octant, cosine, sine)


def lower(far, parent, cosine, sine, weights, parents, rim, packed):
    boxes, kpg = cosine.shape
    rows = weights.shape[0]
    width = LANES if packed else 256

    def body(far_ref, par_ref, cos_ref, sin_ref, w_ref, low_ref, rim_ref, acc_ref):
        base = lax.axis_index("box") * parents
        hot = jnp.where(iota((parents, boxes), 0) == par_ref[...] - base, 1.0, 0.0).astype(bf16)
        hot = hot.T
        for step in range(kpg // width):
            cols = slice(step * width, (step + 1) * width)
            if packed:
                spread = nn(hot, far_ref[step * parents : (step + 1) * parents])
                sr, si = spread[:, :LANES], spread[:, LANES:]
            else:
                sr, si = nn(hot, far_ref[0, :, cols]), nn(hot, far_ref[1, :, cols])
            c, s = cos_ref[:, cols], sin_ref[:, cols]
            low_ref[:boxes, cols] = (sr * c + si * s).astype(bf16)
            low_ref[boxes:, cols] = (si * c - sr * s).astype(bf16)
        first = nt(w_ref[:rim], low_ref[...]).astype(bf16)
        last = nt(w_ref[rows - rim :], low_ref[...]).astype(bf16)
        for side, terms in enumerate((first, last)):
            for r in range(2):
                rim_ref[side, r] = terms[:, r * boxes : (r + 1) * boxes]

    return call(
        body,
        [
            jax.ShapeDtypeStruct((2 * boxes, kpg), bf16),
            jax.ShapeDtypeStruct((2, 2, rim, boxes), bf16),
        ],
        "lower",
        [pltpu.VMEM((8, LANES), f32)],
        flops=2 * 2 * boxes * kpg * 2 * rim,
    )(far, parent, cosine, sine, weights)


def anterpolate(weights, lowered, nearby, rim):
    _, kcg, boxes = nearby.shape

    def body(w_ref, low_ref, near_ref, out_ref):
        terms = nt(w_ref[rim : rim + kcg], low_ref[...]).astype(bf16).astype(f32)
        for r in range(2):
            out_ref[r] = near_ref[r] + terms[:, r * boxes : (r + 1) * boxes]

    return call(
        body,
        jax.ShapeDtypeStruct(nearby.shape, f32),
        "anterpolate",
        flops=2 * kcg * weights.shape[1] * 2 * boxes,
    )(weights, lowered, nearby)


def finish(partial, start_terms, end_terms):
    _, kcg, boxes = partial.shape
    rim = start_terms.shape[1]

    def body(sum_ref, start_ref, end_ref, out_ref):
        out_ref[:, rim : kcg - rim] = sum_ref[:, rim : kcg - rim].astype(bf16)
        out_ref[:, :rim] = (sum_ref[:, :rim] + start_ref[...].astype(f32)).astype(bf16)
        out_ref[:, kcg - rim :] = (sum_ref[:, kcg - rim :] + end_ref[...].astype(f32)).astype(bf16)

    return call(body, jax.ShapeDtypeStruct(partial.shape, bf16), "finish")(partial, start_terms, end_terms)


def near_sums(own, before, after, sources, offsets, counts, table):
    _, kcg, boxes = own.shape
    slots = sources.shape[0]
    operators = table.shape[1]
    reach = boxes + 2 * NEARB
    depth = 2 * boxes
    pair = 2

    def body(own_ref, bef_ref, aft_ref, src_ref, off_ref, cnt_ref, tab_ref, out_ref, ext_ref, tt_ref, acc_ref):
        eye = jnp.where(iota((kcg, kcg), 0) == iota((kcg, kcg), 1), 1.0, 0.0).astype(bf16)
        for r in range(2):
            rows = slice(r * kcg, (r + 1) * kcg)
            ext_ref[rows, :boxes] = own_ref[r]
            halo = jnp.concatenate(
                [bef_ref[r], aft_ref[r], jnp.zeros((boxes - 2 * NEARB, kcg), bf16)], axis=0
            )
            ext_ref[rows, boxes:] = nt(eye, halo).astype(bf16)
            tt_ref[rows] = nt(eye, tab_ref[r]).astype(bf16)
        base = lax.axis_index("box") * boxes
        rel = src_ref[...] - base
        rel = jnp.where(rel < 0, rel + boxes + NEARB, jnp.where(rel >= boxes, rel + NEARB, rel))
        off = jnp.where(iota((slots, boxes), 0) < cnt_ref[...], off_ref[...], -1)
        for m in range(0, slots, pair):
            src = jnp.concatenate([rel[m + j : m + j + 1] for j in range(pair)], axis=1)
            ops = jnp.concatenate([off[m + j : m + j + 1] for j in range(pair)], axis=1)
            hot = jnp.where(iota((depth, pair * boxes), 0) == src, 1.0, 0.0).astype(bf16)
            pick = jnp.where(iota((operators, pair * boxes), 0) == ops, 1.0, 0.0).astype(bf16)
            picked = nn(ext_ref[...], hot)
            coef = nn(tt_ref[...], pick)
            pr, pi, cr, ci = picked[:kcg], picked[kcg:], coef[:kcg], coef[kcg:]
            real, imag = cr * pr - ci * pi, cr * pi + ci * pr
            for r, value in enumerate((real, imag)):
                value = sum(value[:, j * boxes : (j + 1) * boxes] for j in range(pair))
                out_ref[r] = value if m == 0 else out_ref[r] + value

    return call(
        body,
        jax.ShapeDtypeStruct(own.shape, f32),
        "near_sums",
        [
            pltpu.VMEM((2 * kcg, depth), bf16),
            pltpu.VMEM((2 * kcg, operators), bf16),
            pltpu.VMEM((8, LANES), f32),
        ],
        flops=2 * slots * boxes * 2 * kcg * (depth + operators),
        limit=32 << 20,
    )(own, before, after, sources, offsets, counts, table)


def plain_translate(pattern, table, sources, offsets, counts):
    coef = jnp.transpose(table, (0, 2, 1))

    def advance(m, summed):
        src = lax.dynamic_index_in_dim(sources, m, 0, keepdims=False)
        off = lax.dynamic_index_in_dim(offsets, m, 0, keepdims=False)
        p = pattern[:, :, src].astype(f32)
        c = coef[:, :, off].astype(f32) * (m < counts).astype(f32)
        return summed + jnp.stack([c[0] * p[0] - c[1] * p[1], c[0] * p[1] + c[1] * p[0]])

    return lax.fori_loop(
        0, sources.shape[0], advance, jnp.zeros(pattern.shape[:2] + (sources.shape[1],), f32)
    )


def shift(value, axis, step, wrap):
    peers = lax.axis_size(axis)
    pairs = [(i, (i + step) % peers) for i in range(peers) if wrap or 0 <= i + step < peers]
    return lax.ppermute(value, axis, pairs)


def local(
    child_pattern,
    child_parent,
    child_octant,
    child_sources,
    child_offsets,
    child_counts,
    parent_sources,
    parent_offsets,
    parent_counts,
    interp_weights,
    shift_phase,
    child_table,
    parent_table,
):
    own = child_pattern[:, 0]
    _, kcg, boxes = own.shape
    rim = (interp_weights.shape[0] - kcg) // 2
    peers, groups = lax.axis_size("box"), lax.axis_size("samp")
    total = parent_sources.shape[0]
    parents = total // peers
    kpg = interp_weights.shape[1]
    mine = kpg // peers
    packed = mine == LANES and total % CHUNK == 0
    parent, octant = child_parent[None, :], child_octant[None, :]

    if groups == 2:
        before, after = shift(own, "samp", 1, True), None
        spans = ((kcg - rim, kcg), (0, rim))
    else:
        before = shift(own[:, kcg - rim :], "samp", 1, True)
        after = shift(own[:, :rim], "samp", -1, True)
        spans = ((0, rim), (0, rim))
    acc, cosine, sine = interior(own, parent, octant, shift_phase, interp_weights, parents)
    pattern = with_rims(
        before, after, parent, octant, cosine, sine, interp_weights, acc, parents, spans, packed
    )

    edge = jnp.transpose(own, (0, 2, 1))
    near_before = shift(edge[:, boxes - NEARB :], "box", 1, False)
    near_after = shift(edge[:, :NEARB], "box", -1, False)

    table = parent_table[:, :, 0, :]
    if packed:
        regrouped = lax.all_to_all(pattern, "box", split_axis=0, concat_axis=0, tiled=True)
        flat_table = jnp.transpose(table, (1, 0, 2)).reshape(table.shape[1], 2 * mine)
        hot, coef = list_tables(parent_sources.T, parent_offsets.T, parent_counts[None, :], flat_table)
        far = parent_sums(regrouped, hot, coef, parent_sources.shape[1])
        returned = lax.all_to_all(far, "box", split_axis=0, concat_axis=0, tiled=True)
    else:
        regrouped = lax.all_to_all(pattern, "box", split_axis=2, concat_axis=1, tiled=True)
        far = plain_translate(
            jnp.transpose(regrouped, (0, 2, 1)), table, parent_sources.T, parent_offsets.T, parent_counts
        ).astype(bf16)
        far = jnp.transpose(far, (0, 2, 1))
        returned = lax.all_to_all(far, "box", split_axis=1, concat_axis=2, tiled=True)

    child_cos, child_sin = child_phases(octant, cosine, sine)
    nearby = near_sums(
        own,
        near_before,
        near_after,
        child_sources.T,
        child_offsets.T,
        child_counts[None, :],
        child_table[:, :, 0, :],
    )
    lowered, rims = lower(returned, parent, child_cos, child_sin, interp_weights, parents, rim, packed)
    if groups == 2:
        got = shift(rims, "samp", 1, True)
        start_terms, end_terms = got[1], got[0]
    else:
        start_terms = shift(rims[1], "samp", 1, True)
        end_terms = shift(rims[0], "samp", -1, True)
    partial = anterpolate(interp_weights, lowered, nearby, rim)
    return finish(partial, start_terms, end_terms)[:, None]


def solution(mesh):
    return jax.shard_map(
        local,
        mesh=mesh,
        in_specs=(
            P(None, "samp", None, "box"),
            P("box"),
            P("box"),
            P("box", None),
            P("box", None),
            P("box"),
            P(),
            P(),
            P(),
            P(),
            P(None, "samp", None),
            P(None, None, "samp", None),
            P(None, None, "samp", "box"),
        ),
        out_specs=P(None, "samp", None, "box"),
        check_vma=False,
    )
```

time: 163 us -> 66.4 us (0.41)
  the two profiles are of different devices: /device:TPU:0 before, /device:TPU:9 now
where the time goes in v1:
time: 66.4 us; the launch traced here: 65.4 us
  local copies, waits for them, and re-layouts  24.7 us (37%)
  starting transfers between devices  22.5 us (34%)
  Pallas kernels  17.8 us (27%)
    unnamed x62, local copies, waits for them, and re-layouts  22.9 us
    pallas_call x9, Pallas kernels, run(): pl.pallas_call(body, out_shape=outs, in_specs=[VMEM] * len(args), out_spe...  17.8 us
    ppermute x4, starting transfers between devices, shift(): return lax.ppermute(value, axis, pairs)  9.59 us
    all_to_all x1, starting transfers between devices, local(): lax.all_to_all(pattern, 'box', split_axis=0, concat_axis=0, tiled=True)  6.66 us
    all_to_all x1, starting transfers between devices, local(): lax.all_to_all(far, 'box', split_axis=0, concat_axis=0, tiled=True)  6.2 us
  transfers between devices with their start and end apart: 6, of which 1 were waited for; matrix products, arithmetic and copies ran while one was open for 4% of the time, Pallas kernels for 18%

profile of v1, /device:TPU:9, one launch (start us, length us, event | category | flops | bytes accessed | tf_op | source)
XLA Modules:
  0.0 65.4 jit_solution(14223684212834642882)
XLA Ops:
  0.0 1.1 %copy.14 = bf16[2,1,512,128]{2,3,0,1:T(8,128)(2,1)S(1)} copy(bf16[2,1,512,128]{3,2,1,0:T(8,128)(2,1)} %param.13) | data formatting | bytes 524288 | tf_op args[0]
  1.1 0.7 %collective-permute-start = (bf16[2,512,128]{1,2,0:T(8,128)(2,1)S(1)}, bf16[2,512,128]{1,2,0:T(8,128)(2,1)}, u32[]{:S(2)}, u32[]{:S(2)}) collective-permute-start(bf16[2,512,128]{1,2,0:T(8,128)(2,1)S(1)} %bitcast.51), channel_id=1, source_target_pairs={{0,1},{1,0},{2,3},{3,2},{4,5},{5,4},{6,7},{7,6},{8,9},{9,8},{10,11... | collective-permute-start | bytes 786440 | tf_op jit(solution)/shard_map/ppermute | solution.py:377
  1.9 1.7 %copy-done = bf16[640,2048]{1,0:T(8,128)(2,1)S(1)} copy-done((bf16[640,2048]{1,0:T(8,128)(2,1)S(1)}, bf16[640,2048]{1,0:T(8,128)(2,1)}, u32[]{:S(2)}) %copy-start) | copy-done | bytes 2621464
  3.6 0.9 %copy-done.10 = bf16[2,1,512,128]{3,2,1,0:T(8,128)(2,1)S(1)} copy-done((bf16[2,1,512,128]{3,2,1,0:T(8,128)(2,1)S(1)}, bf16[2,1,512,128]{3,2,1,0:T(8,128)(2,1)}, u32[]{:S(2)}) %copy-start.10) | copy-done | bytes 262168
  5.9 0.8 %copy-done.20 = f32[8,1,2048]{2,1,0:T(1,128)S(1)} copy-done((f32[8,1,2048]{2,1,0:T(1,128)S(1)}, f32[8,1,2048]{2,1,0:T(1,128)}, u32[]{:S(2)}) %copy-start.20) | copy-done | bytes 65560
  6.7 2.8 %interior.1 = (f32[2,32,2048]{2,1,0:T(8,128)S(1)}, f32[8,2048]{1,0:T(8,128)S(1)}, f32[8,2048]{1,0:T(8,128)S(1)}) custom-call(bf16[2,512,128]{2,1,0:T(8,128)(2,1)S(1)} %bitcast.35, s32[1,128]{1,0:T(1,128)S(1)} %bitcast.38, s32[1,128]{1,0:T(1,128)S(1)} %bitcast.41, f32[8,1,2048]{2,1,0:T(1,128)S(1)} %copy-done.20, bf16[640,2048]{1,0:T(8,128)(2,1)S(1)} %copy-done), custom_call_target="tpu_custom_call" | custom-call | flops 1073741824 | bytes 1048576 | tf_op jit(solution)/shard_map/interior/pallas_call | solution.py:17
  9.6 1.2 %copy.16.refs_0_ = bf16[2,512,128]{2,1,0:T(8,128)(2,1)S(1)} copy(bf16[2,512,128]{1,2,0:T(8,128)(2,1)} %collective-permute-done) | data formatting | bytes 524288 | tf_op jit(solution)/shard_map/ppermute | solution.py:377
  10.8 2.8 %with_rims.1 = bf16[512,256]{1,0:T(8,128)(2,1)} custom-call(bf16[2,512,128]{2,1,0:T(8,128)(2,1)S(1)} %copy.16.refs_0_, s32[1,128]{1,0:T(1,128)S(1)} %bitcast.39, s32[1,128]{1,0:T(1,128)S(1)} %bitcast.42, f32[8,2048]{1,0:T(8,128)S(1)} %get-tuple-element.14.refs_3_.cos_ref, f32[8,2048]{1,0:T(8,128)S(1)} %get-tuple-element.15.refs_4_.sin_ref, ...), custom_call_target="tpu_custom_call" | custom-call | flops 268435456 | bytes 1048576 | tf_op jit(solution)/shard_map/with_rims/pallas_call | solution.py:17
  13.6 6.7 %all-to-all-start = ((bf16[16,32,256]{2,1,0:T(8,128)(2,1)}), bf16[16,32,256]{2,1,0:T(8,128)(2,1)S(1)}, u32[]{:S(2)}, u32[]{:S(2)}) async-start(bf16[16,32,256]{2,1,0:T(8,128)(2,1)} %bitcast.4), calls=%async_computation | async-start | bytes 524288 | tf_op jit(solution)/shard_map/all_to_all | solution.py:424
  20.3 1.0 %pad = bf16[320,2,128]{2,1,0:T(2,128)(2,1)S(1)} pad(bf16[316,2,128]{2,1,0:T(2,128)(2,1)} %bitcast.53, bf16[]{:T(256)} %constant.4), padding=0_4x0_0x0_0 | pad | bytes 325634
  22.8 1.9 %list_tables.1 = (bf16[4096,512]{1,0:T(8,128)(2,1)S(1)}, bf16[4096,256]{1,0:T(8,128)(2,1)S(1)}) custom-call(s32[8,512]{1,0:T(8,128)S(1)} %bitcast.44, s32[8,512]{1,0:T(8,128)S(1)} %bitcast.45, s32[1,512]{1,0:T(1,128)S(1)} %bitcast.48, bf16[316,256]{1,0:T(8,128)(2,1)S(1)} %bitcast.37), custom_call_target="tpu_custom_call" | custom-call | flops 2650800128 | bytes 8388608 | tf_op jit(solution)/shard_map/list_tables/pallas_call | solution.py:17
  24.7 2.0 %copy-done.2 = bf16[4096,512]{1,0:T(8,128)(2,1)} copy-done((bf16[4096,512]{1,0:T(8,128)(2,1)}, bf16[4096,512]{1,0:T(8,128)(2,1)S(1)}, u32[]{:S(2)}) %copy-start.2) | copy-done | bytes 4194328
  26.7 1.4 %copy-done.4 = bf16[4096,256]{1,0:T(8,128)(2,1)} copy-done((bf16[4096,256]{1,0:T(8,128)(2,1)}, bf16[4096,256]{1,0:T(8,128)(2,1)S(1)}, u32[]{:S(2)}) %copy-start.4) | copy-done | bytes 2097176
  28.2 2.2 %copy-done.3 = bf16[4096,512]{1,0:T(8,128)(2,1)S(1)} copy-done((bf16[4096,512]{1,0:T(8,128)(2,1)S(1)}, bf16[4096,512]{1,0:T(8,128)(2,1)}, u32[]{:S(2)}) %copy-start.3) | copy-done | bytes 4194328
  30.4 1.6 %copy-done.5 = bf16[4096,256]{1,0:T(8,128)(2,1)S(1)} copy-done((bf16[4096,256]{1,0:T(8,128)(2,1)S(1)}, bf16[4096,256]{1,0:T(8,128)(2,1)}, u32[]{:S(2)}) %copy-start.5) | copy-done | bytes 2097176
  32.0 2.1 %parent_sums.1 = bf16[512,256]{1,0:T(8,128)(2,1)} custom-call(bf16[512,256]{1,0:T(8,128)(2,1)S(1)} %bitcast.33, bf16[4096,512]{1,0:T(8,128)(2,1)S(1)} %copy-done.3, bf16[4096,256]{1,0:T(8,128)(2,1)S(1)} %copy-done.5), custom_call_target="tpu_custom_call" | custom-call | flops 1073741824 | bytes 8388608 | tf_op jit(solution)/shard_map/parent_sums/pallas_call | solution.py:17
  34.2 6.2 %all-to-all-start.1 = ((bf16[16,32,256]{2,1,0:T(8,128)(2,1)}), bf16[16,32,256]{2,1,0:T(8,128)(2,1)S(1)}, u32[]{:S(2)}, u32[]{:S(2)}) async-start(bf16[16,32,256]{2,1,0:T(8,128)(2,1)} %bitcast.11), calls=%async_computation.1 | async-start | bytes 524288 | tf_op jit(solution)/shard_map/all_to_all | solution.py:428
  41.0 3.1 %collective-permute-start.1 = (bf16[2,32,512]{2,1,0:T(8,128)(2,1)}, bf16[2,32,512]{2,1,0:T(8,128)(2,1)}, u32[]{:S(2)}, u32[]{:S(2)}) collective-permute-start(bf16[2,32,512]{2,1,0:T(8,128)(2,1)} %get-tuple-element.24), channel_id=1, source_target_pairs={{0,2},{2,4},{4,6},{6,8},{8,10},{10,12},{12,14},{14,16},{16,18},{18... | collective-permute-start | bytes 196616 | tf_op jit(solution)/shard_map/ppermute | solution.py:377
  44.1 4.0 %collective-permute-start.2 = (bf16[2,32,512]{2,1,0:T(8,128)(2,1)}, bf16[2,32,512]{2,1,0:T(8,128)(2,1)}, u32[]{:S(2)}, u32[]{:S(2)}) collective-permute-start(bf16[2,32,512]{2,1,0:T(8,128)(2,1)} %get-tuple-element.23), channel_id=1, source_target_pairs={{2,0},{4,2},{6,4},{8,6},{10,8},{12,10},{14,12},{16,14},{18,16},{20... | collective-permute-start | bytes 196616 | tf_op jit(solution)/shard_map/ppermute | solution.py:377
  48.1 1.2 %copy.23 = bf16[2,316,1,512]{3,1,0,2:T(8,128)(2,1)S(1)} copy(bf16[2,316,1,512]{3,0,2,1:T(2,128)(2,1)} %param.24) | data formatting | bytes 1294336 | tf_op args[11]
  49.3 0.8 %copy-done.13 = f32[8,2048]{1,0:T(8,128)S(1)} copy-done((f32[8,2048]{1,0:T(8,128)S(1)}, f32[8,2048]{1,0:T(8,128)}, u32[]{:S(2)}) %copy-start.13) | copy-done | bytes 65560
  50.1 0.8 %copy-done.15 = f32[8,2048]{1,0:T(8,128)S(1)} copy-done((f32[8,2048]{1,0:T(8,128)S(1)}, f32[8,2048]{1,0:T(8,128)}, u32[]{:S(2)}) %copy-start.15) | copy-done | bytes 65560
  51.0 1.8 %child_phases.1 = (f32[128,2048]{1,0:T(8,128)S(1)}, f32[128,2048]{1,0:T(8,128)S(1)}) custom-call(s32[1,128]{1,0:T(1,128)S(1)} %bitcast.43, f32[8,2048]{1,0:T(8,128)S(1)} %copy-done.13, f32[8,2048]{1,0:T(8,128)S(1)} %copy-done.15), custom_call_target="tpu_custom_call" | custom-call | flops 268435456 | bytes 1048576 | tf_op jit(solution)/shard_map/child_phases/pallas_call | solution.py:17
  52.8 1.0 %copy-done.6 = f32[128,2048]{1,0:T(8,128)} copy-done((f32[128,2048]{1,0:T(8,128)}, f32[128,2048]{1,0:T(8,128)S(1)}, u32[]{:S(2)}) %copy-start.6) | copy-done | bytes 1048600
  53.8 1.0 %copy-done.8 = f32[128,2048]{1,0:T(8,128)} copy-done((f32[128,2048]{1,0:T(8,128)}, f32[128,2048]{1,0:T(8,128)S(1)}, u32[]{:S(2)}) %copy-start.8) | copy-done | bytes 1048600
  54.8 1.2 %copy-done.7 = f32[128,2048]{1,0:T(8,128)S(1)} copy-done((f32[128,2048]{1,0:T(8,128)S(1)}, f32[128,2048]{1,0:T(8,128)}, u32[]{:S(2)}) %copy-start.7) | copy-done | bytes 1048600
  56.0 1.2 %copy-done.9 = f32[128,2048]{1,0:T(8,128)S(1)} copy-done((f32[128,2048]{1,0:T(8,128)S(1)}, f32[128,2048]{1,0:T(8,128)}, u32[]{:S(2)}) %copy-start.9) | copy-done | bytes 1048600
  57.2 1.1 %lower.1 = (bf16[256,2048]{1,0:T(8,128)(2,1)S(1)}, bf16[2,2,64,128]{3,2,1,0:T(8,128)(2,1)S(1)}) custom-call(bf16[512,256]{1,0:T(8,128)(2,1)S(1)} %bitcast.32, s32[1,128]{1,0:T(1,128)S(1)} %bitcast.40, f32[128,2048]{1,0:T(8,128)S(1)} %copy-done.7, f32[128,2048]{1,0:T(8,128)S(1)} %copy-done.9, bf16[640,2048]{1,0:T(8,128)(2,1)S(1)} %copy-done.1), custom_call_target="tpu_custom_call" | custom-call | flops 134217728 | bytes 1048576 | tf_op jit(solution)/shard_map/lower/pallas_call | solution.py:17
  58.4 1.8 %collective-permute-start.3 = (bf16[2,2,64,128]{3,2,1,0:T(8,128)(2,1)S(1)}, bf16[2,2,64,128]{3,2,1,0:T(8,128)(2,1)S(1)}, u32[]{:S(2)}, u32[]{:S(2)}) collective-permute-start(bf16[2,2,64,128]{3,2,1,0:T(8,128)(2,1)S(1)} %get-tuple-element.22), channel_id=1, source_target_pairs={{0,1},{1,0},{2,3},{3,2},{4,5},{5,4},{6,7},{7,6},{8,9},{9,8},{10,11... | collective-permute-start | bytes 196616 | tf_op jit(solution)/shard_map/ppermute | solution.py:377
  60.2 3.7 %near_sums.1.near_ref = f32[2,512,128]{2,1,0:T(8,128)S(1)} custom-call(bf16[2,512,128]{2,1,0:T(8,128)(2,1)S(1)} %bitcast.36, bf16[2,32,512]{2,1,0:T(8,128)(2,1)} %collective-permute-done.1.bef_ref, bf16[2,32,512]{2,1,0:T(8,128)(2,1)} %collective-permute-done.2.aft_ref, s32[8,128]{1,0:T(8,128)S(1)} %bitcast.46, s32[8,128]{1,0:T(8,128)S(1)} %bitcast.47, ...), custom_call_target="tpu_custom_call" | custom-call | flops 1199570944 | bytes 1048576 | tf_op jit(solution)/shard_map/near_sums/pallas_call | solution.py:17
  63.9 0.7 %anterpolate.1.sum_ref = f32[2,512,128]{2,1,0:T(8,128)S(1)} custom-call(bf16[640,2048]{1,0:T(8,128)(2,1)S(1)} %copy-done.1, bf16[256,2048]{1,0:T(8,128)(2,1)S(1)} %get-tuple-element.21.low_ref, f32[2,512,128]{2,1,0:T(8,128)S(1)} %near_sums.1.near_ref), custom_call_target="tpu_custom_call" | custom-call | flops 536870912 | bytes 1048576 | tf_op jit(solution)/shard_map/anterpolate/pallas_call | solution.py:17
  64.7 0.7 %finish.1 = bf16[2,512,128]{2,1,0:T(8,128)(2,1)} custom-call(f32[2,512,128]{2,1,0:T(8,128)S(1)} %anterpolate.1.sum_ref, bf16[2,64,128]{2,1,0:T(8,128)(2,1)S(1)} %get-tuple-element.26.start_ref, bf16[2,64,128]{2,1,0:T(8,128)(2,1)S(1)} %get-tuple-element.25.end_ref), custom_call_target="tpu_custom_call" | custom-call | flops 1048576 | bytes 1048576 | tf_op jit(solution)/shard_map/finish/pallas_call | solution.py:17
  (54 shorter events, 3.7 us)
Async XLA Ops:
  0.0 10.8 %copy-start.17 = (s32[128]{0:T(128)S(1)}, s32[128]{0:T(128)}, u32[]{:S(2)}) copy-start(s32[128]{0:T(128)} %param.14) | copy-start | bytes 1540
  0.0 10.8 %copy-start.19 = (s32[128]{0:T(128)S(1)}, s32[128]{0:T(128)}, u32[]{:S(2)}) copy-start(s32[128]{0:T(128)} %param.15) | copy-start | bytes 1540
  1.1 8.4 %copy-start.27 = (bf16[2,1,512,128]{2,3,0,1:T(8,128)(2,1)}, bf16[2,1,512,128]{2,3,0,1:T(8,128)(2,1)S(1)}, u32[]{:S(2)}) copy-start(bf16[2,1,512,128]{2,3,0,1:T(8,128)(2,1)S(1)} %copy.14) | copy-start | bytes 786436
  1.1 8.5 %collective-permute-start = (bf16[2,512,128]{1,2,0:T(8,128)(2,1)S(1)}, bf16[2,512,128]{1,2,0:T(8,128)(2,1)}, u32[]{:S(2)}, u32[]{:S(2)}) collective-permute-start(bf16[2,512,128]{1,2,0:T(8,128)(2,1)S(1)} %bitcast.51), channel_id=1, source_target_pairs={{0,1},{1,0},{2,3},{3,2},{4,5},{5,4},{6,7},{7,6},{8,9},{9,8},{10,11... | collective-permute-start | bytes 786440 | tf_op jit(solution)/shard_map/ppermute | solution.py:377
  1.9 1.7 %copy-start = (bf16[640,2048]{1,0:T(8,128)(2,1)S(1)}, bf16[640,2048]{1,0:T(8,128)(2,1)}, u32[]{:S(2)}) copy-start(bf16[640,2048]{1,0:T(8,128)(2,1)} %w_ref.5) | copy-start | bytes 7864324
  3.6 0.9 %copy-start.10 = (bf16[2,1,512,128]{3,2,1,0:T(8,128)(2,1)S(1)}, bf16[2,1,512,128]{3,2,1,0:T(8,128)(2,1)}, u32[]{:S(2)}) copy-start(bf16[2,1,512,128]{3,2,1,0:T(8,128)(2,1)} %param.13) | copy-start | bytes 786436
  5.9 0.8 %copy-start.20 = (f32[8,1,2048]{2,1,0:T(1,128)S(1)}, f32[8,1,2048]{2,1,0:T(1,128)}, u32[]{:S(2)}) copy-start(f32[8,1,2048]{2,1,0:T(1,128)} %ph_ref.1) | copy-start | bytes 196612
  6.7 4.1 %copy-start.1 = (bf16[640,2048]{1,0:T(8,128)(2,1)S(1)}, bf16[640,2048]{1,0:T(8,128)(2,1)}, u32[]{:S(2)}) copy-start(bf16[640,2048]{1,0:T(8,128)(2,1)} %w_ref.5) | copy-start | bytes 7864324
  9.6 11.8 %copy-start.12 = (f32[8,2048]{1,0:T(8,128)}, f32[8,2048]{1,0:T(8,128)S(1)}, u32[]{:S(2)}) copy-start(f32[8,2048]{1,0:T(8,128)S(1)} %get-tuple-element.14.refs_3_.cos_ref) | copy-start | bytes 196612
  9.6 11.8 %copy-start.14 = (f32[8,2048]{1,0:T(8,128)}, f32[8,2048]{1,0:T(8,128)S(1)}, u32[]{:S(2)}) copy-start(f32[8,2048]{1,0:T(8,128)S(1)} %get-tuple-element.15.refs_4_.sin_ref) | copy-start | bytes 196612
  10.8 10.6 %copy-start.25 = (s32[512]{0:T(512)S(1)}, s32[512]{0:T(512)}, u32[]{:S(2)}) copy-start(s32[512]{0:T(512)} %param.21) | copy-start | bytes 6148
  13.6 14.6 %all-to-all-start = ((bf16[16,32,256]{2,1,0:T(8,128)(2,1)}), bf16[16,32,256]{2,1,0:T(8,128)(2,1)S(1)}, u32[]{:S(2)}, u32[]{:S(2)}) async-start(bf16[16,32,256]{2,1,0:T(8,128)(2,1)} %bitcast.4), calls=%async_computation | async-start | bytes 524288 | tf_op jit(solution)/shard_map/all_to_all | solution.py:424
  21.4 0.7 %copy-start.21 = (s32[512,8]{0,1:T(8,128)S(1)}, s32[512,8]{0,1:T(8,128)}, u32[]{:S(2)}) copy-start(s32[512,8]{0,1:T(8,128)} %param.19) | copy-start | bytes 49156
  24.7 2.0 %copy-start.2 = (bf16[4096,512]{1,0:T(8,128)(2,1)}, bf16[4096,512]{1,0:T(8,128)(2,1)S(1)}, u32[]{:S(2)}) copy-start(bf16[4096,512]{1,0:T(8,128)(2,1)S(1)} %get-tuple-element.17.hot_ref) | copy-start | bytes 12582916
  26.7 1.4 %copy-start.4 = (bf16[4096,256]{1,0:T(8,128)(2,1)}, bf16[4096,256]{1,0:T(8,128)(2,1)S(1)}, u32[]{:S(2)}) copy-start(bf16[4096,256]{1,0:T(8,128)(2,1)S(1)} %get-tuple-element.18.coef_ref) | copy-start | bytes 6291460
  28.2 2.2 %copy-start.3 = (bf16[4096,512]{1,0:T(8,128)(2,1)S(1)}, bf16[4096,512]{1,0:T(8,128)(2,1)}, u32[]{:S(2)}) copy-start(bf16[4096,512]{1,0:T(8,128)(2,1)} %copy-done.2) | copy-start | bytes 12582916
  30.4 1.6 %copy-start.5 = (bf16[4096,256]{1,0:T(8,128)(2,1)S(1)}, bf16[4096,256]{1,0:T(8,128)(2,1)}, u32[]{:S(2)}) copy-start(bf16[4096,256]{1,0:T(8,128)(2,1)} %copy-done.4) | copy-start | bytes 6291460
  32.0 8.3 %copy-start.28 = (bf16[2,1,512,128]{2,3,0,1:T(8,128)(2,1)S(1)}, bf16[2,1,512,128]{2,3,0,1:T(8,128)(2,1)}, u32[]{:S(2)}) copy-start(bf16[2,1,512,128]{2,3,0,1:T(8,128)(2,1)} %copy-done.27) | copy-start | bytes 786436
  34.2 20.6 %all-to-all-start.1 = ((bf16[16,32,256]{2,1,0:T(8,128)(2,1)}), bf16[16,32,256]{2,1,0:T(8,128)(2,1)S(1)}, u32[]{:S(2)}, u32[]{:S(2)}) async-start(bf16[16,32,256]{2,1,0:T(8,128)(2,1)} %bitcast.11), calls=%async_computation.1 | async-start | bytes 524288 | tf_op jit(solution)/shard_map/all_to_all | solution.py:428
  41.0 19.1 %collective-permute-start.1 = (bf16[2,32,512]{2,1,0:T(8,128)(2,1)}, bf16[2,32,512]{2,1,0:T(8,128)(2,1)}, u32[]{:S(2)}, u32[]{:S(2)}) collective-permute-start(bf16[2,32,512]{2,1,0:T(8,128)(2,1)} %get-tuple-element.24), channel_id=1, source_target_pairs={{0,2},{2,4},{4,6},{6,8},{8,10},{10,12},{12,14},{14,16},{16,18},{18... | collective-permute-start | bytes 196616 | tf_op jit(solution)/shard_map/ppermute | solution.py:377
  44.1 16.0 %collective-permute-start.2 = (bf16[2,32,512]{2,1,0:T(8,128)(2,1)}, bf16[2,32,512]{2,1,0:T(8,128)(2,1)}, u32[]{:S(2)}, u32[]{:S(2)}) collective-permute-start(bf16[2,32,512]{2,1,0:T(8,128)(2,1)} %get-tuple-element.23), channel_id=1, source_target_pairs={{2,0},{4,2},{6,4},{8,6},{10,8},{12,10},{14,12},{16,14},{18,16},{20... | collective-permute-start | bytes 196616 | tf_op jit(solution)/shard_map/ppermute | solution.py:377
  49.3 0.8 %copy-start.13 = (f32[8,2048]{1,0:T(8,128)S(1)}, f32[8,2048]{1,0:T(8,128)}, u32[]{:S(2)}) copy-start(f32[8,2048]{1,0:T(8,128)} %copy-done.12) | copy-start | bytes 196612
  50.1 0.8 %copy-start.15 = (f32[8,2048]{1,0:T(8,128)S(1)}, f32[8,2048]{1,0:T(8,128)}, u32[]{:S(2)}) copy-start(f32[8,2048]{1,0:T(8,128)} %copy-done.14) | copy-start | bytes 196612
  51.0 9.2 %copy-start.24 = (s32[128,8]{0,1:T(8,128)S(1)}, s32[128,8]{0,1:T(8,128)}, u32[]{:S(2)}) copy-start(s32[128,8]{0,1:T(8,128)} %param.17) | copy-start | bytes 12292
  52.8 1.0 %copy-start.6 = (f32[128,2048]{1,0:T(8,128)}, f32[128,2048]{1,0:T(8,128)S(1)}, u32[]{:S(2)}) copy-start(f32[128,2048]{1,0:T(8,128)S(1)} %get-tuple-element.19.cos_ref) | copy-start | bytes 3145732
  53.8 1.0 %copy-start.8 = (f32[128,2048]{1,0:T(8,128)}, f32[128,2048]{1,0:T(8,128)S(1)}, u32[]{:S(2)}) copy-start(f32[128,2048]{1,0:T(8,128)S(1)} %get-tuple-element.20.sin_ref) | copy-start | bytes 3145732
  54.8 5.4 %copy-start.23 = (s32[128,8]{0,1:T(8,128)S(1)}, s32[128,8]{0,1:T(8,128)}, u32[]{:S(2)}) copy-start(s32[128,8]{0,1:T(8,128)} %param.16) | copy-start | bytes 12292
  54.8 5.4 %copy-start.26 = (s32[128]{0:T(128)S(1)}, s32[128]{0:T(128)}, u32[]{:S(2)}) copy-start(s32[128]{0:T(128)} %param.18) | copy-start | bytes 1540
  54.8 1.2 %copy-start.7 = (f32[128,2048]{1,0:T(8,128)S(1)}, f32[128,2048]{1,0:T(8,128)}, u32[]{:S(2)}) copy-start(f32[128,2048]{1,0:T(8,128)} %copy-done.6) | copy-start | bytes 3145732
  56.0 1.2 %copy-start.9 = (f32[128,2048]{1,0:T(8,128)S(1)}, f32[128,2048]{1,0:T(8,128)}, u32[]{:S(2)}) copy-start(f32[128,2048]{1,0:T(8,128)} %copy-done.8) | copy-start | bytes 3145732
  57.2 2.9 %copy-start.11 = (bf16[2,1,512,128]{3,2,1,0:T(8,128)(2,1)S(1)}, bf16[2,1,512,128]{3,2,1,0:T(8,128)(2,1)}, u32[]{:S(2)}) copy-start(bf16[2,1,512,128]{3,2,1,0:T(8,128)(2,1)} %param.13) | copy-start | bytes 786436
  58.4 6.3 %collective-permute-start.3 = (bf16[2,2,64,128]{3,2,1,0:T(8,128)(2,1)S(1)}, bf16[2,2,64,128]{3,2,1,0:T(8,128)(2,1)S(1)}, u32[]{:S(2)}, u32[]{:S(2)}) collective-permute-start(bf16[2,2,64,128]{3,2,1,0:T(8,128)(2,1)S(1)} %get-tuple-element.22), channel_id=1, source_target_pairs={{0,1},{1,0},{2,3},{3,2},{4,5},{5,4},{6,7},{7,6},{8,9},{9,8},{10,11... | collective-permute-start | bytes 196616 | tf_op jit(solution)/shard_map/ppermute | solution.py:377
  (3 other events, 2.0 us)

commit v2 on v1

v2 whole, which is shorter than its diff:
```python
import jax
import jax.numpy as jnp
from jax import lax
from jax.experimental import pallas as pl
from jax.experimental.pallas import tpu as pltpu
from jax.sharding import PartitionSpec as P

NEARB = 32
OCTANTS = 8
LANES = 128
CHUNK = 128
f32, bf16, i32 = jnp.float32, jnp.bfloat16, jnp.int32
V, H = pltpu.VMEM, pltpu.HBM


class Fetched:
    def __init__(self, source, room, semaphore):
        self.copy = pltpu.make_async_copy(source, room, semaphore)
        self.room, self.waited = room, False
        self.copy.start()

    def __call__(self):
        if not self.waited:
            self.copy.wait()
            self.waited = True
        return self.room


def call(body, args, places, outs, name, rooms=(), scratch=(), flops=1 << 20, moved=1 << 20, limit=16 << 20):
    rooms = dict(rooms)
    fetched = [i for i, place in enumerate(places) if place is H and rooms.get(i, 0) is not None]
    spaces = [
        pltpu.VMEM(rooms.get(i, args[i].shape), args[i].dtype) for i in fetched
    ]

    def kernel(*refs):
        ins = list(refs[: len(args)])
        results = refs[len(args) : len(args) + len(outs)]
        rest = refs[len(args) + len(outs) :]
        held, rest = rest[: len(fetched)], rest[len(fetched) :]
        if fetched:
            semaphores, rest = rest[0], rest[1:]
            for n, i in enumerate(fetched):
                ins[i] = Fetched(ins[i], held[n], semaphores.at[n])
        body(ins, results, rest)

    semaphores = [pltpu.SemaphoreType.DMA((len(fetched),))] if fetched else []
    args = [
        pltpu.with_memory_space_constraint(arg, H) if place is H else arg for arg, place in zip(args, places)
    ]
    return pl.pallas_call(
        kernel,
        out_shape=[
            jax.ShapeDtypeStruct(shape, dtype) if place is None else place(shape, dtype)
            for shape, dtype, place in outs
        ],
        in_specs=[pl.BlockSpec(memory_space=place) for place in places],
        out_specs=[pl.BlockSpec(memory_space=place or V) for _, _, place in outs],
        scratch_shapes=spaces + semaphores + list(scratch),
        name=name,
        cost_estimate=pl.CostEstimate(flops=flops, bytes_accessed=moved, transcendentals=0),
        compiler_params=pltpu.CompilerParams(vmem_limit_bytes=limit),
    )(*args)


def nt(a, b):
    return lax.dot_general(a, b, (((1,), (1,)), ((), ())), preferred_element_type=f32)


def tn(a, b):
    return lax.dot_general(a, b, (((0,), (0,)), ((), ())), preferred_element_type=f32)


def nn(a, b):
    return lax.dot_general(a, b, (((1,), (0,)), ((), ())), preferred_element_type=f32)


def iota(shape, dim):
    return lax.broadcasted_iota(i32, shape, dim)


def ones_where(mask):
    return jnp.where(mask, 1.0, 0.0).astype(bf16)


def identity(n):
    return ones_where(iota((n, n), 0) == iota((n, n), 1))


def sincos(x):
    h = 0.5 * x
    q = h * h
    s = -2.50521083854417e-08 + q * 1.60590438368216e-10
    s = 2.75573192239859e-06 + q * s
    s = -1.98412698412698e-04 + q * s
    s = 8.33333333333333e-03 + q * s
    s = -1.66666666666667e-01 + q * s
    s = h + h * (q * s)
    c = 2.08767569878681e-09 + q * -1.14707455977297e-11
    c = -2.75573192239859e-07 + q * c
    c = 2.48015873015873e-05 + q * c
    c = -1.38888888888889e-03 + q * c
    c = 4.16666666666667e-02 + q * c
    c = -0.5 + q * c
    c = 1.0 + q * c
    return 2.0 * (s * c), 1.0 - 2.0 * (s * s)


def parts(x):
    high = x.astype(bf16)
    rest = x - high.astype(f32)
    middle = rest.astype(bf16)
    return [high, middle, (rest - middle.astype(f32)).astype(bf16)]


def phase_rows(cosine, sine):
    halves = [jnp.concatenate(parts(x) + [jnp.zeros(x.shape, bf16)], axis=0) for x in (cosine, sine)]
    return jnp.concatenate(halves, axis=1)


def octant_rows(octant, boxes):
    onehot = ones_where(iota((OCTANTS, boxes), 0) == octant)
    return jnp.concatenate([onehot] * 4, axis=0)


def prepare(own, octant, parent, phase, weights, parents):
    _, kcg, boxes = own.shape
    rows, kpg = weights.shape
    rim = (rows - kcg) // 2
    width = 512

    def body(ins, outs, rest):
        own_in, oct_in, par_in, ph_in, w_hbm = ins
        cos_ref, sin_ref, y_ref, w_ref, family_ref, phase_out, lead_out, trail_out = outs
        e_ref, phase_ref, sems = rest
        pieces = [
            pltpu.make_async_copy(
                w_hbm.at[:, pl.ds(n * (kpg // 2), kpg // 2)], w_ref.at[:, pl.ds(n * (kpg // 2), kpg // 2)], sems.at[n]
            )
            for n in range(2)
        ]
        for piece in pieces:
            piece.start()
        eye = identity(boxes)
        me = lax.axis_index("box")
        family = ones_where(iota((parents, boxes), 0) == par_in()[...] - me * parents)
        family_ref[...] = jnp.concatenate([family, family], axis=1)
        onehot = octant_rows(oct_in()[...], boxes)
        sine, cosine = sincos(ph_in()[:, 0, :])
        phase_ref[...] = phase_rows(cosine, sine)
        room = own_in()
        for r in range(2):
            e_ref[r * boxes : (r + 1) * boxes] = nt(eye, room[r]).astype(bf16)
        odd = lax.rem(me, 2)
        copies = [pltpu.make_async_copy(phase_ref, phase_out, sems.at[2])]
        for n, out in enumerate((lead_out, trail_out)):
            begin = pl.multiple_of(jnp.where(odd == n, boxes - NEARB, 0), NEARB)
            for r in range(2):
                copies.append(
                    pltpu.make_async_copy(
                        e_ref.at[pl.ds(r * boxes + begin, NEARB)], out.at[r], sems.at[3 + 2 * n + r]
                    )
                )
        for copy in copies:
            copy.start()
        cos_ref[...] = tn(onehot, phase_ref[:, :kpg])
        sin_ref[...] = tn(onehot, phase_ref[:, kpg:])
        for n, piece in enumerate(pieces):
            piece.wait()
            for step in range(kpg // 2 // width):
                begin = n * (kpg // 2) + step * width
                cols = slice(begin, begin + width)
                y_ref[:, cols] = nn(e_ref[...], w_ref[rim : rim + kcg, cols])
        for copy in copies:
            copy.wait()

    wave = ((boxes, kpg), f32, V)
    edge = ((2, NEARB, kcg), bf16, H)
    phases = (4 * OCTANTS, 2 * kpg)
    return call(
        body,
        [own, octant, parent, phase, weights],
        [H] * 5,
        [
            wave,
            wave,
            ((2 * boxes, kpg), f32, V),
            (weights.shape, bf16, V),
            ((parents, 2 * boxes), bf16, V),
            (phases, bf16, H),
            edge,
            edge,
        ],
        "prepare",
        rooms={4: None},
        scratch=[pltpu.VMEM((2 * boxes, kcg), bf16), pltpu.VMEM(phases, bf16), pltpu.SemaphoreType.DMA((7,))],
        flops=2 * 2 * boxes * kcg * kpg,
    )


def rise(rims, spans, family, cosine, sine, inner, weights, parents, packed):
    boxes, kpg = cosine.shape
    rows = weights.shape[0]
    rim = spans[0][2] - spans[0][1]
    width = 256
    shape = (kpg // LANES * parents, 2 * LANES) if packed else (2, parents, kpg)

    def body(ins, outs, rest):
        sides = ins[: len(rims)]
        family_ref, cos_ref, sin_ref, y_ref, w_ref = ins[len(rims) :]
        (out_hbm,) = outs
        out_ref, e_ref, wr_ref, shift_ref, sems = rest
        eye = identity(boxes)
        wr_ref[:rim] = w_ref[:rim]
        wr_ref[rim:] = w_ref[rows - rim :]
        for r in range(2):
            for side, (n, low, high) in enumerate(spans):
                e_ref[r * boxes : (r + 1) * boxes, side * rim : (side + 1) * rim] = nt(
                    eye, sides[n][r, low:high, :]
                ).astype(bf16)
        for step in range(kpg // width):
            cols = slice(step * width, (step + 1) * width)
            y = y_ref[:, cols] + nn(e_ref[...], wr_ref[:, cols])
            yr, yi, c, s = y[:boxes], y[boxes:], cos_ref[:, cols], sin_ref[:, cols]
            for r, value in enumerate((yr * c - yi * s, yr * s + yi * c)):
                high = value.astype(bf16)
                shift_ref[r, :boxes, cols] = high
                shift_ref[r, boxes:, cols] = (value - high.astype(f32)).astype(bf16)
        for step in range(kpg // width):
            cols = slice(step * width, (step + 1) * width)
            for r in range(2):
                total = nn(family_ref[...], shift_ref[r, :, cols]).astype(bf16)
                if packed:
                    for part in range(width // LANES):
                        row = (step * (width // LANES) + part) * parents
                        out_ref[row : row + parents, r * LANES : (r + 1) * LANES] = total[
                            :, part * LANES : (part + 1) * LANES
                        ]
                else:
                    out_ref[r, :, cols] = total
        copy = pltpu.make_async_copy(out_ref, out_hbm, sems)
        copy.start()
        copy.wait()

    return call(
        body,
        [*rims, family, cosine, sine, inner, weights],
        [V] * (len(rims) + 5),
        [(shape, bf16, H)],
        "rise",
        scratch=[
            pltpu.VMEM(shape, bf16),
            pltpu.VMEM((2 * boxes, 2 * rim), bf16),
            pltpu.VMEM((2 * rim, kpg), bf16),
            pltpu.VMEM((2, 2 * boxes, kpg), bf16),
            pltpu.SemaphoreType.DMA,
        ],
        flops=2 * 2 * boxes * 2 * rim * kpg,
    )[0]


def operators_of_lists(offsets, counts, table):
    slots, boxes = offsets.shape
    operators, lanes = table.shape

    def body(ins, outs, rest):
        off_in, cnt_in, tab_in = ins
        (coef_out,) = outs
        coef_ref, sems = rest
        off = jnp.where(iota((slots, boxes), 0) < cnt_in()[...], off_in()[...], -1).T
        size = slots * CHUNK
        copies = []
        for chunk in range(boxes // CHUNK):
            rows = slice(chunk * CHUNK, (chunk + 1) * CHUNK)
            pick = jnp.concatenate(
                [ones_where(off[rows, m : m + 1] == iota((CHUNK, operators), 1)) for m in range(slots)], axis=0
            )
            coef_ref[chunk * size : (chunk + 1) * size] = nn(pick, tab_in()[...]).astype(bf16)
            part = pl.ds(chunk * size, size)
            copies.append(pltpu.make_async_copy(coef_ref.at[part], coef_out.at[part], sems.at[chunk]))
            copies[-1].start()
        for copy in copies:
            copy.wait()

    return call(
        body,
        [offsets, counts, table],
        [H, H, H],
        [((slots * boxes, lanes), bf16, H)],
        "operators_of_lists",
        scratch=[pltpu.VMEM((slots * boxes, lanes), bf16), pltpu.SemaphoreType.DMA((boxes // CHUNK,))],
        flops=2 * slots * boxes * operators * lanes,
    )[0]


def parent_sums(pattern, sources, coef):
    total, lanes = pattern.shape
    slots = sources.shape[0]
    half = lanes // 2
    size = slots * CHUNK
    chunks = total // CHUNK
    halves = 2

    def body(ins, outs, rest):
        pat_ref, src_in, coef_in = ins
        (out_hbm,) = outs
        pick_ref, out_ref, sems = rest
        src = src_in()[...].T
        for chunk in range(chunks):
            rows = slice(chunk * CHUNK, (chunk + 1) * CHUNK)
            hot = jnp.concatenate(
                [ones_where(src[rows, m : m + 1] == iota((CHUNK, total), 1)) for m in range(slots)], axis=0
            )
            pick_ref[chunk * size : (chunk + 1) * size] = nn(hot, pat_ref[...])
        coef_ref = coef_in()
        copies = []
        for chunk in range(chunks):
            real = imag = 0.0
            for m in range(slots):
                part = slice(chunk * size + m * CHUNK, chunk * size + (m + 1) * CHUNK)
                pr, pi = pick_ref[part, :half], pick_ref[part, half:]
                c = coef_ref[part].astype(f32)
                cr, ci = c[:, :half], c[:, half:]
                real += cr * pr - ci * pi
                imag += cr * pi + ci * pr
            rows = slice(chunk * CHUNK, (chunk + 1) * CHUNK)
            out_ref[rows, :half] = real.astype(bf16)
            out_ref[rows, half:] = imag.astype(bf16)
            if (chunk + 1) % (chunks // halves) == 0:
                part = pl.ds(len(copies) * (total // halves), total // halves)
                copies.append(
                    pltpu.make_async_copy(out_ref.at[part], out_hbm.at[part], sems.at[len(copies)])
                )
                copies[-1].start()
        for copy in copies:
            copy.wait()

    return call(
        body,
        [pattern, sources, coef],
        [V, H, H],
        [((total, lanes), bf16, H)],
        "parent_sums",
        scratch=[
            pltpu.VMEM((slots * total, lanes), f32),
            pltpu.VMEM((total, lanes), bf16),
            pltpu.SemaphoreType.DMA((halves,)),
        ],
        flops=2 * slots * total * total * lanes,
        limit=24 << 20,
    )[0]


def lower(far, parent, octant, phases, weights, parents, rim, packed):
    boxes = parent.shape[1]
    rows, kpg = weights.shape
    width = LANES if packed else 256

    def body(ins, outs, rest):
        far_ref, par_in, oct_in, phase_in, w_ref = ins
        low_ref, rim_ref = outs
        base = lax.axis_index("box") * parents
        hot = ones_where(iota((parents, boxes), 0) == par_in()[...] - base).T
        onehot = octant_rows(oct_in()[...], boxes).T
        phase_ref = phase_in()
        for step in range(kpg // width):
            cols = slice(step * width, (step + 1) * width)
            if packed:
                spread = nn(hot, far_ref[step * parents : (step + 1) * parents])
                sr, si = spread[:, :LANES], spread[:, LANES:]
            else:
                sr, si = nn(hot, far_ref[0, :, cols]), nn(hot, far_ref[1, :, cols])
            sine_cols = slice(kpg + step * width, kpg + (step + 1) * width)
            both = nn(onehot, jnp.concatenate([phase_ref[:, cols], phase_ref[:, sine_cols]], axis=1))
            c, s = both[:, :width], both[:, width:]
            low_ref[:boxes, cols] = (sr * c + si * s).astype(bf16)
            low_ref[boxes:, cols] = (si * c - sr * s).astype(bf16)
        first = nt(w_ref[:rim], low_ref[...]).astype(bf16)
        last = nt(w_ref[rows - rim :], low_ref[...]).astype(bf16)
        for side, terms in enumerate((first, last)):
            for r in range(2):
                rim_ref[side, r] = terms[:, r * boxes : (r + 1) * boxes]

    return call(
        body,
        [far, parent, octant, phases, weights],
        [V, H, H, H, V],
        [((2 * boxes, kpg), bf16, V), ((2, 2, rim, boxes), bf16, V)],
        "lower",
        flops=2 * 2 * boxes * kpg * 2 * rim,
    )


def anterpolate(weights, lowered, nearby, rim):
    _, kcg, boxes = nearby.shape

    def body(ins, outs, rest):
        w_ref, low_ref, near_in = ins
        (out_ref,) = outs
        terms = nt(w_ref[rim : rim + kcg], low_ref[...]).astype(bf16).astype(f32)
        for r in range(2):
            out_ref[r] = near_in()[r] + terms[:, r * boxes : (r + 1) * boxes]

    return call(
        body,
        [weights, lowered, nearby],
        [V, V, H],
        [(nearby.shape, f32, V)],
        "anterpolate",
        flops=2 * kcg * weights.shape[1] * 2 * boxes,
    )[0]


def finish(partial, start_terms, end_terms):
    _, kcg, boxes = partial.shape
    rim = start_terms[0].shape[-2]
    arrays = [start_terms[0]] if end_terms[0] is start_terms[0] else [start_terms[0], end_terms[0]]

    def body(ins, outs, rest):
        sum_ref, start_ref, end_ref = ins[0], ins[1], ins[-1]
        (out_ref,) = outs
        start = start_ref[...] if start_terms[1] is None else start_ref[start_terms[1]]
        end = end_ref[...] if end_terms[1] is None else end_ref[end_terms[1]]
        out_ref[:, rim : kcg - rim] = sum_ref[:, rim : kcg - rim].astype(bf16)
        out_ref[:, :rim] = (sum_ref[:, :rim] + start.astype(f32)).astype(bf16)
        out_ref[:, kcg - rim :] = (sum_ref[:, kcg - rim :] + end.astype(f32)).astype(bf16)

    return call(
        body, [partial, *arrays], [V] * (1 + len(arrays)), [(partial.shape, bf16, None)], "finish"
    )[0]


def near_sums(own, lead, trail, sources, offsets, counts, table):
    _, kcg, boxes = own.shape
    slots = sources.shape[0]
    operators = table.shape[1]
    depth = 2 * boxes
    pair = 2

    def body(ins, outs, rest):
        own_in, lead_in, trail_in, src_in, off_in, cnt_in, tab_in = ins
        (near_out,) = outs
        out_ref, ext_ref, tt_ref, sem = rest
        eye = identity(boxes)
        own_ref, tab_ref = own_in(), tab_in()
        for r in range(2):
            rows = slice(r * kcg, (r + 1) * kcg)
            ext_ref[rows, :boxes] = own_ref[r]
            for step in range(kcg // boxes):
                cols = slice(step * boxes, (step + 1) * boxes)
                part = slice(r * kcg + step * boxes, r * kcg + (step + 1) * boxes)
                tt_ref[part] = nt(eye, tab_ref[r, :, cols]).astype(bf16)
        lead_ref, trail_ref = lead_in(), trail_in()
        for r in range(2):
            for step in range(kcg // boxes):
                cols = slice(step * boxes, (step + 1) * boxes)
                part = slice(r * kcg + step * boxes, r * kcg + (step + 1) * boxes)
                halo = jnp.concatenate(
                    [lead_ref[r, :, cols], trail_ref[r, :, cols], jnp.zeros((boxes - 2 * NEARB, boxes), bf16)],
                    axis=0,
                )
                ext_ref[part, boxes:] = nt(eye, halo).astype(bf16)
        me = lax.axis_index("box")
        odd = lax.rem(me, 2)
        rel = src_in()[...] - me * boxes
        below = rel + (boxes + NEARB) + (1 - odd) * NEARB
        above = rel + odd * NEARB
        rel = jnp.where(rel < 0, below, jnp.where(rel >= boxes, above, rel))
        off = jnp.where(iota((slots, boxes), 0) < cnt_in()[...], off_in()[...], -1)
        for m in range(0, slots, pair):
            src = jnp.concatenate([rel[m + j : m + j + 1] for j in range(pair)], axis=1)
            ops = jnp.concatenate([off[m + j : m + j + 1] for j in range(pair)], axis=1)
            hot = ones_where(iota((depth, pair * boxes), 0) == src)
            pick = ones_where(iota((operators, pair * boxes), 0) == ops)
            picked = nn(ext_ref[...], hot)
            coef = nn(tt_ref[...], pick)
            pr, pi, cr, ci = picked[:kcg], picked[kcg:], coef[:kcg], coef[kcg:]
            real, imag = cr * pr - ci * pi, cr * pi + ci * pr
            for r, value in enumerate((real, imag)):
                value = sum(value[:, j * boxes : (j + 1) * boxes] for j in range(pair))
                out_ref[r] = value if m == 0 else out_ref[r] + value
        copy = pltpu.make_async_copy(out_ref, near_out, sem)
        copy.start()
        copy.wait()

    return call(
        body,
        [own, lead, trail, sources, offsets, counts, table],
        [H] * 7,
        [(own.shape, f32, H)],
        "near_sums",
        scratch=[
            pltpu.VMEM(own.shape, f32),
            pltpu.VMEM((2 * kcg, depth), bf16),
            pltpu.VMEM((2 * kcg, operators), bf16),
            pltpu.SemaphoreType.DMA,
        ],
        flops=2 * slots * boxes * 2 * kcg * (depth + operators),
        limit=24 << 20,
    )[0]


def plain_translate(pattern, table, sources, offsets, counts):
    coef = jnp.transpose(table, (0, 2, 1))

    def advance(m, summed):
        src = lax.dynamic_index_in_dim(sources, m, 0, keepdims=False)
        off = lax.dynamic_index_in_dim(offsets, m, 0, keepdims=False)
        p = pattern[:, :, src].astype(f32)
        c = coef[:, :, off].astype(f32) * (m < counts).astype(f32)
        return summed + jnp.stack([c[0] * p[0] - c[1] * p[1], c[0] * p[1] + c[1] * p[0]])

    return lax.fori_loop(
        0, sources.shape[0], advance, jnp.zeros(pattern.shape[:2] + (sources.shape[1],), f32)
    )


def shift(value, axis, step):
    peers = lax.axis_size(axis)
    return lax.ppermute(value, axis, [(i, (i + step) % peers) for i in range(peers)])


def exchange(value, axis, first):
    peers = lax.axis_size(axis)
    pairs = [(i, i + 1) for i in range(first, peers - 1, 2)]
    return lax.ppermute(value, axis, pairs + [(j, i) for i, j in pairs])


def local(
    child_pattern,
    child_parent,
    child_octant,
    child_sources,
    child_offsets,
    child_counts,
    parent_sources,
    parent_offsets,
    parent_counts,
    interp_weights,
    shift_phase,
    child_table,
    parent_table,
):
    own = child_pattern[:, 0]
    _, kcg, boxes = own.shape
    rim = (interp_weights.shape[0] - kcg) // 2
    peers, groups = lax.axis_size("box"), lax.axis_size("samp")
    total = parent_sources.shape[0]
    parents = total // peers
    kpg = interp_weights.shape[1]
    mine = kpg // peers
    packed = mine == LANES and total % CHUNK == 0
    parent, octant = child_parent[None, :], child_octant[None, :]

    if groups == 2:
        rims = [shift(own, "samp", 1)]
        spans = ((0, kcg - rim, kcg), (0, 0, rim))
    else:
        rims = [shift(own[:, kcg - rim :], "samp", 1), shift(own[:, :rim], "samp", -1)]
        spans = ((0, 0, rim), (1, 0, rim))
    cosine, sine, inner, weights, family, phases, lead, trail = prepare(
        own, octant, parent, shift_phase, interp_weights, parents
    )
    pattern = rise(rims, spans, family, cosine, sine, inner, weights, parents, packed)
    lead, trail = exchange(lead, "box", 0), exchange(trail, "box", 1)

    table = parent_table[:, :, 0, :]
    if packed:
        regrouped = lax.all_to_all(pattern, "box", split_axis=0, concat_axis=0, tiled=True)
        regrouped, lead, trail = lax.optimization_barrier((regrouped, lead, trail))
        flat_table = jnp.transpose(table, (1, 0, 2)).reshape(table.shape[1], 2 * mine)
        coef = operators_of_lists(parent_offsets.T, parent_counts[None, :], flat_table)
        far = parent_sums(regrouped, parent_sources.T, coef)
        returned = lax.all_to_all(far, "box", split_axis=0, concat_axis=0, tiled=True)
    else:
        regrouped = lax.all_to_all(pattern, "box", split_axis=2, concat_axis=1, tiled=True)
        far = plain_translate(
            jnp.transpose(regrouped, (0, 2, 1)), table, parent_sources.T, parent_offsets.T, parent_counts
        ).astype(bf16)
        far = jnp.transpose(far, (0, 2, 1))
        returned = lax.all_to_all(far, "box", split_axis=1, concat_axis=2, tiled=True)

    nearby = near_sums(
        own,
        lead,
        trail,
        child_sources.T,
        child_offsets.T,
        child_counts[None, :],
        child_table[:, :, 0, :],
    )
    returned, nearby = lax.optimization_barrier((returned, nearby))
    lowered, terms = lower(returned, parent, octant, phases, interp_weights, parents, rim, packed)
    if groups == 2:
        got = shift(terms, "samp", 1)
        start_terms, end_terms = (got, 1), (got, 0)
    else:
        start_terms = (shift(terms[1], "samp", 1), None)
        end_terms = (shift(terms[0], "samp", -1), None)
    partial = anterpolate(interp_weights, lowered, nearby, rim)
    return finish(partial, start_terms, end_terms)[:, None]


def solution(mesh):
    return jax.shard_map(
        local,
        mesh=mesh,
        in_specs=(
            P(None, "samp", None, "box"),
            P("box"),
            P("box"),
            P("box", None),
            P("box", None),
            P("box"),
            P(),
            P(),
            P(),
            P(),
            P(None, "samp", None),
            P(None, None, "samp", None),
            P(None, None, "samp", "box"),
        ),
        out_specs=P(None, "samp", None, "box"),
        check_vma=False,
    )
```

time: 66.4 us -> 48 us (0.72)
  the two profiles are of different devices: /device:TPU:9 before, /device:TPU:0 now
where the time goes in v2:
time: 48 us; the launch traced here: 47.5 us
  Pallas kernels  22.4 us (47%)
  starting transfers between devices  15.8 us (33%)
  waiting for transfers between devices  7.2 us (15%)
  local copies, waits for them, and re-layouts  1.77 us (4%)
    pallas_call x8, Pallas kernels, call(): pl.pallas_call(kernel, out_shape=[jax.ShapeDtypeStruct(shape, dtype) if p...  22.4 us
    all_to_all x1, starting transfers between devices, local(): lax.all_to_all(pattern, 'box', split_axis=0, concat_axis=0, tiled=True)  7.87 us
    all_to_all x1, starting transfers between devices, local(): lax.all_to_all(far, 'box', split_axis=0, concat_axis=0, tiled=True)  4.79 us
    all_to_all x1, waiting for transfers between devices, local(): lax.all_to_all(far, 'box', split_axis=0, concat_axis=0, tiled=True)  3.62 us
    all_to_all x1, waiting for transfers between devices, local(): lax.all_to_all(pattern, 'box', split_axis=0, concat_axis=0, tiled=True)  3.56 us
    ppermute x2, starting transfers between devices, exchange(): return lax.ppermute(value, axis, pairs + [(j, i) for i, j in pairs])  2.64 us
    unnamed x17, local copies, waits for them, and re-layouts  1.77 us
  transfers between devices with their start and end apart: 6, of which 2 were waited for; matrix products, arithmetic and copies ran while one was open for 4% of the time, Pallas kernels for 29%

profile of v2, /device:TPU:0, one launch (start us, length us, event | category | flops | bytes accessed | tf_op | source)
XLA Modules:
  0.0 47.5 jit_solution(15223351000706043054)
XLA Ops:
  0.0 0.5 collective-permute-start
  0.5 3.7 %prepare.1 = (f32[128,2048]{1,0:T(8,128)S(1)}, f32[128,2048]{1,0:T(8,128)S(1)}, f32[256,2048]{1,0:T(8,128)S(1)}, bf16[640,2048]{1,0:T(8,128)(2,1)S(1)}, bf16[32,...) custom-call(bf16[2,512,128]{2,1,0:T(8,128)(2,1)} %bitcast.32, ...), custom_call_target="tpu_custom_call" | custom-call | flops 536870912 | bytes 1048576 | tf_op jit(solution)/shard_map/prepare/pallas_call | solution.py:51
  4.1 0.0 collective-permute-done.refs_0_
  4.1 0.0 copy-start.5
  4.2 0.0 copy-start.3
  4.2 0.0 copy-start.2
  4.2 2.0 %rise.1 = bf16[512,256]{1,0:T(8,128)(2,1)} custom-call(bf16[2,512,128]{2,1,0:T(8,128)(2,1)S(1)} %collective-permute-done.refs_0_, bf16[32,256]{1,0:T(8,128)(2,1)S(1)} %get-tuple-element.20.refs_1_, f32[128,2048]{1,0:T(8,128)S(1)} %get-tuple-element.21.refs_2_, f32[128,2048]{1,0:T(8,128)S(1)} %get-tuple-element.22.refs_3_, ...), custom_call_target="tpu_custom_call" | custom-call | flops 134217728 | bytes 1048576 | tf_op jit(solution)/shard_map/rise/pallas_call | solution.py:51
  6.2 7.9 %all-to-all-start = ((bf16[16,32,256]{2,1,0:T(8,128)(2,1)}), bf16[16,32,256]{2,1,0:T(8,128)(2,1)S(1)}, u32[]{:S(2)}, u32[]{:S(2)}) async-start(bf16[16,32,256]{2,1,0:T(8,128)(2,1)} %bitcast.27), calls=%async_computation | async-start | bytes 524288 | tf_op jit(solution)/shard_map/all_to_all | solution.py:569
  14.1 0.0 copy-done.5
  14.1 2.0 %collective-permute-start.1 = (bf16[2,32,512]{2,1,0:T(8,128)(2,1)S(1)}, bf16[2,32,512]{2,1,0:T(8,128)(2,1)S(1)}, u32[]{:S(2)}, u32[]{:S(2)}) collective-permute-start(bf16[2,32,512]{2,1,0:T(8,128)(2,1)S(1)} %copy-done.5), channel_id=1, source_target_pairs={{0,2},{4,6},{8,10},{12,14},{16,18},{20,22},{24,26},{28,30},{2,0},{... | collective-permute-start | bytes 196616 | tf_op jit(solution)/shard_map/ppermute | solution.py:526
  16.1 0.0 copy-done.3
  16.1 0.7 %collective-permute-start.2 = (bf16[2,32,512]{2,1,0:T(8,128)(2,1)S(1)}, bf16[2,32,512]{2,1,0:T(8,128)(2,1)S(1)}, u32[]{:S(2)}, u32[]{:S(2)}) collective-permute-start(bf16[2,32,512]{2,1,0:T(8,128)(2,1)S(1)} %copy-done.3), channel_id=1, source_target_pairs={{2,4},{6,8},{10,12},{14,16},{18,20},{22,24},{26,28},{4,2},{8,6},{1... | collective-permute-start | bytes 196616 | tf_op jit(solution)/shard_map/ppermute | solution.py:526
  16.7 0.1 pad
  16.9 0.7 %copy.16 = bf16[40,8,2,128]{3,1,2,0:T(8,128)(2,1)} copy(bf16[40,8,2,128]{3,2,1,0:T(2,128)(2,1)S(1)} %bitcast.29) | data formatting | bytes 327680
  17.6 3.4 %operators_of_lists.1.refs_2_ = bf16[4096,256]{1,0:T(8,128)(2,1)} custom-call(s32[8,512]{1,0:T(8,128)} %bitcast.40, s32[1,512]{1,0:T(1,128)} %bitcast.44, bf16[316,256]{1,0:T(8,128)(2,1)} %bitcast.34), custom_call_target="tpu_custom_call" | custom-call | flops 662700032 | bytes 1048576 | tf_op jit(solution)/shard_map/operators_of_lists/pallas_call | solution.py:51
  21.0 0.0 copy-start.1
  21.0 0.0 collective-permute-done.1.refs_1_
  21.0 0.0 collective-permute-done.2.refs_2_
  21.1 3.6 %all-to-all-done = bf16[16,32,256]{2,1,0:T(8,128)(2,1)S(1)} async-done(((bf16[16,32,256]{2,1,0:T(8,128)(2,1)}), bf16[16,32,256]{2,1,0:T(8,128)(2,1)S(1)}, u32[]{:S(2)}, u32[]{:S(2)}) %all-to-all-start) | async-done | bytes 262176 | tf_op jit(solution)/shard_map/all_to_all | solution.py:569
  24.6 3.7 %parent_sums.1 = bf16[512,256]{1,0:T(8,128)(2,1)} custom-call(bf16[512,256]{1,0:T(8,128)(2,1)S(1)} %bitcast.26, s32[8,512]{1,0:T(8,128)} %bitcast.41, bf16[4096,256]{1,0:T(8,128)(2,1)} %operators_of_lists.1.refs_2_), custom_call_target="tpu_custom_call" | custom-call | flops 1073741824 | bytes 1048576 | tf_op jit(solution)/shard_map/parent_sums/pallas_call | solution.py:51
  28.4 0.0 copy-done.4
  28.4 0.0 copy-done.6
  28.4 4.8 %all-to-all-start.1 = ((bf16[16,32,256]{2,1,0:T(8,128)(2,1)}), bf16[16,32,256]{2,1,0:T(8,128)(2,1)S(1)}, u32[]{:S(2)}, u32[]{:S(2)}) async-start(bf16[16,32,256]{2,1,0:T(8,128)(2,1)} %bitcast.30), calls=%async_computation.1 | async-start | bytes 524288 | tf_op jit(solution)/shard_map/all_to_all | solution.py:574
  33.2 0.0 copy-start
  33.2 0.9 %copy.18 = bf16[2,316,1,512]{3,1,0,2:T(8,128)(2,1)} copy(bf16[2,316,1,512]{3,0,2,1:T(2,128)(2,1)S(1)} %copy-done.1) | data formatting | bytes 1294336 | tf_op args[11]
  34.1 4.9 %near_sums.1.refs_2_ = f32[2,512,128]{2,1,0:T(8,128)} custom-call(bf16[2,512,128]{2,1,0:T(8,128)(2,1)} %bitcast.33, bf16[2,32,512]{2,1,0:T(8,128)(2,1)} %copy-done.4, bf16[2,32,512]{2,1,0:T(8,128)(2,1)} %copy-done.6, s32[8,128]{1,0:T(8,128)} %bitcast.42, s32[8,128]{1,0:T(8,128)} %bitcast.43, s32[1,128]{1,0:T(1,128)} %bitcast.45, bf16[2,316,512]{2,1,0:T(8,128)(2,1)} %bitcast.28), custom_call_target="tpu_custom_call" | custom-call | flops 1199570944 | bytes 1048576 | tf_op jit(solution)/shard_map/near_sums/pallas_call | solution.py:51
  39.0 3.6 %all-to-all-done.1 = bf16[16,32,256]{2,1,0:T(8,128)(2,1)S(1)} async-done(((bf16[16,32,256]{2,1,0:T(8,128)(2,1)}), bf16[16,32,256]{2,1,0:T(8,128)(2,1)S(1)}, u32[]{:S(2)}, u32[]{:S(2)}) %all-to-all-start.1) | async-done | bytes 262176 | tf_op jit(solution)/shard_map/all_to_all | solution.py:574
  42.6 2.3 %lower.1 = (bf16[256,2048]{1,0:T(8,128)(2,1)S(1)}, bf16[2,2,64,128]{3,2,1,0:T(8,128)(2,1)S(1)}) custom-call(bf16[512,256]{1,0:T(8,128)(2,1)S(1)} %bitcast.25, s32[1,128]{1,0:T(1,128)} %bitcast.39, s32[1,128]{1,0:T(1,128)} %bitcast.37, bf16[32,4096]{1,0:T(8,128)(2,1)} %get-tuple-element.31.refs_3_, bf16[640,2048]{1,0:T(8,128)(2,1)S(1)} %copy-done), custom_call_target="tpu_custom_call" | custom-call | flops 134217728 | bytes 1048576 | tf_op jit(solution)/shard_map/lower/pallas_call | solution.py:51
  44.9 0.1 collective-permute-start.3
  45.0 1.7 %anterpolate.1.refs_0_ = f32[2,512,128]{2,1,0:T(8,128)S(1)} custom-call(bf16[640,2048]{1,0:T(8,128)(2,1)S(1)} %copy-done, bf16[256,2048]{1,0:T(8,128)(2,1)S(1)} %get-tuple-element.32.refs_1_, f32[2,512,128]{2,1,0:T(8,128)} %near_sums.1.refs_2_), custom_call_target="tpu_custom_call" | custom-call | flops 536870912 | bytes 1048576 | tf_op jit(solution)/shard_map/anterpolate/pallas_call | solution.py:51
  46.7 0.0 collective-permute-done.3.refs_1_
  46.7 0.7 %finish.1 = bf16[2,512,128]{2,1,0:T(8,128)(2,1)} custom-call(f32[2,512,128]{2,1,0:T(8,128)S(1)} %anterpolate.1.refs_0_, bf16[2,2,64,128]{3,2,1,0:T(8,128)(2,1)S(1)} %collective-permute-done.3.refs_1_), custom_call_target="tpu_custom_call" | custom-call | flops 1048576 | bytes 1048576 | tf_op jit(solution)/shard_map/finish/pallas_call | solution.py:51
  (5 shorter events, 0.0 us)
Async XLA Ops:
  0.0 4.1 %collective-permute-start = (bf16[2,512,128]{2,1,0:T(8,128)(2,1)}, bf16[2,512,128]{2,1,0:T(8,128)(2,1)S(1)}, u32[]{:S(2)}, u32[]{:S(2)}) collective-permute-start(bf16[2,512,128]{2,1,0:T(8,128)(2,1)} %bitcast.31), channel_id=1, source_target_pairs={{0,1},{1,0},{2,3},{3,2},{4,5},{5,4},{6,7},{7,6},{8,9},{9,8},{10,11... | collective-permute-start | bytes 786440 | tf_op jit(solution)/shard_map/ppermute | solution.py:520
  4.1 9.9 %copy-start.5 = (bf16[2,32,512]{2,1,0:T(8,128)(2,1)S(1)}, bf16[2,32,512]{2,1,0:T(8,128)(2,1)}, u32[]{:S(2)}) copy-start(bf16[2,32,512]{2,1,0:T(8,128)(2,1)} %get-tuple-element.25) | copy-start | bytes 196612
  4.2 11.9 %copy-start.3 = (bf16[2,32,512]{2,1,0:T(8,128)(2,1)S(1)}, bf16[2,32,512]{2,1,0:T(8,128)(2,1)}, u32[]{:S(2)}) copy-start(bf16[2,32,512]{2,1,0:T(8,128)(2,1)} %get-tuple-element.26) | copy-start | bytes 196612
  4.2 12.6 %copy-start.2 = (bf16[2,316,1,128]{3,0,2,1:T(2,128)(2,1)S(1)}, bf16[2,316,1,128]{3,0,2,1:T(2,128)(2,1)}, u32[]{:S(2)}) copy-start(bf16[2,316,1,128]{3,0,2,1:T(2,128)(2,1)} %param.25) | copy-start | bytes 485380
  6.2 18.4 %all-to-all-start = ((bf16[16,32,256]{2,1,0:T(8,128)(2,1)}), bf16[16,32,256]{2,1,0:T(8,128)(2,1)S(1)}, u32[]{:S(2)}, u32[]{:S(2)}) async-start(bf16[16,32,256]{2,1,0:T(8,128)(2,1)} %bitcast.27), calls=%async_computation | async-start | bytes 524288 | tf_op jit(solution)/shard_map/all_to_all | solution.py:569
  14.1 6.9 %collective-permute-start.1 = (bf16[2,32,512]{2,1,0:T(8,128)(2,1)S(1)}, bf16[2,32,512]{2,1,0:T(8,128)(2,1)S(1)}, u32[]{:S(2)}, u32[]{:S(2)}) collective-permute-start(bf16[2,32,512]{2,1,0:T(8,128)(2,1)S(1)} %copy-done.5), channel_id=1, source_target_pairs={{0,2},{4,6},{8,10},{12,14},{16,18},{20,22},{24,26},{28,30},{2,0},{... | collective-permute-start | bytes 196616 | tf_op jit(solution)/shard_map/ppermute | solution.py:526
  16.1 5.0 %collective-permute-start.2 = (bf16[2,32,512]{2,1,0:T(8,128)(2,1)S(1)}, bf16[2,32,512]{2,1,0:T(8,128)(2,1)S(1)}, u32[]{:S(2)}, u32[]{:S(2)}) collective-permute-start(bf16[2,32,512]{2,1,0:T(8,128)(2,1)S(1)} %copy-done.3), channel_id=1, source_target_pairs={{2,4},{6,8},{10,12},{14,16},{18,20},{22,24},{26,28},{4,2},{8,6},{1... | collective-permute-start | bytes 196616 | tf_op jit(solution)/shard_map/ppermute | solution.py:526
  21.0 12.2 %copy-start.1 = (bf16[2,316,1,512]{3,0,2,1:T(2,128)(2,1)S(1)}, bf16[2,316,1,512]{3,0,2,1:T(2,128)(2,1)}, u32[]{:S(2)}) copy-start(bf16[2,316,1,512]{3,0,2,1:T(2,128)(2,1)} %param.24) | copy-start | bytes 1941508
  21.0 7.3 %copy-start.4 = (bf16[2,32,512]{2,1,0:T(8,128)(2,1)}, bf16[2,32,512]{2,1,0:T(8,128)(2,1)S(1)}, u32[]{:S(2)}) copy-start(bf16[2,32,512]{2,1,0:T(8,128)(2,1)S(1)} %collective-permute-done.1.refs_1_) | copy-start | bytes 196612
  21.0 7.3 %copy-start.6 = (bf16[2,32,512]{2,1,0:T(8,128)(2,1)}, bf16[2,32,512]{2,1,0:T(8,128)(2,1)S(1)}, u32[]{:S(2)}) copy-start(bf16[2,32,512]{2,1,0:T(8,128)(2,1)S(1)} %collective-permute-done.2.refs_2_) | copy-start | bytes 196612
  28.4 14.2 %all-to-all-start.1 = ((bf16[16,32,256]{2,1,0:T(8,128)(2,1)}), bf16[16,32,256]{2,1,0:T(8,128)(2,1)S(1)}, u32[]{:S(2)}, u32[]{:S(2)}) async-start(bf16[16,32,256]{2,1,0:T(8,128)(2,1)} %bitcast.30), calls=%async_computation.1 | async-start | bytes 524288 | tf_op jit(solution)/shard_map/all_to_all | solution.py:574
  33.2 9.4 %copy-start = (bf16[640,2048]{1,0:T(8,128)(2,1)S(1)}, bf16[640,2048]{1,0:T(8,128)(2,1)}, u32[]{:S(2)}) copy-start(bf16[640,2048]{1,0:T(8,128)(2,1)} %refs_0_.1) | copy-start | bytes 7864324
  44.9 1.8 %collective-permute-start.3 = (bf16[2,2,64,128]{3,2,1,0:T(8,128)(2,1)S(1)}, bf16[2,2,64,128]{3,2,1,0:T(8,128)(2,1)S(1)}, u32[]{:S(2)}, u32[]{:S(2)}) collective-permute-start(bf16[2,2,64,128]{3,2,1,0:T(8,128)(2,1)S(1)} %get-tuple-element.34), channel_id=1, source_target_pairs={{0,1},{1,0},{2,3},{3,2},{4,5},{5,4},{6,7},{7,6},{8,9},{9,8},{10,11... | collective-permute-start | bytes 196616 | tf_op jit(solution)/shard_map/ppermute | solution.py:520

commit v3 on v2

--- a/solution.py
+++ b/solution.py
@@ -113,9 +113,8 @@
     return [high, middle, (rest - middle.astype(f32)).astype(bf16)]
 
 
-def phase_rows(cosine, sine):
-    halves = [jnp.concatenate(parts(x) + [jnp.zeros(x.shape, bf16)], axis=0) for x in (cosine, sine)]
-    return jnp.concatenate(halves, axis=1)
+def phase_rows(x):
+    return jnp.concatenate(parts(x) + [jnp.zeros(x.shape, bf16)], axis=0)
 
 
 def octant_rows(octant, boxes):
@@ -147,7 +146,8 @@
         family_ref[...] = jnp.concatenate([family, family], axis=1)
         onehot = octant_rows(oct_in()[...], boxes)
         sine, cosine = sincos(ph_in()[:, 0, :])
-        phase_ref[...] = phase_rows(cosine, sine)
+        phase_ref[:OCTANTS] = cosine
+        phase_ref[OCTANTS:] = sine
         room = own_in()
         for r in range(2):
             e_ref[r * boxes : (r + 1) * boxes] = nt(eye, room[r]).astype(bf16)
@@ -163,8 +163,8 @@
                 )
         for copy in copies:
             copy.start()
-        cos_ref[...] = tn(onehot, phase_ref[:, :kpg])
-        sin_ref[...] = tn(onehot, phase_ref[:, kpg:])
+        cos_ref[...] = tn(onehot, phase_rows(cosine))
+        sin_ref[...] = tn(onehot, phase_rows(sine))
         for n, piece in enumerate(pieces):
             piece.wait()
             for step in range(kpg // 2 // width):
@@ -176,7 +176,7 @@
 
     wave = ((boxes, kpg), f32, V)
     edge = ((2, NEARB, kcg), bf16, H)
-    phases = (4 * OCTANTS, 2 * kpg)
+    phases = (2 * OCTANTS, kpg)
     return call(
         body,
         [own, octant, parent, phase, weights],
@@ -187,13 +187,13 @@
             ((2 * boxes, kpg), f32, V),
             (weights.shape, bf16, V),
             ((parents, 2 * boxes), bf16, V),
-            (phases, bf16, H),
+            (phases, f32, H),
             edge,
             edge,
         ],
         "prepare",
         rooms={4: None},
-        scratch=[pltpu.VMEM((2 * boxes, kcg), bf16), pltpu.VMEM(phases, bf16), pltpu.SemaphoreType.DMA((7,))],
+        scratch=[pltpu.VMEM((2 * boxes, kcg), bf16), pltpu.VMEM(phases, f32), pltpu.SemaphoreType.DMA((7,))],
         flops=2 * 2 * boxes * kcg * kpg,
     )
 
@@ -261,34 +261,29 @@
 
 def operators_of_lists(offsets, counts, table):
     slots, boxes = offsets.shape
-    operators, lanes = table.shape
+    operators, _, half = table.shape
+    lanes = 2 * half
 
     def body(ins, outs, rest):
         off_in, cnt_in, tab_in = ins
-        (coef_out,) = outs
-        coef_ref, sems = rest
+        (coef_ref,) = outs
         off = jnp.where(iota((slots, boxes), 0) < cnt_in()[...], off_in()[...], -1).T
         size = slots * CHUNK
-        copies = []
+        tables = jnp.swapaxes(tab_in()[...], 0, 1)
+        flat = jnp.concatenate([tables[0], tables[1]], axis=1)
         for chunk in range(boxes // CHUNK):
             rows = slice(chunk * CHUNK, (chunk + 1) * CHUNK)
             pick = jnp.concatenate(
                 [ones_where(off[rows, m : m + 1] == iota((CHUNK, operators), 1)) for m in range(slots)], axis=0
             )
-            coef_ref[chunk * size : (chunk + 1) * size] = nn(pick, tab_in()[...]).astype(bf16)
-            part = pl.ds(chunk * size, size)
-            copies.append(pltpu.make_async_copy(coef_ref.at[part], coef_out.at[part], sems.at[chunk]))
-            copies[-1].start()
-        for copy in copies:
-            copy.wait()
+            coef_ref[chunk * size : (chunk + 1) * size] = nn(pick, flat).astype(bf16)
 
     return call(
         body,
         [offsets, counts, table],
         [H, H, H],
-        [((slots * boxes, lanes), bf16, H)],
+        [((slots * boxes, lanes), bf16, V)],
         "operators_of_lists",
-        scratch=[pltpu.VMEM((slots * boxes, lanes), bf16), pltpu.SemaphoreType.DMA((boxes // CHUNK,))],
         flops=2 * slots * boxes * operators * lanes,
     )[0]
 
@@ -302,17 +297,16 @@
     halves = 2
 
     def body(ins, outs, rest):
-        pat_ref, src_in, coef_in = ins
+        pat_ref, src_ref, coef_ref = ins
         (out_hbm,) = outs
         pick_ref, out_ref, sems = rest
-        src = src_in()[...].T
+        src = src_ref[...].T
         for chunk in range(chunks):
             rows = slice(chunk * CHUNK, (chunk + 1) * CHUNK)
             hot = jnp.concatenate(
                 [ones_where(src[rows, m : m + 1] == iota((CHUNK, total), 1)) for m in range(slots)], axis=0
             )
             pick_ref[chunk * size : (chunk + 1) * size] = nn(hot, pat_ref[...])
-        coef_ref = coef_in()
         copies = []
         for chunk in range(chunks):
             real = imag = 0.0
@@ -338,7 +332,7 @@
     return call(
         body,
         [pattern, sources, coef],
-        [V, H, H],
+        [V, V, V],
         [((total, lanes), bf16, H)],
         "parent_sums",
         scratch=[
@@ -357,12 +351,11 @@
     width = LANES if packed else 256
 
     def body(ins, outs, rest):
-        far_ref, par_in, oct_in, phase_in, w_ref = ins
+        far_ref, par_ref, oct_ref, phase_ref, w_ref = ins
         low_ref, rim_ref = outs
         base = lax.axis_index("box") * parents
-        hot = ones_where(iota((parents, boxes), 0) == par_in()[...] - base).T
-        onehot = octant_rows(oct_in()[...], boxes).T
-        phase_ref = phase_in()
+        hot = ones_where(iota((parents, boxes), 0) == par_ref[...] - base).T
+        onehot = octant_rows(oct_ref[...], boxes).T
         for step in range(kpg // width):
             cols = slice(step * width, (step + 1) * width)
             if packed:
@@ -370,8 +363,12 @@
                 sr, si = spread[:, :LANES], spread[:, LANES:]
             else:
                 sr, si = nn(hot, far_ref[0, :, cols]), nn(hot, far_ref[1, :, cols])
-            sine_cols = slice(kpg + step * width, kpg + (step + 1) * width)
-            both = nn(onehot, jnp.concatenate([phase_ref[:, cols], phase_ref[:, sine_cols]], axis=1))
+            both = nn(
+                onehot,
+                jnp.concatenate(
+                    [phase_rows(phase_ref[:OCTANTS, cols]), phase_rows(phase_ref[OCTANTS:, cols])], axis=1
+                ),
+            )
             c, s = both[:, :width], both[:, width:]
             low_ref[:boxes, cols] = (sr * c + si * s).astype(bf16)
             low_ref[boxes:, cols] = (si * c - sr * s).astype(bf16)
@@ -384,7 +381,7 @@
     return call(
         body,
         [far, parent, octant, phases, weights],
-        [V, H, H, H, V],
+        [V, V, V, V, V],
         [((2 * boxes, kpg), bf16, V), ((2, 2, rim, boxes), bf16, V)],
         "lower",
         flops=2 * 2 * boxes * kpg * 2 * rim,
@@ -395,16 +392,16 @@
     _, kcg, boxes = nearby.shape
 
     def body(ins, outs, rest):
-        w_ref, low_ref, near_in = ins
+        w_ref, low_ref, near_ref = ins
         (out_ref,) = outs
         terms = nt(w_ref[rim : rim + kcg], low_ref[...]).astype(bf16).astype(f32)
         for r in range(2):
-            out_ref[r] = near_in()[r] + terms[:, r * boxes : (r + 1) * boxes]
+            out_ref[r] = near_ref[r] + terms[:, r * boxes : (r + 1) * boxes]
 
     return call(
         body,
         [weights, lowered, nearby],
-        [V, V, H],
+        [V, V, V],
         [(nearby.shape, f32, V)],
         "anterpolate",
         flops=2 * kcg * weights.shape[1] * 2 * boxes,
@@ -433,23 +430,24 @@
 def near_sums(own, lead, trail, sources, offsets, counts, table):
     _, kcg, boxes = own.shape
     slots = sources.shape[0]
-    operators = table.shape[1]
+    operators = table.shape[0]
     depth = 2 * boxes
     pair = 2
 
     def body(ins, outs, rest):
         own_in, lead_in, trail_in, src_in, off_in, cnt_in, tab_in = ins
-        (near_out,) = outs
-        out_ref, ext_ref, tt_ref, sem = rest
+        (out_ref,) = outs
+        ext_ref, tt_ref = rest
         eye = identity(boxes)
-        own_ref, tab_ref = own_in(), tab_in()
+        own_ref = own_in()
+        tables = jnp.swapaxes(tab_in()[...], 0, 1)
         for r in range(2):
             rows = slice(r * kcg, (r + 1) * kcg)
             ext_ref[rows, :boxes] = own_ref[r]
             for step in range(kcg // boxes):
                 cols = slice(step * boxes, (step + 1) * boxes)
                 part = slice(r * kcg + step * boxes, r * kcg + (step + 1) * boxes)
-                tt_ref[part] = nt(eye, tab_ref[r, :, cols]).astype(bf16)
+                tt_ref[part] = nt(eye, tables[r, :, cols]).astype(bf16)
         lead_ref, trail_ref = lead_in(), trail_in()
         for r in range(2):
             for step in range(kcg // boxes):
@@ -479,22 +477,14 @@
             for r, value in enumerate((real, imag)):
                 value = sum(value[:, j * boxes : (j + 1) * boxes] for j in range(pair))
                 out_ref[r] = value if m == 0 else out_ref[r] + value
-        copy = pltpu.make_async_copy(out_ref, near_out, sem)
-        copy.start()
-        copy.wait()
 
     return call(
         body,
         [own, lead, trail, sources, offsets, counts, table],
         [H] * 7,
-        [(own.shape, f32, H)],
+        [(own.shape, f32, V)],
         "near_sums",
-        scratch=[
-            pltpu.VMEM(own.shape, f32),
-            pltpu.VMEM((2 * kcg, depth), bf16),
-            pltpu.VMEM((2 * kcg, operators), bf16),
-            pltpu.SemaphoreType.DMA,
-        ],
+        scratch=[pltpu.VMEM((2 * kcg, depth), bf16), pltpu.VMEM((2 * kcg, operators), bf16)],
         flops=2 * slots * boxes * 2 * kcg * (depth + operators),
         limit=24 << 20,
     )[0]
@@ -567,10 +557,9 @@
     table = parent_table[:, :, 0, :]
     if packed:
         regrouped = lax.all_to_all(pattern, "box", split_axis=0, concat_axis=0, tiled=True)
-        regrouped, lead, trail = lax.optimization_barrier((regrouped, lead, trail))
-        flat_table = jnp.transpose(table, (1, 0, 2)).reshape(table.shape[1], 2 * mine)
-        coef = operators_of_lists(parent_offsets.T, parent_counts[None, :], flat_table)
+        coef = operators_of_lists(parent_offsets.T, parent_counts[None, :], jnp.swapaxes(table, 0, 1))
         far = parent_sums(regrouped, parent_sources.T, coef)
+        far, lead, trail = lax.optimization_barrier((far, lead, trail))
         returned = lax.all_to_all(far, "box", split_axis=0, concat_axis=0, tiled=True)
     else:
         regrouped = lax.all_to_all(pattern, "box", split_axis=2, concat_axis=1, tiled=True)
@@ -587,7 +576,7 @@
         child_sources.T,
         child_offsets.T,
         child_counts[None, :],
-        child_table[:, :, 0, :],
+        jnp.swapaxes(child_table[:, :, 0, :], 0, 1),
     )
     returned, nearby = lax.optimization_barrier((returned, nearby))
     lowered, terms = lower(returned, parent, octant, phases, interp_weights, parents, rim, packed)

time: 48 us -> 44.9 us (0.935)
  Pallas kernels: 22.4 us -> 17.6 us
  waiting for transfers between devices: 7.2 us -> 11.2 us
  local copies, waits for them, and re-layouts: 1.77 us -> 0.66 us
  starting transfers between devices: 15.8 us -> 14.7 us
    pallas_call x8, Pallas kernels: 22.4 us -> 17.6 us  [call(): pl.pallas_call(kernel, out_shape=[jax.ShapeDtypeStruct(shape, dtype) if p...]
    all_to_all x1, waiting for transfers between devices: 3.56 us -> 5.52 us  [local(): lax.all_to_all(pattern, 'box', split_axis=0, concat_axis=0, tiled=True)]
    all_to_all x1, waiting for transfers between devices: 3.62 us -> 5.18 us  [local(): lax.all_to_all(far, 'box', split_axis=0, concat_axis=0, tiled=True)]
    all_to_all x1, starting transfers between devices: 4.79 us -> 3.68 us  [local(): lax.all_to_all(far, 'box', split_axis=0, concat_axis=0, tiled=True)]
    unnamed x17 -> x18, local copies, waits for them, and re-layouts: 1.77 us -> 0.66 us
    ppermute x2, waiting for transfers between devices: 0.01 us -> 0.49 us  [shift(): lax.ppermute(value, axis, [(i, (i + step) % peers) for i in range(peers)])]
  transfers between devices with their start and end apart: 6 -> 6, of which waited for: 2 -> 3; matrix products, arithmetic and copies ran while one was open for 4% -> 0% of each run, Pallas kernels for 29% -> 30%
where the time goes in v3:
time: 44.9 us; the launch traced here: 44.4 us
  Pallas kernels  17.6 us (39%)
  starting transfers between devices  14.7 us (33%)
  waiting for transfers between devices  11.2 us (25%)
  local copies, waits for them, and re-layouts  0.66 us (1%)
    pallas_call x8, Pallas kernels, call(): pl.pallas_call(kernel, out_shape=[jax.ShapeDtypeStruct(shape, dtype) if p...  17.6 us
    all_to_all x1, starting transfers between devices, local(): lax.all_to_all(pattern, 'box', split_axis=0, concat_axis=0, tiled=True)  7.87 us
    all_to_all x1, waiting for transfers between devices, local(): lax.all_to_all(pattern, 'box', split_axis=0, concat_axis=0, tiled=True)  5.52 us
    all_to_all x1, waiting for transfers between devices, local(): lax.all_to_all(far, 'box', split_axis=0, concat_axis=0, tiled=True)  5.18 us
    all_to_all x1, starting transfers between devices, local(): lax.all_to_all(far, 'box', split_axis=0, concat_axis=0, tiled=True)  3.68 us
    ppermute x2, starting transfers between devices, exchange(): return lax.ppermute(value, axis, pairs + [(j, i) for i, j in pairs])  2.64 us
  transfers between devices with their start and end apart: 6, of which 3 were waited for; matrix products, arithmetic and copies ran while one was open for 0% of the time, Pallas kernels for 30%

profile of v3, /device:TPU:0, one launch (start us, length us, event | category | flops | bytes accessed | tf_op | source)
XLA Modules:
  0.0 44.4 jit_solution(5051227731458514988)
XLA Ops:
  0.0 0.5 %collective-permute-start = (bf16[2,512,128]{2,1,0:T(8,128)(2,1)}, bf16[2,512,128]{2,1,0:T(8,128)(2,1)S(1)}, u32[]{:S(2)}, u32[]{:S(2)}) collective-permute-start(bf16[2,512,128]{2,1,0:T(8,128)(2,1)} %bitcast.31), channel_id=1, source_target_pairs={{0,1},{1,0},{2,3},{3,2},{4,5},{5,4},{6,7},{7,6},{8,9},{9,8},{10,11... | collective-permute-start | bytes 786440 | tf_op jit(solution)/shard_map/ppermute | solution.py:510
  0.5 3.5 %prepare.1 = (f32[128,2048]{1,0:T(8,128)S(1)}, f32[128,2048]{1,0:T(8,128)S(1)}, f32[256,2048]{1,0:T(8,128)S(1)}, bf16[640,2048]{1,0:T(8,128)(2,1)S(1)}, bf16[32,...) custom-call(bf16[2,512,128]{2,1,0:T(8,128)(2,1)} %bitcast.32, ...), custom_call_target="tpu_custom_call" | custom-call | flops 536870912 | bytes 1048576 | tf_op jit(solution)/shard_map/prepare/pallas_call | solution.py:51
  4.0 0.0 collective-permute-done.refs_0_
  4.0 0.0 copy-start.6
  4.0 0.0 copy-start.5
  4.0 2.0 %rise.1 = bf16[512,256]{1,0:T(8,128)(2,1)} custom-call(bf16[2,512,128]{2,1,0:T(8,128)(2,1)S(1)} %collective-permute-done.refs_0_, bf16[32,256]{1,0:T(8,128)(2,1)S(1)} %get-tuple-element.20.refs_1_, f32[128,2048]{1,0:T(8,128)S(1)} %get-tuple-element.21.refs_2_, f32[128,2048]{1,0:T(8,128)S(1)} %get-tuple-element.22.refs_3_, ...), custom_call_target="tpu_custom_call" | custom-call | flops 134217728 | bytes 1048576 | tf_op jit(solution)/shard_map/rise/pallas_call | solution.py:51
  6.0 0.0 copy-start.4
  6.0 7.9 %all-to-all-start = ((bf16[16,32,256]{2,1,0:T(8,128)(2,1)}), bf16[16,32,256]{2,1,0:T(8,128)(2,1)S(1)}, u32[]{:S(2)}, u32[]{:S(2)}) async-start(bf16[16,32,256]{2,1,0:T(8,128)(2,1)} %bitcast.29), calls=%async_computation | async-start | bytes 524288 | tf_op jit(solution)/shard_map/all_to_all | solution.py:559
  13.9 0.0 copy-done.6
  13.9 2.0 %collective-permute-start.1 = (bf16[2,32,512]{2,1,0:T(8,128)(2,1)S(1)}, bf16[2,32,512]{2,1,0:T(8,128)(2,1)S(1)}, u32[]{:S(2)}, u32[]{:S(2)}) collective-permute-start(bf16[2,32,512]{2,1,0:T(8,128)(2,1)S(1)} %copy-done.6), channel_id=1, source_target_pairs={{0,2},{4,6},{8,10},{12,14},{16,18},{20,22},{24,26},{28,30},{2,0},{... | collective-permute-start | bytes 196616 | tf_op jit(solution)/shard_map/ppermute | solution.py:516
  15.9 0.0 copy-done.5
  15.9 0.7 %collective-permute-start.2 = (bf16[2,32,512]{2,1,0:T(8,128)(2,1)S(1)}, bf16[2,32,512]{2,1,0:T(8,128)(2,1)S(1)}, u32[]{:S(2)}, u32[]{:S(2)}) collective-permute-start(bf16[2,32,512]{2,1,0:T(8,128)(2,1)S(1)} %copy-done.5), channel_id=1, source_target_pairs={{2,4},{6,8},{10,12},{14,16},{18,20},{22,24},{26,28},{4,2},{8,6},{1... | collective-permute-start | bytes 196616 | tf_op jit(solution)/shard_map/ppermute | solution.py:516
  16.6 2.3 %operators_of_lists.1.refs_2_ = bf16[4096,256]{1,0:T(8,128)(2,1)S(1)} custom-call(s32[8,512]{1,0:T(8,128)} %bitcast.36, s32[1,512]{1,0:T(1,128)} %bitcast.39, bf16[316,2,128]{2,1,0:T(2,128)(2,1)} %bitcast.35), custom_call_target="tpu_custom_call" | custom-call | flops 662700032 | bytes 1048576 | tf_op jit(solution)/shard_map/operators_of_lists/pallas_call | solution.py:51
  18.9 5.5 %all-to-all-done = bf16[16,32,256]{2,1,0:T(8,128)(2,1)S(1)} async-done(((bf16[16,32,256]{2,1,0:T(8,128)(2,1)}), bf16[16,32,256]{2,1,0:T(8,128)(2,1)S(1)}, u32[]{:S(2)}, u32[]{:S(2)}) %all-to-all-start) | async-done | bytes 262176 | tf_op jit(solution)/shard_map/all_to_all | solution.py:559
  24.5 0.0 copy-done.4
  24.5 2.6 %parent_sums.1 = bf16[512,256]{1,0:T(8,128)(2,1)} custom-call(bf16[512,256]{1,0:T(8,128)(2,1)S(1)} %bitcast.23, s32[8,512]{1,0:T(8,128)S(1)} %bitcast.28, bf16[4096,256]{1,0:T(8,128)(2,1)S(1)} %operators_of_lists.1.refs_2_), custom_call_target="tpu_custom_call" | custom-call | flops 1073741824 | bytes 1048576 | tf_op jit(solution)/shard_map/parent_sums/pallas_call | solution.py:51
  27.1 0.0 copy-start
  27.1 0.0 copy-start.2
  27.1 0.0 copy-start.3
  27.1 0.0 collective-permute-done.1.refs_1_
  27.2 0.0 collective-permute-done.2.refs_2_
  27.2 0.6 %copy-done.7 = bf16[2,32,512]{2,1,0:T(8,128)(2,1)} copy-done((bf16[2,32,512]{2,1,0:T(8,128)(2,1)}, bf16[2,32,512]{2,1,0:T(8,128)(2,1)S(1)}, u32[]{:S(2)}) %copy-start.7) | copy-done | bytes 65560
  27.8 0.0 copy-done.8
  27.8 3.7 %all-to-all-start.1 = ((bf16[16,32,256]{2,1,0:T(8,128)(2,1)}), bf16[16,32,256]{2,1,0:T(8,128)(2,1)S(1)}, u32[]{:S(2)}, u32[]{:S(2)}) async-start(bf16[16,32,256]{2,1,0:T(8,128)(2,1)} %bitcast.30), calls=%async_computation.1 | async-start | bytes 524288 | tf_op jit(solution)/shard_map/all_to_all | solution.py:563
  31.5 4.3 %near_sums.1.refs_2_ = f32[2,512,128]{2,1,0:T(8,128)S(1)} custom-call(bf16[2,512,128]{2,1,0:T(8,128)(2,1)} %bitcast.33, bf16[2,32,512]{2,1,0:T(8,128)(2,1)} %copy-done.7, bf16[2,32,512]{2,1,0:T(8,128)(2,1)} %copy-done.8, s32[8,128]{1,0:T(8,128)} %bitcast.37, s32[8,128]{1,0:T(8,128)} %bitcast.38, s32[1,128]{1,0:T(1,128)} %bitcast.40, ...), custom_call_target="tpu_custom_call" | custom-call | flops 1199570944 | bytes 1048576 | tf_op jit(solution)/shard_map/near_sums/pallas_call | solution.py:51
  35.8 5.2 %all-to-all-done.1 = bf16[16,32,256]{2,1,0:T(8,128)(2,1)S(1)} async-done(((bf16[16,32,256]{2,1,0:T(8,128)(2,1)}), bf16[16,32,256]{2,1,0:T(8,128)(2,1)S(1)}, u32[]{:S(2)}, u32[]{:S(2)}) %all-to-all-start.1) | async-done | bytes 262176 | tf_op jit(solution)/shard_map/all_to_all | solution.py:563
  41.0 0.0 copy-done.1
  41.0 1.3 %lower.1 = (bf16[256,2048]{1,0:T(8,128)(2,1)S(1)}, bf16[2,2,64,128]{3,2,1,0:T(8,128)(2,1)S(1)}) custom-call(bf16[512,256]{1,0:T(8,128)(2,1)S(1)} %bitcast.22, s32[1,128]{1,0:T(1,128)S(1)} %bitcast.27, s32[1,128]{1,0:T(1,128)S(1)} %bitcast.25, f32[16,2048]{1,0:T(8,128)S(1)} %copy-done.1, bf16[640,2048]{1,0:T(8,128)(2,1)S(1)} %copy-done), custom_call_target="tpu_custom_call" | custom-call | flops 134217728 | bytes 1048576 | tf_op jit(solution)/shard_map/lower/pallas_call | solution.py:51
  42.3 0.1 collective-permute-start.3
  42.4 0.7 %anterpolate.1.refs_0_ = f32[2,512,128]{2,1,0:T(8,128)S(1)} custom-call(bf16[640,2048]{1,0:T(8,128)(2,1)S(1)} %copy-done, bf16[256,2048]{1,0:T(8,128)(2,1)S(1)} %get-tuple-element.32.refs_1_, f32[2,512,128]{2,1,0:T(8,128)S(1)} %near_sums.1.refs_2_), custom_call_target="tpu_custom_call" | custom-call | flops 536870912 | bytes 1048576 | tf_op jit(solution)/shard_map/anterpolate/pallas_call | solution.py:51
  43.2 0.5 %collective-permute-done.3.refs_1_ = bf16[2,2,64,128]{3,2,1,0:T(8,128)(2,1)S(1)} collective-permute-done((bf16[2,2,64,128]{3,2,1,0:T(8,128)(2,1)S(1)}, bf16[2,2,64,128]{3,2,1,0:T(8,128)(2,1)S(1)}, u32[]{:S(2)}, u32[]{:S(2)}) %collective-permute-start.3) | collective-permute-done | bytes 65568 | tf_op jit(solution)/shard_map/ppermute | solution.py:510
  43.7 0.7 %finish.1 = bf16[2,512,128]{2,1,0:T(8,128)(2,1)} custom-call(f32[2,512,128]{2,1,0:T(8,128)S(1)} %anterpolate.1.refs_0_, bf16[2,2,64,128]{3,2,1,0:T(8,128)(2,1)S(1)} %collective-permute-done.3.refs_1_), custom_call_target="tpu_custom_call" | custom-call | flops 1048576 | bytes 1048576 | tf_op jit(solution)/shard_map/finish/pallas_call | solution.py:51
  (6 shorter events, 0.0 us)
Async XLA Ops:
  0.0 4.0 %collective-permute-start = (bf16[2,512,128]{2,1,0:T(8,128)(2,1)}, bf16[2,512,128]{2,1,0:T(8,128)(2,1)S(1)}, u32[]{:S(2)}, u32[]{:S(2)}) collective-permute-start(bf16[2,512,128]{2,1,0:T(8,128)(2,1)} %bitcast.31), channel_id=1, source_target_pairs={{0,1},{1,0},{2,3},{3,2},{4,5},{5,4},{6,7},{7,6},{8,9},{9,8},{10,11... | collective-permute-start | bytes 786440 | tf_op jit(solution)/shard_map/ppermute | solution.py:510
  4.0 9.9 %copy-start.6 = (bf16[2,32,512]{2,1,0:T(8,128)(2,1)S(1)}, bf16[2,32,512]{2,1,0:T(8,128)(2,1)}, u32[]{:S(2)}) copy-start(bf16[2,32,512]{2,1,0:T(8,128)(2,1)} %get-tuple-element.25) | copy-start | bytes 196612
  4.0 11.9 %copy-start.5 = (bf16[2,32,512]{2,1,0:T(8,128)(2,1)S(1)}, bf16[2,32,512]{2,1,0:T(8,128)(2,1)}, u32[]{:S(2)}) copy-start(bf16[2,32,512]{2,1,0:T(8,128)(2,1)} %get-tuple-element.26) | copy-start | bytes 196612
  6.0 18.4 %copy-start.4 = (s32[512,8]{0,1:T(8,128)S(1)}, s32[512,8]{0,1:T(8,128)}, u32[]{:S(2)}) copy-start(s32[512,8]{0,1:T(8,128)} %param.19) | copy-start | bytes 49156
  6.0 18.4 %all-to-all-start = ((bf16[16,32,256]{2,1,0:T(8,128)(2,1)}), bf16[16,32,256]{2,1,0:T(8,128)(2,1)S(1)}, u32[]{:S(2)}, u32[]{:S(2)}) async-start(bf16[16,32,256]{2,1,0:T(8,128)(2,1)} %bitcast.29), calls=%async_computation | async-start | bytes 524288 | tf_op jit(solution)/shard_map/all_to_all | solution.py:559
  13.9 13.2 %collective-permute-start.1 = (bf16[2,32,512]{2,1,0:T(8,128)(2,1)S(1)}, bf16[2,32,512]{2,1,0:T(8,128)(2,1)S(1)}, u32[]{:S(2)}, u32[]{:S(2)}) collective-permute-start(bf16[2,32,512]{2,1,0:T(8,128)(2,1)S(1)} %copy-done.6), channel_id=1, source_target_pairs={{0,2},{4,6},{8,10},{12,14},{16,18},{20,22},{24,26},{28,30},{2,0},{... | collective-permute-start | bytes 196616 | tf_op jit(solution)/shard_map/ppermute | solution.py:516
  15.9 11.2 %collective-permute-start.2 = (bf16[2,32,512]{2,1,0:T(8,128)(2,1)S(1)}, bf16[2,32,512]{2,1,0:T(8,128)(2,1)S(1)}, u32[]{:S(2)}, u32[]{:S(2)}) collective-permute-start(bf16[2,32,512]{2,1,0:T(8,128)(2,1)S(1)} %copy-done.5), channel_id=1, source_target_pairs={{2,4},{6,8},{10,12},{14,16},{18,20},{22,24},{26,28},{4,2},{8,6},{1... | collective-permute-start | bytes 196616 | tf_op jit(solution)/shard_map/ppermute | solution.py:516
  27.1 13.9 %copy-start = (bf16[640,2048]{1,0:T(8,128)(2,1)S(1)}, bf16[640,2048]{1,0:T(8,128)(2,1)}, u32[]{:S(2)}) copy-start(bf16[640,2048]{1,0:T(8,128)(2,1)} %refs_0_.1) | copy-start | bytes 7864324
  27.1 13.9 %copy-start.1 = (f32[16,2048]{1,0:T(8,128)S(1)}, f32[16,2048]{1,0:T(8,128)}, u32[]{:S(2)}) copy-start(f32[16,2048]{1,0:T(8,128)} %get-tuple-element.31.refs_3_) | copy-start | bytes 393220
  27.1 13.9 %copy-start.2 = (s32[128]{0:T(128)S(1)}, s32[128]{0:T(128)}, u32[]{:S(2)}) copy-start(s32[128]{0:T(128)} %param.15) | copy-start | bytes 1540
  27.1 13.9 %copy-start.3 = (s32[128]{0:T(128)S(1)}, s32[128]{0:T(128)}, u32[]{:S(2)}) copy-start(s32[128]{0:T(128)} %param.14) | copy-start | bytes 1540
  27.1 0.6 %copy-start.7 = (bf16[2,32,512]{2,1,0:T(8,128)(2,1)}, bf16[2,32,512]{2,1,0:T(8,128)(2,1)S(1)}, u32[]{:S(2)}) copy-start(bf16[2,32,512]{2,1,0:T(8,128)(2,1)S(1)} %collective-permute-done.1.refs_1_) | copy-start | bytes 196612
  27.2 0.6 %copy-start.8 = (bf16[2,32,512]{2,1,0:T(8,128)(2,1)}, bf16[2,32,512]{2,1,0:T(8,128)(2,1)S(1)}, u32[]{:S(2)}) copy-start(bf16[2,32,512]{2,1,0:T(8,128)(2,1)S(1)} %collective-permute-done.2.refs_2_) | copy-start | bytes 196612
  27.8 13.2 %all-to-all-start.1 = ((bf16[16,32,256]{2,1,0:T(8,128)(2,1)}), bf16[16,32,256]{2,1,0:T(8,128)(2,1)S(1)}, u32[]{:S(2)}, u32[]{:S(2)}) async-start(bf16[16,32,256]{2,1,0:T(8,128)(2,1)} %bitcast.30), calls=%async_computation.1 | async-start | bytes 524288 | tf_op jit(solution)/shard_map/all_to_all | solution.py:563
  42.3 1.3 %collective-permute-start.3 = (bf16[2,2,64,128]{3,2,1,0:T(8,128)(2,1)S(1)}, bf16[2,2,64,128]{3,2,1,0:T(8,128)(2,1)S(1)}, u32[]{:S(2)}, u32[]{:S(2)}) collective-permute-start(bf16[2,2,64,128]{3,2,1,0:T(8,128)(2,1)S(1)} %get-tuple-element.34), channel_id=1, source_target_pairs={{0,1},{1,0},{2,3},{3,2},{4,5},{5,4},{6,7},{7,6},{8,9},{9,8},{10,11... | collective-permute-start | bytes 196616 | tf_op jit(solution)/shard_map/ppermute | solution.py:510

commit v4 on v3

--- a/solution.py
+++ b/solution.py
@@ -124,59 +124,44 @@
 
 def prepare(own, octant, parent, phase, weights, parents):
     _, kcg, boxes = own.shape
-    rows, kpg = weights.shape
-    rim = (rows - kcg) // 2
-    width = 512
+    kpg = phase.shape[2]
 
     def body(ins, outs, rest):
         own_in, oct_in, par_in, ph_in, w_hbm = ins
-        cos_ref, sin_ref, y_ref, w_ref, family_ref, phase_out, lead_out, trail_out = outs
-        e_ref, phase_ref, sems = rest
-        pieces = [
-            pltpu.make_async_copy(
-                w_hbm.at[:, pl.ds(n * (kpg // 2), kpg // 2)], w_ref.at[:, pl.ds(n * (kpg // 2), kpg // 2)], sems.at[n]
-            )
-            for n in range(2)
-        ]
-        for piece in pieces:
-            piece.start()
+        cos_ref, sin_ref, e_ref, family_ref, w_ref, lead_out, trail_out = outs
+        phase_ref, sems = rest
+        fill = pltpu.make_async_copy(w_hbm, w_ref, sems.at[4])
+        fill.start()
         eye = identity(boxes)
         me = lax.axis_index("box")
         family = ones_where(iota((parents, boxes), 0) == par_in()[...] - me * parents)
         family_ref[...] = jnp.concatenate([family, family], axis=1)
         onehot = octant_rows(oct_in()[...], boxes)
-        sine, cosine = sincos(ph_in()[:, 0, :])
-        phase_ref[:OCTANTS] = cosine
-        phase_ref[OCTANTS:] = sine
+        phases = ph_in()
         room = own_in()
         for r in range(2):
             e_ref[r * boxes : (r + 1) * boxes] = nt(eye, room[r]).astype(bf16)
         odd = lax.rem(me, 2)
-        copies = [pltpu.make_async_copy(phase_ref, phase_out, sems.at[2])]
+        copies = []
         for n, out in enumerate((lead_out, trail_out)):
             begin = pl.multiple_of(jnp.where(odd == n, boxes - NEARB, 0), NEARB)
             for r in range(2):
                 copies.append(
                     pltpu.make_async_copy(
-                        e_ref.at[pl.ds(r * boxes + begin, NEARB)], out.at[r], sems.at[3 + 2 * n + r]
+                        e_ref.at[pl.ds(r * boxes + begin, NEARB)], out.at[r], sems.at[2 * n + r]
                     )
                 )
         for copy in copies:
             copy.start()
+        phase_ref[...] = phases[:, 0, :]
+        sine, cosine = sincos(phase_ref[...])
         cos_ref[...] = tn(onehot, phase_rows(cosine))
         sin_ref[...] = tn(onehot, phase_rows(sine))
-        for n, piece in enumerate(pieces):
-            piece.wait()
-            for step in range(kpg // 2 // width):
-                begin = n * (kpg // 2) + step * width
-                cols = slice(begin, begin + width)
-                y_ref[:, cols] = nn(e_ref[...], w_ref[rim : rim + kcg, cols])
-        for copy in copies:
+        for copy in copies + [fill]:
             copy.wait()
 
     wave = ((boxes, kpg), f32, V)
     edge = ((2, NEARB, kcg), bf16, H)
-    phases = (2 * OCTANTS, kpg)
     return call(
         body,
         [own, octant, parent, phase, weights],
@@ -184,17 +169,15 @@
         [
             wave,
             wave,
-            ((2 * boxes, kpg), f32, V),
+            ((2 * boxes, kcg), bf16, V),
+            ((parents, 2 * boxes), bf16, V),
             (weights.shape, bf16, V),
-            ((parents, 2 * boxes), bf16, V),
-            (phases, f32, H),
             edge,
             edge,
         ],
         "prepare",
         rooms={4: None},
-        scratch=[pltpu.VMEM((2 * boxes, kcg), bf16), pltpu.VMEM(phases, f32), pltpu.SemaphoreType.DMA((7,))],
-        flops=2 * 2 * boxes * kcg * kpg,
+        scratch=[pltpu.VMEM((OCTANTS, kpg), f32), pltpu.SemaphoreType.DMA((5,))],
     )
 
 
@@ -207,7 +190,7 @@
 
     def body(ins, outs, rest):
         sides = ins[: len(rims)]
-        family_ref, cos_ref, sin_ref, y_ref, w_ref = ins[len(rims) :]
+        family_ref, cos_ref, sin_ref, inner_ref, w_ref = ins[len(rims) :]
         (out_hbm,) = outs
         out_ref, e_ref, wr_ref, shift_ref, sems = rest
         eye = identity(boxes)
@@ -220,12 +203,13 @@
                 ).astype(bf16)
         for step in range(kpg // width):
             cols = slice(step * width, (step + 1) * width)
-            y = y_ref[:, cols] + nn(e_ref[...], wr_ref[:, cols])
+            y = nn(inner_ref[...], w_ref[rim : rows - rim, cols]) + nn(e_ref[...], wr_ref[:, cols])
             yr, yi, c, s = y[:boxes], y[boxes:], cos_ref[:, cols], sin_ref[:, cols]
             for r, value in enumerate((yr * c - yi * s, yr * s + yi * c)):
                 high = value.astype(bf16)
                 shift_ref[r, :boxes, cols] = high
                 shift_ref[r, boxes:, cols] = (value - high.astype(f32)).astype(bf16)
+        copies = []
         for step in range(kpg // width):
             cols = slice(step * width, (step + 1) * width)
             for r in range(2):
@@ -238,9 +222,17 @@
                         ]
                 else:
                     out_ref[r, :, cols] = total
-        copy = pltpu.make_async_copy(out_ref, out_hbm, sems)
-        copy.start()
-        copy.wait()
+            if (step + 1) * width * 2 % kpg == 0:
+                if packed:
+                    part = pl.ds(len(copies) * (shape[0] // 2), shape[0] // 2)
+                    pair = out_ref.at[part], out_hbm.at[part]
+                else:
+                    part = pl.ds(len(copies) * (kpg // 2), kpg // 2)
+                    pair = out_ref.at[:, :, part], out_hbm.at[:, :, part]
+                copies.append(pltpu.make_async_copy(*pair, sems.at[len(copies)]))
+                copies[-1].start()
+        for copy in copies:
+            copy.wait()
 
     return call(
         body,
@@ -253,20 +245,21 @@
             pltpu.VMEM((2 * boxes, 2 * rim), bf16),
             pltpu.VMEM((2 * rim, kpg), bf16),
             pltpu.VMEM((2, 2 * boxes, kpg), bf16),
-            pltpu.SemaphoreType.DMA,
+            pltpu.SemaphoreType.DMA((2,)),
         ],
-        flops=2 * 2 * boxes * 2 * rim * kpg,
+        flops=2 * 2 * boxes * rows * kpg,
     )[0]
 
 
-def operators_of_lists(offsets, counts, table):
+def operators_of_lists(sources, offsets, counts, table):
     slots, boxes = offsets.shape
     operators, _, half = table.shape
     lanes = 2 * half
 
     def body(ins, outs, rest):
-        off_in, cnt_in, tab_in = ins
-        (coef_ref,) = outs
+        src_in, off_in, cnt_in, tab_in = ins
+        coef_ref, lane_ref = outs
+        src = src_in()[...].T
         off = jnp.where(iota((slots, boxes), 0) < cnt_in()[...], off_in()[...], -1).T
         size = slots * CHUNK
         tables = jnp.swapaxes(tab_in()[...], 0, 1)
@@ -277,20 +270,22 @@
                 [ones_where(off[rows, m : m + 1] == iota((CHUNK, operators), 1)) for m in range(slots)], axis=0
             )
             coef_ref[chunk * size : (chunk + 1) * size] = nn(pick, flat).astype(bf16)
+            for m in range(slots):
+                at = chunk * size + m * CHUNK
+                lane_ref[at : at + CHUNK] = jnp.broadcast_to(src[rows, m : m + 1], (CHUNK, LANES)).astype(jnp.int16)
 
     return call(
         body,
-        [offsets, counts, table],
-        [H, H, H],
-        [((slots * boxes, lanes), bf16, V)],
+        [sources, offsets, counts, table],
+        [H, H, H, H],
+        [((slots * boxes, lanes), bf16, V), ((slots * boxes, LANES), jnp.int16, V)],
         "operators_of_lists",
         flops=2 * slots * boxes * operators * lanes,
-    )[0]
-
-
-def parent_sums(pattern, sources, coef):
+    )
+
+
+def parent_sums(pattern, sources, coef, slots):
     total, lanes = pattern.shape
-    slots = sources.shape[0]
     half = lanes // 2
     size = slots * CHUNK
     chunks = total // CHUNK
@@ -300,13 +295,15 @@
         pat_ref, src_ref, coef_ref = ins
         (out_hbm,) = outs
         pick_ref, out_ref, sems = rest
-        src = src_ref[...].T
+        one, zero = jnp.ones((), bf16), jnp.zeros((), bf16)
         for chunk in range(chunks):
-            rows = slice(chunk * CHUNK, (chunk + 1) * CHUNK)
+            part = slice(chunk * size, (chunk + 1) * size)
+            src = src_ref[part]
+            lane = lax.broadcasted_iota(jnp.int16, src.shape, 1)
             hot = jnp.concatenate(
-                [ones_where(src[rows, m : m + 1] == iota((CHUNK, total), 1)) for m in range(slots)], axis=0
+                [jnp.where(src == lane + jnp.int16(at), one, zero) for at in range(0, total, LANES)], axis=1
             )
-            pick_ref[chunk * size : (chunk + 1) * size] = nn(hot, pat_ref[...])
+            pick_ref[part] = nn(hot, pat_ref[...])
         copies = []
         for chunk in range(chunks):
             real = imag = 0.0
@@ -372,11 +369,11 @@
             c, s = both[:, :width], both[:, width:]
             low_ref[:boxes, cols] = (sr * c + si * s).astype(bf16)
             low_ref[boxes:, cols] = (si * c - sr * s).astype(bf16)
-        first = nt(w_ref[:rim], low_ref[...]).astype(bf16)
-        last = nt(w_ref[rows - rim :], low_ref[...]).astype(bf16)
-        for side, terms in enumerate((first, last)):
+        ends = jnp.concatenate([w_ref[:rim], w_ref[rows - rim :]], axis=0)
+        terms = nt(ends, low_ref[...]).astype(bf16)
+        for side in range(2):
             for r in range(2):
-                rim_ref[side, r] = terms[:, r * boxes : (r + 1) * boxes]
+                rim_ref[side, r] = terms[side * rim : (side + 1) * rim, r * boxes : (r + 1) * boxes]
 
     return call(
         body,
@@ -427,17 +424,22 @@
     )[0]
 
 
-def near_sums(own, lead, trail, sources, offsets, counts, table):
+def near_sums(own, lead, trail, sources, offsets, counts, table, phase):
     _, kcg, boxes = own.shape
+    kpg = phase.shape[2]
     slots = sources.shape[0]
     operators = table.shape[0]
     depth = 2 * boxes
     pair = 2
 
     def body(ins, outs, rest):
-        own_in, lead_in, trail_in, src_in, off_in, cnt_in, tab_in = ins
-        (out_ref,) = outs
-        ext_ref, tt_ref = rest
+        own_in, lead_in, trail_in, src_in, off_in, cnt_in, tab_in, ph_in = ins
+        out_ref, phase_ref = outs
+        ext_ref, tt_ref, dense_ref = rest
+        dense_ref[...] = ph_in()[:, 0, :]
+        sine, cosine = sincos(dense_ref[...])
+        phase_ref[:OCTANTS] = cosine
+        phase_ref[OCTANTS:] = sine
         eye = identity(boxes)
         own_ref = own_in()
         tables = jnp.swapaxes(tab_in()[...], 0, 1)
@@ -480,14 +482,18 @@
 
     return call(
         body,
-        [own, lead, trail, sources, offsets, counts, table],
-        [H] * 7,
-        [(own.shape, f32, V)],
+        [own, lead, trail, sources, offsets, counts, table, phase],
+        [H] * 8,
+        [(own.shape, f32, V), ((2 * OCTANTS, kpg), f32, V)],
         "near_sums",
-        scratch=[pltpu.VMEM((2 * kcg, depth), bf16), pltpu.VMEM((2 * kcg, operators), bf16)],
+        scratch=[
+            pltpu.VMEM((2 * kcg, depth), bf16),
+            pltpu.VMEM((2 * kcg, operators), bf16),
+            pltpu.VMEM((OCTANTS, kpg), f32),
+        ],
         flops=2 * slots * boxes * 2 * kcg * (depth + operators),
         limit=24 << 20,
-    )[0]
+    )
 
 
 def plain_translate(pattern, table, sources, offsets, counts):
@@ -548,7 +554,7 @@
     else:
         rims = [shift(own[:, kcg - rim :], "samp", 1), shift(own[:, :rim], "samp", -1)]
         spans = ((0, 0, rim), (1, 0, rim))
-    cosine, sine, inner, weights, family, phases, lead, trail = prepare(
+    cosine, sine, inner, family, weights, lead, trail = prepare(
         own, octant, parent, shift_phase, interp_weights, parents
     )
     pattern = rise(rims, spans, family, cosine, sine, inner, weights, parents, packed)
@@ -557,8 +563,10 @@
     table = parent_table[:, :, 0, :]
     if packed:
         regrouped = lax.all_to_all(pattern, "box", split_axis=0, concat_axis=0, tiled=True)
-        coef = operators_of_lists(parent_offsets.T, parent_counts[None, :], jnp.swapaxes(table, 0, 1))
-        far = parent_sums(regrouped, parent_sources.T, coef)
+        coef, sources = operators_of_lists(
+            parent_sources.T, parent_offsets.T, parent_counts[None, :], jnp.swapaxes(table, 0, 1)
+        )
+        far = parent_sums(regrouped, sources, coef, parent_sources.shape[1])
         far, lead, trail = lax.optimization_barrier((far, lead, trail))
         returned = lax.all_to_all(far, "box", split_axis=0, concat_axis=0, tiled=True)
     else:
@@ -569,7 +577,7 @@
         far = jnp.transpose(far, (0, 2, 1))
         returned = lax.all_to_all(far, "box", split_axis=1, concat_axis=2, tiled=True)
 
-    nearby = near_sums(
+    nearby, phases = near_sums(
         own,
         lead,
         trail,
@@ -577,6 +585,7 @@
         child_offsets.T,
         child_counts[None, :],
         jnp.swapaxes(child_table[:, :, 0, :], 0, 1),
+        shift_phase,
     )
     returned, nearby = lax.optimization_barrier((returned, nearby))
     lowered, terms = lower(returned, parent, octant, phases, interp_weights, parents, rim, packed)

time: 44.9 us -> 42.5 us (0.947)
  Pallas kernels: 17.6 us -> 16.4 us
  waiting for transfers between devices: 11.2 us -> 10.1 us
  local copies, waits for them, and re-layouts: 0.66 us -> 0.03 us
  starting transfers between devices: 14.7 us -> 15.3 us
    pallas_call x8, Pallas kernels: 17.6 us -> 16.4 us  [call(): pl.pallas_call(kernel, out_shape=[jax.ShapeDtypeStruct(shape, dtype) if p...]
    all_to_all x1, waiting for transfers between devices: 5.52 us -> 4.59 us  [local(): lax.all_to_all(pattern, 'box', split_axis=0, concat_axis=0, tiled=True)]
    unnamed x18 -> x10, local copies, waits for them, and re-layouts: 0.66 us -> 0.03 us
    ppermute x2, starting transfers between devices: 2.64 us -> 3.26 us  [exchange(): return lax.ppermute(value, axis, pairs + [(j, i) for i, j in pairs])]
  transfers between devices with their start and end apart: 6 -> 6, of which waited for: 3 -> 3; matrix products, arithmetic and copies ran while one was open for 0% -> 0% of each run, Pallas kernels for 30% -> 29%
where the time goes in v4:
time: 42.5 us; the launch traced here: 42 us
  Pallas kernels  16.4 us (39%)
  starting transfers between devices  15.3 us (36%)
  waiting for transfers between devices  10.1 us (24%)
    pallas_call x8, Pallas kernels, call(): pl.pallas_call(kernel, out_shape=[jax.ShapeDtypeStruct(shape, dtype) if p...  16.4 us
    all_to_all x1, starting transfers between devices, local(): lax.all_to_all(pattern, 'box', split_axis=0, concat_axis=0, tiled=True)  7.88 us
    all_to_all x1, waiting for transfers between devices, local(): lax.all_to_all(far, 'box', split_axis=0, concat_axis=0, tiled=True)  5.03 us
    all_to_all x1, waiting for transfers between devices, local(): lax.all_to_all(pattern, 'box', split_axis=0, concat_axis=0, tiled=True)  4.59 us
    all_to_all x1, starting transfers between devices, local(): lax.all_to_all(far, 'box', split_axis=0, concat_axis=0, tiled=True)  3.69 us
    ppermute x2, starting transfers between devices, exchange(): return lax.ppermute(value, axis, pairs + [(j, i) for i, j in pairs])  3.26 us
  transfers between devices with their start and end apart: 6, of which 3 were waited for; matrix products, arithmetic and copies ran while one was open for 0% of the time, Pallas kernels for 29%

profile of v4, /device:TPU:0, one launch (start us, length us, event | category | flops | bytes accessed | tf_op | source)
XLA Modules:
  0.0 42.0 jit_solution(17752624197261286868)
XLA Ops:
  0.0 0.5 %collective-permute-start = (bf16[2,512,128]{2,1,0:T(8,128)(2,1)}, bf16[2,512,128]{2,1,0:T(8,128)(2,1)S(1)}, u32[]{:S(2)}, u32[]{:S(2)}) collective-permute-start(bf16[2,512,128]{2,1,0:T(8,128)(2,1)} %bitcast.30), channel_id=1, source_target_pairs={{0,1},{1,0},{2,3},{3,2},{4,5},{5,4},{6,7},{7,6},{8,9},{9,8},{10,11... | collective-permute-start | bytes 786440 | tf_op jit(solution)/shard_map/ppermute | solution.py:516
  0.5 2.0 %prepare.1 = (f32[128,2048]{1,0:T(8,128)S(1)}, f32[128,2048]{1,0:T(8,128)S(1)}, bf16[256,512]{1,0:T(8,128)(2,1)S(1)}, bf16[32,256]{1,0:T(8,128)(2,1)S(1)}, bf16[...) custom-call(bf16[2,512,128]{2,1,0:T(8,128)(2,1)} %bitcast.31, ...), custom_call_target="tpu_custom_call" | custom-call | flops 1048576 | bytes 1048576 | tf_op jit(solution)/shard_map/prepare/pallas_call | solution.py:51
  2.5 0.0 collective-permute-done.refs_0_
  2.5 0.0 copy-start.4
  2.5 0.0 copy-start.3
  2.5 2.4 %rise.1 = bf16[512,256]{1,0:T(8,128)(2,1)} custom-call(bf16[2,512,128]{2,1,0:T(8,128)(2,1)S(1)} %collective-permute-done.refs_0_, bf16[32,256]{1,0:T(8,128)(2,1)S(1)} %get-tuple-element.23.refs_1_, f32[128,2048]{1,0:T(8,128)S(1)} %get-tuple-element.24.refs_2_, f32[128,2048]{1,0:T(8,128)S(1)} %get-tuple-element.25.refs_3_, ...), custom_call_target="tpu_custom_call" | custom-call | flops 671088640 | bytes 1048576 | tf_op jit(solution)/shard_map/rise/pallas_call | solution.py:51
  4.9 7.9 %all-to-all-start = ((bf16[16,32,256]{2,1,0:T(8,128)(2,1)}), bf16[16,32,256]{2,1,0:T(8,128)(2,1)S(1)}, u32[]{:S(2)}, u32[]{:S(2)}) async-start(bf16[16,32,256]{2,1,0:T(8,128)(2,1)} %bitcast.28), calls=%async_computation | async-start | bytes 524288 | tf_op jit(solution)/shard_map/all_to_all | solution.py:565
  12.7 0.0 copy-done.4
  12.8 2.0 %collective-permute-start.1 = (bf16[2,32,512]{2,1,0:T(8,128)(2,1)S(1)}, bf16[2,32,512]{2,1,0:T(8,128)(2,1)}, u32[]{:S(2)}, u32[]{:S(2)}) collective-permute-start(bf16[2,32,512]{2,1,0:T(8,128)(2,1)S(1)} %copy-done.4), channel_id=1, source_target_pairs={{0,2},{4,6},{8,10},{12,14},{16,18},{20,22},{24,26},{28,30},{2,0},{... | collective-permute-start | bytes 196616 | tf_op jit(solution)/shard_map/ppermute | solution.py:522
  14.7 0.0 copy-done.3
  14.7 1.3 %collective-permute-start.2 = (bf16[2,32,512]{2,1,0:T(8,128)(2,1)S(1)}, bf16[2,32,512]{2,1,0:T(8,128)(2,1)}, u32[]{:S(2)}, u32[]{:S(2)}) collective-permute-start(bf16[2,32,512]{2,1,0:T(8,128)(2,1)S(1)} %copy-done.3), channel_id=1, source_target_pairs={{2,4},{6,8},{10,12},{14,16},{18,20},{22,24},{26,28},{4,2},{8,6},{1... | collective-permute-start | bytes 196616 | tf_op jit(solution)/shard_map/ppermute | solution.py:522
  16.0 2.7 %operators_of_lists.1 = (bf16[4096,256]{1,0:T(8,128)(2,1)S(1)}, s16[4096,128]{1,0:T(8,128)(2,1)S(1)}) custom-call(s32[8,512]{1,0:T(8,128)} %bitcast.35, s32[8,512]{1,0:T(8,128)} %bitcast.36, s32[1,512]{1,0:T(1,128)} %bitcast.39, bf16[316,2,128]{2,1,0:T(2,128)(2,1)} %bitcast.34), custom_call_target="tpu_custom_call" | custom-call | flops 662700032 | bytes 1048576 | tf_op jit(solution)/shard_map/operators_of_lists/pallas_call | solution.py:51
  18.7 4.6 %all-to-all-done = bf16[16,32,256]{2,1,0:T(8,128)(2,1)S(1)} async-done(((bf16[16,32,256]{2,1,0:T(8,128)(2,1)}), bf16[16,32,256]{2,1,0:T(8,128)(2,1)S(1)}, u32[]{:S(2)}, u32[]{:S(2)}) %all-to-all-start) | async-done | bytes 262176 | tf_op jit(solution)/shard_map/all_to_all | solution.py:565
  23.3 2.3 %parent_sums.1 = bf16[512,256]{1,0:T(8,128)(2,1)} custom-call(bf16[512,256]{1,0:T(8,128)(2,1)S(1)} %bitcast.23, s16[4096,128]{1,0:T(8,128)(2,1)S(1)} %get-tuple-element.28.refs_1_, bf16[4096,256]{1,0:T(8,128)(2,1)S(1)} %get-tuple-element.29.refs_2_), custom_call_target="tpu_custom_call" | custom-call | flops 1073741824 | bytes 1048576 | tf_op jit(solution)/shard_map/parent_sums/pallas_call | solution.py:51
  25.6 0.0 copy-start
  25.6 0.0 copy-start.1
  25.7 0.0 copy-start.2
  25.7 0.0 collective-permute-done.1.refs_1_
  25.7 0.0 collective-permute-done.2.refs_2_
  25.7 3.7 %all-to-all-start.1 = ((bf16[16,32,256]{2,1,0:T(8,128)(2,1)}), bf16[16,32,256]{2,1,0:T(8,128)(2,1)S(1)}, u32[]{:S(2)}, u32[]{:S(2)}) async-start(bf16[16,32,256]{2,1,0:T(8,128)(2,1)} %bitcast.29), calls=%async_computation.1 | async-start | bytes 524288 | tf_op jit(solution)/shard_map/all_to_all | solution.py:571
  29.4 4.5 %near_sums.1 = (f32[2,512,128]{2,1,0:T(8,128)S(1)}, f32[16,2048]{1,0:T(8,128)S(1)}) custom-call(bf16[2,512,128]{2,1,0:T(8,128)(2,1)} %bitcast.32, bf16[2,32,512]{2,1,0:T(8,128)(2,1)} %collective-permute-done.1.refs_1_, bf16[2,32,512]{2,1,0:T(8,128)(2,1)} %collective-permute-done.2.refs_2_, s32[8,128]{1,0:T(8,128)} %bitcast.37, s32[8,128]{1,0:T(8,128)} %bitcast.38, ...), custom_call_target="tpu_custom_call" | custom-call | flops 1199570944 | bytes 1048576 | tf_op jit(solution)/shard_map/near_sums/pallas_call | solution.py:51
  33.9 5.0 %all-to-all-done.1 = bf16[16,32,256]{2,1,0:T(8,128)(2,1)S(1)} async-done(((bf16[16,32,256]{2,1,0:T(8,128)(2,1)}), bf16[16,32,256]{2,1,0:T(8,128)(2,1)S(1)}, u32[]{:S(2)}, u32[]{:S(2)}) %all-to-all-start.1) | async-done | bytes 262176 | tf_op jit(solution)/shard_map/all_to_all | solution.py:571
  38.9 0.0 copy-done
  38.9 0.0 copy-done.1
  38.9 0.0 copy-done.2
  38.9 1.1 %lower.1 = (bf16[256,2048]{1,0:T(8,128)(2,1)S(1)}, bf16[2,2,64,128]{3,2,1,0:T(8,128)(2,1)S(1)}) custom-call(bf16[512,256]{1,0:T(8,128)(2,1)S(1)} %bitcast.22, s32[1,128]{1,0:T(1,128)S(1)} %bitcast.27, s32[1,128]{1,0:T(1,128)S(1)} %bitcast.25, f32[16,2048]{1,0:T(8,128)S(1)} %get-tuple-element.37.refs_3_, bf16[640,2048]{1,0:T(8,128)(2,1)S(1)} %copy-done), custom_call_target="tpu_custom_call" | custom-call | flops 134217728 | bytes 1048576 | tf_op jit(solution)/shard_map/lower/pallas_call | solution.py:51
  40.0 0.1 collective-permute-start.3
  40.1 0.7 %anterpolate.1.refs_0_ = f32[2,512,128]{2,1,0:T(8,128)S(1)} custom-call(bf16[640,2048]{1,0:T(8,128)(2,1)S(1)} %copy-done, bf16[256,2048]{1,0:T(8,128)(2,1)S(1)} %get-tuple-element.38.refs_1_, f32[2,512,128]{2,1,0:T(8,128)S(1)} %get-tuple-element.39.refs_2_), custom_call_target="tpu_custom_call" | custom-call | flops 536870912 | bytes 1048576 | tf_op jit(solution)/shard_map/anterpolate/pallas_call | solution.py:51
  40.8 0.5 %collective-permute-done.3.refs_1_ = bf16[2,2,64,128]{3,2,1,0:T(8,128)(2,1)S(1)} collective-permute-done((bf16[2,2,64,128]{3,2,1,0:T(8,128)(2,1)S(1)}, bf16[2,2,64,128]{3,2,1,0:T(8,128)(2,1)S(1)}, u32[]{:S(2)}, u32[]{:S(2)}) %collective-permute-start.3) | collective-permute-done | bytes 65568 | tf_op jit(solution)/shard_map/ppermute | solution.py:516
  41.3 0.7 %finish.1 = bf16[2,512,128]{2,1,0:T(8,128)(2,1)} custom-call(f32[2,512,128]{2,1,0:T(8,128)S(1)} %anterpolate.1.refs_0_, bf16[2,2,64,128]{3,2,1,0:T(8,128)(2,1)S(1)} %collective-permute-done.3.refs_1_), custom_call_target="tpu_custom_call" | custom-call | flops 1048576 | bytes 1048576 | tf_op jit(solution)/shard_map/finish/pallas_call | solution.py:51
Async XLA Ops:
  0.0 2.5 %collective-permute-start = (bf16[2,512,128]{2,1,0:T(8,128)(2,1)}, bf16[2,512,128]{2,1,0:T(8,128)(2,1)S(1)}, u32[]{:S(2)}, u32[]{:S(2)}) collective-permute-start(bf16[2,512,128]{2,1,0:T(8,128)(2,1)} %bitcast.30), channel_id=1, source_target_pairs={{0,1},{1,0},{2,3},{3,2},{4,5},{5,4},{6,7},{7,6},{8,9},{9,8},{10,11... | collective-permute-start | bytes 786440 | tf_op jit(solution)/shard_map/ppermute | solution.py:516
  2.5 10.3 %copy-start.4 = (bf16[2,32,512]{2,1,0:T(8,128)(2,1)S(1)}, bf16[2,32,512]{2,1,0:T(8,128)(2,1)}, u32[]{:S(2)}) copy-start(bf16[2,32,512]{2,1,0:T(8,128)(2,1)} %get-tuple-element.30) | copy-start | bytes 196612
  2.5 12.3 %copy-start.3 = (bf16[2,32,512]{2,1,0:T(8,128)(2,1)S(1)}, bf16[2,32,512]{2,1,0:T(8,128)(2,1)}, u32[]{:S(2)}) copy-start(bf16[2,32,512]{2,1,0:T(8,128)(2,1)} %get-tuple-element.31) | copy-start | bytes 196612
  4.9 18.4 %all-to-all-start = ((bf16[16,32,256]{2,1,0:T(8,128)(2,1)}), bf16[16,32,256]{2,1,0:T(8,128)(2,1)S(1)}, u32[]{:S(2)}, u32[]{:S(2)}) async-start(bf16[16,32,256]{2,1,0:T(8,128)(2,1)} %bitcast.28), calls=%async_computation | async-start | bytes 524288 | tf_op jit(solution)/shard_map/all_to_all | solution.py:565
  12.8 12.9 %collective-permute-start.1 = (bf16[2,32,512]{2,1,0:T(8,128)(2,1)S(1)}, bf16[2,32,512]{2,1,0:T(8,128)(2,1)}, u32[]{:S(2)}, u32[]{:S(2)}) collective-permute-start(bf16[2,32,512]{2,1,0:T(8,128)(2,1)S(1)} %copy-done.4), channel_id=1, source_target_pairs={{0,2},{4,6},{8,10},{12,14},{16,18},{20,22},{24,26},{28,30},{2,0},{... | collective-permute-start | bytes 196616 | tf_op jit(solution)/shard_map/ppermute | solution.py:522
  14.7 10.9 %collective-permute-start.2 = (bf16[2,32,512]{2,1,0:T(8,128)(2,1)S(1)}, bf16[2,32,512]{2,1,0:T(8,128)(2,1)}, u32[]{:S(2)}, u32[]{:S(2)}) collective-permute-start(bf16[2,32,512]{2,1,0:T(8,128)(2,1)S(1)} %copy-done.3), channel_id=1, source_target_pairs={{2,4},{6,8},{10,12},{14,16},{18,20},{22,24},{26,28},{4,2},{8,6},{1... | collective-permute-start | bytes 196616 | tf_op jit(solution)/shard_map/ppermute | solution.py:522
  25.6 13.3 %copy-start = (bf16[640,2048]{1,0:T(8,128)(2,1)S(1)}, bf16[640,2048]{1,0:T(8,128)(2,1)}, u32[]{:S(2)}) copy-start(bf16[640,2048]{1,0:T(8,128)(2,1)} %refs_0_.1) | copy-start | bytes 7864324
  25.6 13.2 %copy-start.1 = (s32[128]{0:T(128)S(1)}, s32[128]{0:T(128)}, u32[]{:S(2)}) copy-start(s32[128]{0:T(128)} %param.15) | copy-start | bytes 1540
  25.7 13.2 %copy-start.2 = (s32[128]{0:T(128)S(1)}, s32[128]{0:T(128)}, u32[]{:S(2)}) copy-start(s32[128]{0:T(128)} %param.14) | copy-start | bytes 1540
  25.7 13.2 %all-to-all-start.1 = ((bf16[16,32,256]{2,1,0:T(8,128)(2,1)}), bf16[16,32,256]{2,1,0:T(8,128)(2,1)S(1)}, u32[]{:S(2)}, u32[]{:S(2)}) async-start(bf16[16,32,256]{2,1,0:T(8,128)(2,1)} %bitcast.29), calls=%async_computation.1 | async-start | bytes 524288 | tf_op jit(solution)/shard_map/all_to_all | solution.py:571
  40.0 1.3 %collective-permute-start.3 = (bf16[2,2,64,128]{3,2,1,0:T(8,128)(2,1)S(1)}, bf16[2,2,64,128]{3,2,1,0:T(8,128)(2,1)S(1)}, u32[]{:S(2)}, u32[]{:S(2)}) collective-permute-start(bf16[2,2,64,128]{3,2,1,0:T(8,128)(2,1)S(1)} %get-tuple-element.40), channel_id=1, source_target_pairs={{0,1},{1,0},{2,3},{3,2},{4,5},{5,4},{6,7},{7,6},{8,9},{9,8},{10,11... | collective-permute-start | bytes 196616 | tf_op jit(solution)/shard_map/ppermute | solution.py:516

commit v5 on v4

--- a/solution.py
+++ b/solution.py
@@ -181,11 +181,12 @@
     )
 
 
-def rise(rims, spans, family, cosine, sine, inner, weights, parents, packed):
+def rise(rims, spans, family, cosine, sine, inner, weights, parents, order):
     boxes, kpg = cosine.shape
     rows = weights.shape[0]
     rim = spans[0][2] - spans[0][1]
     width = 256
+    packed = order is not None
     shape = (kpg // LANES * parents, 2 * LANES) if packed else (2, parents, kpg)
 
     def body(ins, outs, rest):
@@ -210,19 +211,17 @@
                 shift_ref[r, :boxes, cols] = high
                 shift_ref[r, boxes:, cols] = (value - high.astype(f32)).astype(bf16)
         copies = []
-        for step in range(kpg // width):
-            cols = slice(step * width, (step + 1) * width)
-            for r in range(2):
-                total = nn(family_ref[...], shift_ref[r, :, cols]).astype(bf16)
-                if packed:
-                    for part in range(width // LANES):
-                        row = (step * (width // LANES) + part) * parents
-                        out_ref[row : row + parents, r * LANES : (r + 1) * LANES] = total[
-                            :, part * LANES : (part + 1) * LANES
-                        ]
-                else:
-                    out_ref[r, :, cols] = total
-            if (step + 1) * width * 2 % kpg == 0:
+        pieces = kpg // LANES
+        for n in range(pieces):
+            piece = order[n] if packed else n
+            cols = slice(piece * LANES, (piece + 1) * LANES)
+            both = nn(family_ref[...], jnp.concatenate([shift_ref[0, :, cols], shift_ref[1, :, cols]], axis=1))
+            both = both.astype(bf16)
+            if packed:
+                out_ref[n * parents : (n + 1) * parents] = both
+            else:
+                out_ref[0, :, cols], out_ref[1, :, cols] = both[:, :LANES], both[:, LANES:]
+            if (n + 1) * 2 % pieces == 0:
                 if packed:
                     part = pl.ds(len(copies) * (shape[0] // 2), shape[0] // 2)
                     pair = out_ref.at[part], out_hbm.at[part]
@@ -251,7 +250,7 @@
     )[0]
 
 
-def operators_of_lists(sources, offsets, counts, table):
+def operators_of_lists(sources, offsets, counts, table, order):
     slots, boxes = offsets.shape
     operators, _, half = table.shape
     lanes = 2 * half
@@ -259,8 +258,17 @@
     def body(ins, outs, rest):
         src_in, off_in, cnt_in, tab_in = ins
         coef_ref, lane_ref = outs
-        src = src_in()[...].T
-        off = jnp.where(iota((slots, boxes), 0) < cnt_in()[...], off_in()[...], -1).T
+        family = boxes // len(order)
+        src = src_in()[...]
+        home = src // family
+        moved = src
+        for n, index in enumerate(order):
+            moved = jnp.where(home == index, src + (n - index) * family, moved)
+        off = jnp.where(iota((slots, boxes), 0) < cnt_in()[...], off_in()[...], -1)
+        src, off = (
+            jnp.concatenate([x.T[index * family : (index + 1) * family] for index in order], axis=0)
+            for x in (moved, off)
+        )
         size = slots * CHUNK
         tables = jnp.swapaxes(tab_in()[...], 0, 1)
         flat = jnp.concatenate([tables[0], tables[1]], axis=1)
@@ -342,9 +350,10 @@
     )[0]
 
 
-def lower(far, parent, octant, phases, weights, parents, rim, packed):
+def lower(far, parent, octant, phases, weights, parents, rim, order):
     boxes = parent.shape[1]
     rows, kpg = weights.shape
+    packed = order is not None
     width = LANES if packed else 256
 
     def body(ins, outs, rest):
@@ -356,7 +365,8 @@
         for step in range(kpg // width):
             cols = slice(step * width, (step + 1) * width)
             if packed:
-                spread = nn(hot, far_ref[step * parents : (step + 1) * parents])
+                at = order.index(step) * parents
+                spread = nn(hot, far_ref[at : at + parents])
                 sr, si = spread[:, :LANES], spread[:, LANES:]
             else:
                 sr, si = nn(hot, far_ref[0, :, cols]), nn(hot, far_ref[1, :, cols])
@@ -511,6 +521,20 @@
     )
 
 
+def ring(peers):
+    gray = [i ^ (i >> 1) for i in range(peers)]
+    if sorted(gray) != list(range(peers)):
+        return list(range(peers))
+    middle = gray.index((peers // 2 + 1) % peers)
+    return gray[middle:] + gray[:middle]
+
+
+def regroup(value, order):
+    return lax.all_to_all(
+        value, "box", split_axis=0, concat_axis=0, tiled=True, axis_index_groups=[list(order)]
+    )
+
+
 def shift(value, axis, step):
     peers = lax.axis_size(axis)
     return lax.ppermute(value, axis, [(i, (i + step) % peers) for i in range(peers)])
@@ -546,6 +570,7 @@
     kpg = interp_weights.shape[1]
     mine = kpg // peers
     packed = mine == LANES and total % CHUNK == 0
+    order = ring(peers) if packed else None
     parent, octant = child_parent[None, :], child_octant[None, :]
 
     if groups == 2:
@@ -557,18 +582,18 @@
     cosine, sine, inner, family, weights, lead, trail = prepare(
         own, octant, parent, shift_phase, interp_weights, parents
     )
-    pattern = rise(rims, spans, family, cosine, sine, inner, weights, parents, packed)
+    pattern = rise(rims, spans, family, cosine, sine, inner, weights, parents, order)
     lead, trail = exchange(lead, "box", 0), exchange(trail, "box", 1)
 
     table = parent_table[:, :, 0, :]
     if packed:
-        regrouped = lax.all_to_all(pattern, "box", split_axis=0, concat_axis=0, tiled=True)
+        regrouped = regroup(pattern, order)
         coef, sources = operators_of_lists(
-            parent_sources.T, parent_offsets.T, parent_counts[None, :], jnp.swapaxes(table, 0, 1)
+            parent_sources.T, parent_offsets.T, parent_counts[None, :], jnp.swapaxes(table, 0, 1), order
         )
         far = parent_sums(regrouped, sources, coef, parent_sources.shape[1])
         far, lead, trail = lax.optimization_barrier((far, lead, trail))
-        returned = lax.all_to_all(far, "box", split_axis=0, concat_axis=0, tiled=True)
+        returned = regroup(far, order)
     else:
         regrouped = lax.all_to_all(pattern, "box", split_axis=2, concat_axis=1, tiled=True)
         far = plain_translate(
@@ -588,7 +613,7 @@
         shift_phase,
     )
     returned, nearby = lax.optimization_barrier((returned, nearby))
-    lowered, terms = lower(returned, parent, octant, phases, interp_weights, parents, rim, packed)
+    lowered, terms = lower(returned, parent, octant, phases, interp_weights, parents, rim, order)
     if groups == 2:
         got = shift(terms, "samp", 1)
         start_terms, end_terms = (got, 1), (got, 0)

time: 42.5 us -> 38.7 us (0.911)
  waiting for transfers between devices: 10.1 us -> 4.63 us
  starting transfers between devices: 15.3 us -> 16.9 us
    all_to_all x2, waiting for transfers between devices: 9.62 us -> 4.13 us  [regroup(): lax.all_to_all(value, 'box', split_axis=0, concat_axis=0, tiled=True, axi...]
    all_to_all x2, starting transfers between devices: 11.6 us -> 14.5 us  [regroup(): lax.all_to_all(value, 'box', split_axis=0, concat_axis=0, tiled=True, axi...]
    ppermute x2, starting transfers between devices: 3.26 us -> 1.9 us  [exchange(): return lax.ppermute(value, axis, pairs + [(j, i) for i, j in pairs])]
  transfers between devices with their start and end apart: 6 -> 6, of which waited for: 3 -> 3; matrix products, arithmetic and copies ran while one was open for 0% -> 0% of each run, Pallas kernels for 29% -> 32%
where the time goes in v5:
time: 38.7 us; the launch traced here: 38.2 us
  starting transfers between devices  16.9 us (44%)
  Pallas kernels  16.5 us (43%)
  waiting for transfers between devices  4.63 us (12%)
    pallas_call x8, Pallas kernels, call(): pl.pallas_call(kernel, out_shape=[jax.ShapeDtypeStruct(shape, dtype) if p...  16.5 us
    all_to_all x2, starting transfers between devices, regroup(): lax.all_to_all(value, 'box', split_axis=0, concat_axis=0, tiled=True, axi...  14.5 us
    all_to_all x2, waiting for transfers between devices, regroup(): lax.all_to_all(value, 'box', split_axis=0, concat_axis=0, tiled=True, axi...  4.13 us
    ppermute x2, starting transfers between devices, exchange(): return lax.ppermute(value, axis, pairs + [(j, i) for i, j in pairs])  1.9 us
  transfers between devices with their start and end apart: 6, of which 3 were waited for; matrix products, arithmetic and copies ran while one was open for 0% of the time, Pallas kernels for 32%

profile of v5, /device:TPU:0, one launch (start us, length us, event | category | flops | bytes accessed | tf_op | source)
XLA Modules:
  0.0 38.2 jit_solution(277070499978315293)
XLA Ops:
  0.0 0.5 %collective-permute-start = (bf16[2,512,128]{2,1,0:T(8,128)(2,1)}, bf16[2,512,128]{2,1,0:T(8,128)(2,1)S(1)}, u32[]{:S(2)}, u32[]{:S(2)}) collective-permute-start(bf16[2,512,128]{2,1,0:T(8,128)(2,1)} %bitcast.30), channel_id=1, source_target_pairs={{0,1},{1,0},{2,3},{3,2},{4,5},{5,4},{6,7},{7,6},{8,9},{9,8},{10,11... | collective-permute-start | bytes 786440 | tf_op jit(solution)/shard_map/ppermute | solution.py:540
  0.5 2.0 %prepare.1 = (f32[128,2048]{1,0:T(8,128)S(1)}, f32[128,2048]{1,0:T(8,128)S(1)}, bf16[256,512]{1,0:T(8,128)(2,1)S(1)}, bf16[32,256]{1,0:T(8,128)(2,1)S(1)}, bf16[...) custom-call(bf16[2,512,128]{2,1,0:T(8,128)(2,1)} %bitcast.31, ...), custom_call_target="tpu_custom_call" | custom-call | flops 1048576 | bytes 1048576 | tf_op jit(solution)/shard_map/prepare/pallas_call | solution.py:51
  2.5 0.0 collective-permute-done.refs_0_
  2.5 0.0 copy-start.4
  2.5 0.0 copy-start.3
  2.5 2.5 %rise.1 = bf16[512,256]{1,0:T(8,128)(2,1)} custom-call(bf16[2,512,128]{2,1,0:T(8,128)(2,1)S(1)} %collective-permute-done.refs_0_, bf16[32,256]{1,0:T(8,128)(2,1)S(1)} %get-tuple-element.23.refs_1_, f32[128,2048]{1,0:T(8,128)S(1)} %get-tuple-element.24.refs_2_, f32[128,2048]{1,0:T(8,128)S(1)} %get-tuple-element.25.refs_3_, ...), custom_call_target="tpu_custom_call" | custom-call | flops 671088640 | bytes 1048576 | tf_op jit(solution)/shard_map/rise/pallas_call | solution.py:51
  5.0 8.3 %all-to-all-start = ((bf16[16,32,256]{2,1,0:T(8,128)(2,1)}), bf16[16,32,256]{2,1,0:T(8,128)(2,1)S(1)}, u32[]{:S(2)}, u32[]{:S(2)}) async-start(bf16[16,32,256]{2,1,0:T(8,128)(2,1)} %bitcast.28), calls=%async_computation | async-start | bytes 524288 | tf_op jit(solution)/shard_map/all_to_all | solution.py:533
  13.3 0.0 copy-done.4
  13.3 0.6 %collective-permute-start.1 = (bf16[2,32,512]{2,1,0:T(8,128)(2,1)S(1)}, bf16[2,32,512]{2,1,0:T(8,128)(2,1)}, u32[]{:S(2)}, u32[]{:S(2)}) collective-permute-start(bf16[2,32,512]{2,1,0:T(8,128)(2,1)S(1)} %copy-done.4), channel_id=1, source_target_pairs={{0,2},{4,6},{8,10},{12,14},{16,18},{20,22},{24,26},{28,30},{2,0},{... | collective-permute-start | bytes 196616 | tf_op jit(solution)/shard_map/ppermute | solution.py:546
  14.0 0.0 copy-done.3
  14.0 1.3 %collective-permute-start.2 = (bf16[2,32,512]{2,1,0:T(8,128)(2,1)S(1)}, bf16[2,32,512]{2,1,0:T(8,128)(2,1)}, u32[]{:S(2)}, u32[]{:S(2)}) collective-permute-start(bf16[2,32,512]{2,1,0:T(8,128)(2,1)S(1)} %copy-done.3), channel_id=1, source_target_pairs={{2,4},{6,8},{10,12},{14,16},{18,20},{22,24},{26,28},{4,2},{8,6},{1... | collective-permute-start | bytes 196616 | tf_op jit(solution)/shard_map/ppermute | solution.py:546
  15.3 2.6 %operators_of_lists.1 = (bf16[4096,256]{1,0:T(8,128)(2,1)S(1)}, s16[4096,128]{1,0:T(8,128)(2,1)S(1)}) custom-call(s32[8,512]{1,0:T(8,128)} %bitcast.35, s32[8,512]{1,0:T(8,128)} %bitcast.36, s32[1,512]{1,0:T(1,128)} %bitcast.39, bf16[316,2,128]{2,1,0:T(2,128)(2,1)} %bitcast.34), custom_call_target="tpu_custom_call" | custom-call | flops 662700032 | bytes 1048576 | tf_op jit(solution)/shard_map/operators_of_lists/pallas_call | solution.py:51
  17.9 3.0 %all-to-all-done = bf16[16,32,256]{2,1,0:T(8,128)(2,1)S(1)} async-done(((bf16[16,32,256]{2,1,0:T(8,128)(2,1)}), bf16[16,32,256]{2,1,0:T(8,128)(2,1)S(1)}, u32[]{:S(2)}, u32[]{:S(2)}) %all-to-all-start) | async-done | bytes 262176 | tf_op jit(solution)/shard_map/all_to_all | solution.py:533
  20.9 2.3 %parent_sums.1 = bf16[512,256]{1,0:T(8,128)(2,1)} custom-call(bf16[512,256]{1,0:T(8,128)(2,1)S(1)} %bitcast.23, s16[4096,128]{1,0:T(8,128)(2,1)S(1)} %get-tuple-element.28.refs_1_, bf16[4096,256]{1,0:T(8,128)(2,1)S(1)} %get-tuple-element.29.refs_2_), custom_call_target="tpu_custom_call" | custom-call | flops 1073741824 | bytes 1048576 | tf_op jit(solution)/shard_map/parent_sums/pallas_call | solution.py:51
  23.2 0.0 copy-start
  23.2 0.0 copy-start.1
  23.3 0.0 copy-start.2
  23.3 0.0 collective-permute-done.1.refs_1_
  23.3 0.0 collective-permute-done.2.refs_2_
  23.3 6.2 %all-to-all-start.1 = ((bf16[16,32,256]{2,1,0:T(8,128)(2,1)}), bf16[16,32,256]{2,1,0:T(8,128)(2,1)S(1)}, u32[]{:S(2)}, u32[]{:S(2)}) async-start(bf16[16,32,256]{2,1,0:T(8,128)(2,1)} %bitcast.29), calls=%async_computation.1 | async-start | bytes 524288 | tf_op jit(solution)/shard_map/all_to_all | solution.py:533
  29.5 4.4 %near_sums.1 = (f32[2,512,128]{2,1,0:T(8,128)S(1)}, f32[16,2048]{1,0:T(8,128)S(1)}) custom-call(bf16[2,512,128]{2,1,0:T(8,128)(2,1)} %bitcast.32, bf16[2,32,512]{2,1,0:T(8,128)(2,1)} %collective-permute-done.1.refs_1_, bf16[2,32,512]{2,1,0:T(8,128)(2,1)} %collective-permute-done.2.refs_2_, s32[8,128]{1,0:T(8,128)} %bitcast.37, s32[8,128]{1,0:T(8,128)} %bitcast.38, ...), custom_call_target="tpu_custom_call" | custom-call | flops 1199570944 | bytes 1048576 | tf_op jit(solution)/shard_map/near_sums/pallas_call | solution.py:51
  33.9 1.1 %all-to-all-done.1 = bf16[16,32,256]{2,1,0:T(8,128)(2,1)S(1)} async-done(((bf16[16,32,256]{2,1,0:T(8,128)(2,1)}), bf16[16,32,256]{2,1,0:T(8,128)(2,1)S(1)}, u32[]{:S(2)}, u32[]{:S(2)}) %all-to-all-start.1) | async-done | bytes 262176 | tf_op jit(solution)/shard_map/all_to_all | solution.py:533
  35.0 0.0 copy-done
  35.0 0.0 copy-done.1
  35.0 0.0 copy-done.2
  35.0 1.1 %lower.1 = (bf16[256,2048]{1,0:T(8,128)(2,1)S(1)}, bf16[2,2,64,128]{3,2,1,0:T(8,128)(2,1)S(1)}) custom-call(bf16[512,256]{1,0:T(8,128)(2,1)S(1)} %bitcast.22, s32[1,128]{1,0:T(1,128)S(1)} %bitcast.27, s32[1,128]{1,0:T(1,128)S(1)} %bitcast.25, f32[16,2048]{1,0:T(8,128)S(1)} %get-tuple-element.37.refs_3_, bf16[640,2048]{1,0:T(8,128)(2,1)S(1)} %copy-done), custom_call_target="tpu_custom_call" | custom-call | flops 134217728 | bytes 1048576 | tf_op jit(solution)/shard_map/lower/pallas_call | solution.py:51
  36.1 0.1 collective-permute-start.3
  36.2 0.7 %anterpolate.1.refs_0_ = f32[2,512,128]{2,1,0:T(8,128)S(1)} custom-call(bf16[640,2048]{1,0:T(8,128)(2,1)S(1)} %copy-done, bf16[256,2048]{1,0:T(8,128)(2,1)S(1)} %get-tuple-element.38.refs_1_, f32[2,512,128]{2,1,0:T(8,128)S(1)} %get-tuple-element.39.refs_2_), custom_call_target="tpu_custom_call" | custom-call | flops 536870912 | bytes 1048576 | tf_op jit(solution)/shard_map/anterpolate/pallas_call | solution.py:51
  37.0 0.5 %collective-permute-done.3.refs_1_ = bf16[2,2,64,128]{3,2,1,0:T(8,128)(2,1)S(1)} collective-permute-done((bf16[2,2,64,128]{3,2,1,0:T(8,128)(2,1)S(1)}, bf16[2,2,64,128]{3,2,1,0:T(8,128)(2,1)S(1)}, u32[]{:S(2)}, u32[]{:S(2)}) %collective-permute-start.3) | collective-permute-done | bytes 65568 | tf_op jit(solution)/shard_map/ppermute | solution.py:540
  37.4 0.7 %finish.1 = bf16[2,512,128]{2,1,0:T(8,128)(2,1)} custom-call(f32[2,512,128]{2,1,0:T(8,128)S(1)} %anterpolate.1.refs_0_, bf16[2,2,64,128]{3,2,1,0:T(8,128)(2,1)S(1)} %collective-permute-done.3.refs_1_), custom_call_target="tpu_custom_call" | custom-call | flops 1048576 | bytes 1048576 | tf_op jit(solution)/shard_map/finish/pallas_call | solution.py:51
Async XLA Ops:
  0.0 2.5 %collective-permute-start = (bf16[2,512,128]{2,1,0:T(8,128)(2,1)}, bf16[2,512,128]{2,1,0:T(8,128)(2,1)S(1)}, u32[]{:S(2)}, u32[]{:S(2)}) collective-permute-start(bf16[2,512,128]{2,1,0:T(8,128)(2,1)} %bitcast.30), channel_id=1, source_target_pairs={{0,1},{1,0},{2,3},{3,2},{4,5},{5,4},{6,7},{7,6},{8,9},{9,8},{10,11... | collective-permute-start | bytes 786440 | tf_op jit(solution)/shard_map/ppermute | solution.py:540
  2.5 10.9 %copy-start.4 = (bf16[2,32,512]{2,1,0:T(8,128)(2,1)S(1)}, bf16[2,32,512]{2,1,0:T(8,128)(2,1)}, u32[]{:S(2)}) copy-start(bf16[2,32,512]{2,1,0:T(8,128)(2,1)} %get-tuple-element.30) | copy-start | bytes 196612
  2.5 11.5 %copy-start.3 = (bf16[2,32,512]{2,1,0:T(8,128)(2,1)S(1)}, bf16[2,32,512]{2,1,0:T(8,128)(2,1)}, u32[]{:S(2)}) copy-start(bf16[2,32,512]{2,1,0:T(8,128)(2,1)} %get-tuple-element.31) | copy-start | bytes 196612
  5.0 15.9 %all-to-all-start = ((bf16[16,32,256]{2,1,0:T(8,128)(2,1)}), bf16[16,32,256]{2,1,0:T(8,128)(2,1)S(1)}, u32[]{:S(2)}, u32[]{:S(2)}) async-start(bf16[16,32,256]{2,1,0:T(8,128)(2,1)} %bitcast.28), calls=%async_computation | async-start | bytes 524288 | tf_op jit(solution)/shard_map/all_to_all | solution.py:533
  13.3 9.9 %collective-permute-start.1 = (bf16[2,32,512]{2,1,0:T(8,128)(2,1)S(1)}, bf16[2,32,512]{2,1,0:T(8,128)(2,1)}, u32[]{:S(2)}, u32[]{:S(2)}) collective-permute-start(bf16[2,32,512]{2,1,0:T(8,128)(2,1)S(1)} %copy-done.4), channel_id=1, source_target_pairs={{0,2},{4,6},{8,10},{12,14},{16,18},{20,22},{24,26},{28,30},{2,0},{... | collective-permute-start | bytes 196616 | tf_op jit(solution)/shard_map/ppermute | solution.py:546
  14.0 9.3 %collective-permute-start.2 = (bf16[2,32,512]{2,1,0:T(8,128)(2,1)S(1)}, bf16[2,32,512]{2,1,0:T(8,128)(2,1)}, u32[]{:S(2)}, u32[]{:S(2)}) collective-permute-start(bf16[2,32,512]{2,1,0:T(8,128)(2,1)S(1)} %copy-done.3), channel_id=1, source_target_pairs={{2,4},{6,8},{10,12},{14,16},{18,20},{22,24},{26,28},{4,2},{8,6},{1... | collective-permute-start | bytes 196616 | tf_op jit(solution)/shard_map/ppermute | solution.py:546
  23.2 11.8 %copy-start = (bf16[640,2048]{1,0:T(8,128)(2,1)S(1)}, bf16[640,2048]{1,0:T(8,128)(2,1)}, u32[]{:S(2)}) copy-start(bf16[640,2048]{1,0:T(8,128)(2,1)} %refs_0_.1) | copy-start | bytes 7864324
  23.2 11.8 %copy-start.1 = (s32[128]{0:T(128)S(1)}, s32[128]{0:T(128)}, u32[]{:S(2)}) copy-start(s32[128]{0:T(128)} %param.15) | copy-start | bytes 1540
  23.3 11.8 %copy-start.2 = (s32[128]{0:T(128)S(1)}, s32[128]{0:T(128)}, u32[]{:S(2)}) copy-start(s32[128]{0:T(128)} %param.14) | copy-start | bytes 1540
  23.3 11.7 %all-to-all-start.1 = ((bf16[16,32,256]{2,1,0:T(8,128)(2,1)}), bf16[16,32,256]{2,1,0:T(8,128)(2,1)S(1)}, u32[]{:S(2)}, u32[]{:S(2)}) async-start(bf16[16,32,256]{2,1,0:T(8,128)(2,1)} %bitcast.29), calls=%async_computation.1 | async-start | bytes 524288 | tf_op jit(solution)/shard_map/all_to_all | solution.py:533
  36.1 1.3 %collective-permute-start.3 = (bf16[2,2,64,128]{3,2,1,0:T(8,128)(2,1)S(1)}, bf16[2,2,64,128]{3,2,1,0:T(8,128)(2,1)S(1)}, u32[]{:S(2)}, u32[]{:S(2)}) collective-permute-start(bf16[2,2,64,128]{3,2,1,0:T(8,128)(2,1)S(1)} %get-tuple-element.40), channel_id=1, source_target_pairs={{0,1},{1,0},{2,3},{3,2},{4,5},{5,4},{6,7},{7,6},{8,9},{9,8},{10,11... | collective-permute-start | bytes 196616 | tf_op jit(solution)/shard_map/ppermute | solution.py:540

commit v6 on v5

--- a/solution.py
+++ b/solution.py
@@ -193,18 +193,15 @@
         sides = ins[: len(rims)]
         family_ref, cos_ref, sin_ref, inner_ref, w_ref = ins[len(rims) :]
         (out_hbm,) = outs
-        out_ref, e_ref, wr_ref, shift_ref, sems = rest
+        out_ref, e_ref, shift_ref, sems = rest
         eye = identity(boxes)
-        wr_ref[:rim] = w_ref[:rim]
-        wr_ref[rim:] = w_ref[rows - rim :]
         for r in range(2):
-            for side, (n, low, high) in enumerate(spans):
-                e_ref[r * boxes : (r + 1) * boxes, side * rim : (side + 1) * rim] = nt(
-                    eye, sides[n][r, low:high, :]
-                ).astype(bf16)
+            part = slice(r * boxes, (r + 1) * boxes)
+            before, after = (nt(eye, sides[n][r, low:high, :]).astype(bf16) for n, low, high in spans)
+            e_ref[part] = jnp.concatenate([before, inner_ref[part], after], axis=1)
         for step in range(kpg // width):
             cols = slice(step * width, (step + 1) * width)
-            y = nn(inner_ref[...], w_ref[rim : rows - rim, cols]) + nn(e_ref[...], wr_ref[:, cols])
+            y = nn(e_ref[...], w_ref[:, cols])
             yr, yi, c, s = y[:boxes], y[boxes:], cos_ref[:, cols], sin_ref[:, cols]
             for r, value in enumerate((yr * c - yi * s, yr * s + yi * c)):
                 high = value.astype(bf16)
@@ -241,8 +238,7 @@
         "rise",
         scratch=[
             pltpu.VMEM(shape, bf16),
-            pltpu.VMEM((2 * boxes, 2 * rim), bf16),
-            pltpu.VMEM((2 * rim, kpg), bf16),
+            pltpu.VMEM((2 * boxes, rows), bf16),
             pltpu.VMEM((2, 2 * boxes, kpg), bf16),
             pltpu.SemaphoreType.DMA((2,)),
         ],
@@ -250,7 +246,7 @@
     )[0]
 
 
-def operators_of_lists(sources, offsets, counts, table, order):
+def operators_of_lists(sources, offsets, counts, table, order, back):
     slots, boxes = offsets.shape
     operators, _, half = table.shape
     lanes = 2 * half
@@ -266,7 +262,7 @@
             moved = jnp.where(home == index, src + (n - index) * family, moved)
         off = jnp.where(iota((slots, boxes), 0) < cnt_in()[...], off_in()[...], -1)
         src, off = (
-            jnp.concatenate([x.T[index * family : (index + 1) * family] for index in order], axis=0)
+            jnp.concatenate([x.T[index * family : (index + 1) * family] for index in back], axis=0)
             for x in (moved, off)
         )
         size = slots * CHUNK
@@ -570,7 +566,7 @@
     kpg = interp_weights.shape[1]
     mine = kpg // peers
     packed = mine == LANES and total % CHUNK == 0
-    order = ring(peers) if packed else None
+    order, back = (ring(peers), ring(peers)) if packed else (None, None)
     parent, octant = child_parent[None, :], child_octant[None, :]
 
     if groups == 2:
@@ -589,11 +585,11 @@
     if packed:
         regrouped = regroup(pattern, order)
         coef, sources = operators_of_lists(
-            parent_sources.T, parent_offsets.T, parent_counts[None, :], jnp.swapaxes(table, 0, 1), order
+            parent_sources.T, parent_offsets.T, parent_counts[None, :], jnp.swapaxes(table, 0, 1), order, back
         )
         far = parent_sums(regrouped, sources, coef, parent_sources.shape[1])
         far, lead, trail = lax.optimization_barrier((far, lead, trail))
-        returned = regroup(far, order)
+        returned = regroup(far, back)
     else:
         regrouped = lax.all_to_all(pattern, "box", split_axis=2, concat_axis=1, tiled=True)
         far = plain_translate(
@@ -613,7 +609,7 @@
         shift_phase,
     )
     returned, nearby = lax.optimization_barrier((returned, nearby))
-    lowered, terms = lower(returned, parent, octant, phases, interp_weights, parents, rim, order)
+    lowered, terms = lower(returned, parent, octant, phases, interp_weights, parents, rim, back)
     if groups == 2:
         got = shift(terms, "samp", 1)
         start_terms, end_terms = (got, 1), (got, 0)

time: 38.7 us -> 38.6 us (level)
  no operation moved by 1% of the time
where the time goes in v6:
time: 38.6 us; the launch traced here: 38.1 us
  starting transfers between devices  16.9 us (44%)
  Pallas kernels  16.4 us (42%)
  waiting for transfers between devices  4.63 us (12%)
    pallas_call x8, Pallas kernels, call(): pl.pallas_call(kernel, out_shape=[jax.ShapeDtypeStruct(shape, dtype) if p...  16.4 us
    all_to_all x2, starting transfers between devices, regroup(): lax.all_to_all(value, 'box', split_axis=0, concat_axis=0, tiled=True, axi...  14.5 us
    all_to_all x2, waiting for transfers between devices, regroup(): lax.all_to_all(value, 'box', split_axis=0, concat_axis=0, tiled=True, axi...  4.13 us
    ppermute x2, starting transfers between devices, exchange(): return lax.ppermute(value, axis, pairs + [(j, i) for i, j in pairs])  1.9 us
  transfers between devices with their start and end apart: 6, of which 3 were waited for; matrix products, arithmetic and copies ran while one was open for 0% of the time, Pallas kernels for 32%

profile of v6, /device:TPU:0, one launch (start us, length us, event | category | flops | bytes accessed | tf_op | source)
XLA Modules:
  0.0 38.1 jit_solution(3176045055342795630)
XLA Ops:
  0.0 0.5 %collective-permute-start = (bf16[2,512,128]{2,1,0:T(8,128)(2,1)}, bf16[2,512,128]{2,1,0:T(8,128)(2,1)S(1)}, u32[]{:S(2)}, u32[]{:S(2)}) collective-permute-start(bf16[2,512,128]{2,1,0:T(8,128)(2,1)} %bitcast.30), channel_id=1, source_target_pairs={{0,1},{1,0},{2,3},{3,2},{4,5},{5,4},{6,7},{7,6},{8,9},{9,8},{10,11... | collective-permute-start | bytes 786440 | tf_op jit(solution)/shard_map/ppermute | solution.py:536
  0.5 2.0 %prepare.1 = (f32[128,2048]{1,0:T(8,128)S(1)}, f32[128,2048]{1,0:T(8,128)S(1)}, bf16[256,512]{1,0:T(8,128)(2,1)S(1)}, bf16[32,256]{1,0:T(8,128)(2,1)S(1)}, bf16[...) custom-call(bf16[2,512,128]{2,1,0:T(8,128)(2,1)} %bitcast.31, ...), custom_call_target="tpu_custom_call" | custom-call | flops 1048576 | bytes 1048576 | tf_op jit(solution)/shard_map/prepare/pallas_call | solution.py:51
  2.5 0.0 collective-permute-done.refs_0_
  2.5 0.0 copy-start.4
  2.5 0.0 copy-start.3
  2.5 2.4 %rise.1 = bf16[512,256]{1,0:T(8,128)(2,1)} custom-call(bf16[2,512,128]{2,1,0:T(8,128)(2,1)S(1)} %collective-permute-done.refs_0_, bf16[32,256]{1,0:T(8,128)(2,1)S(1)} %get-tuple-element.23.refs_1_, f32[128,2048]{1,0:T(8,128)S(1)} %get-tuple-element.24.refs_2_, f32[128,2048]{1,0:T(8,128)S(1)} %get-tuple-element.25.refs_3_, ...), custom_call_target="tpu_custom_call" | custom-call | flops 671088640 | bytes 1048576 | tf_op jit(solution)/shard_map/rise/pallas_call | solution.py:51
  4.9 8.3 %all-to-all-start = ((bf16[16,32,256]{2,1,0:T(8,128)(2,1)}), bf16[16,32,256]{2,1,0:T(8,128)(2,1)S(1)}, u32[]{:S(2)}, u32[]{:S(2)}) async-start(bf16[16,32,256]{2,1,0:T(8,128)(2,1)} %bitcast.28), calls=%async_computation | async-start | bytes 524288 | tf_op jit(solution)/shard_map/all_to_all | solution.py:529
  13.2 0.0 copy-done.4
  13.2 0.6 %collective-permute-start.1 = (bf16[2,32,512]{2,1,0:T(8,128)(2,1)S(1)}, bf16[2,32,512]{2,1,0:T(8,128)(2,1)}, u32[]{:S(2)}, u32[]{:S(2)}) collective-permute-start(bf16[2,32,512]{2,1,0:T(8,128)(2,1)S(1)} %copy-done.4), channel_id=1, source_target_pairs={{0,2},{4,6},{8,10},{12,14},{16,18},{20,22},{24,26},{28,30},{2,0},{... | collective-permute-start | bytes 196616 | tf_op jit(solution)/shard_map/ppermute | solution.py:542
  13.9 0.0 copy-done.3
  13.9 1.3 %collective-permute-start.2 = (bf16[2,32,512]{2,1,0:T(8,128)(2,1)S(1)}, bf16[2,32,512]{2,1,0:T(8,128)(2,1)}, u32[]{:S(2)}, u32[]{:S(2)}) collective-permute-start(bf16[2,32,512]{2,1,0:T(8,128)(2,1)S(1)} %copy-done.3), channel_id=1, source_target_pairs={{2,4},{6,8},{10,12},{14,16},{18,20},{22,24},{26,28},{4,2},{8,6},{1... | collective-permute-start | bytes 196616 | tf_op jit(solution)/shard_map/ppermute | solution.py:542
  15.2 2.6 %operators_of_lists.1 = (bf16[4096,256]{1,0:T(8,128)(2,1)S(1)}, s16[4096,128]{1,0:T(8,128)(2,1)S(1)}) custom-call(s32[8,512]{1,0:T(8,128)} %bitcast.35, s32[8,512]{1,0:T(8,128)} %bitcast.36, s32[1,512]{1,0:T(1,128)} %bitcast.39, bf16[316,2,128]{2,1,0:T(2,128)(2,1)} %bitcast.34), custom_call_target="tpu_custom_call" | custom-call | flops 662700032 | bytes 1048576 | tf_op jit(solution)/shard_map/operators_of_lists/pallas_call | solution.py:51
  17.8 3.0 %all-to-all-done = bf16[16,32,256]{2,1,0:T(8,128)(2,1)S(1)} async-done(((bf16[16,32,256]{2,1,0:T(8,128)(2,1)}), bf16[16,32,256]{2,1,0:T(8,128)(2,1)S(1)}, u32[]{:S(2)}, u32[]{:S(2)}) %all-to-all-start) | async-done | bytes 262176 | tf_op jit(solution)/shard_map/all_to_all | solution.py:529
  20.8 2.3 %parent_sums.1 = bf16[512,256]{1,0:T(8,128)(2,1)} custom-call(bf16[512,256]{1,0:T(8,128)(2,1)S(1)} %bitcast.23, s16[4096,128]{1,0:T(8,128)(2,1)S(1)} %get-tuple-element.28.refs_1_, bf16[4096,256]{1,0:T(8,128)(2,1)S(1)} %get-tuple-element.29.refs_2_), custom_call_target="tpu_custom_call" | custom-call | flops 1073741824 | bytes 1048576 | tf_op jit(solution)/shard_map/parent_sums/pallas_call | solution.py:51
  23.1 0.0 copy-start
  23.1 0.0 copy-start.1
  23.2 0.0 copy-start.2
  23.2 0.0 collective-permute-done.1.refs_1_
  23.2 0.0 collective-permute-done.2.refs_2_
  23.2 6.2 %all-to-all-start.1 = ((bf16[16,32,256]{2,1,0:T(8,128)(2,1)}), bf16[16,32,256]{2,1,0:T(8,128)(2,1)S(1)}, u32[]{:S(2)}, u32[]{:S(2)}) async-start(bf16[16,32,256]{2,1,0:T(8,128)(2,1)} %bitcast.29), calls=%async_computation.1 | async-start | bytes 524288 | tf_op jit(solution)/shard_map/all_to_all | solution.py:529
  29.4 4.4 %near_sums.1 = (f32[2,512,128]{2,1,0:T(8,128)S(1)}, f32[16,2048]{1,0:T(8,128)S(1)}) custom-call(bf16[2,512,128]{2,1,0:T(8,128)(2,1)} %bitcast.32, bf16[2,32,512]{2,1,0:T(8,128)(2,1)} %collective-permute-done.1.refs_1_, bf16[2,32,512]{2,1,0:T(8,128)(2,1)} %collective-permute-done.2.refs_2_, s32[8,128]{1,0:T(8,128)} %bitcast.37, s32[8,128]{1,0:T(8,128)} %bitcast.38, ...), custom_call_target="tpu_custom_call" | custom-call | flops 1199570944 | bytes 1048576 | tf_op jit(solution)/shard_map/near_sums/pallas_call | solution.py:51
  33.8 1.1 %all-to-all-done.1 = bf16[16,32,256]{2,1,0:T(8,128)(2,1)S(1)} async-done(((bf16[16,32,256]{2,1,0:T(8,128)(2,1)}), bf16[16,32,256]{2,1,0:T(8,128)(2,1)S(1)}, u32[]{:S(2)}, u32[]{:S(2)}) %all-to-all-start.1) | async-done | bytes 262176 | tf_op jit(solution)/shard_map/all_to_all | solution.py:529
  34.9 0.0 copy-done
  34.9 0.0 copy-done.1
  34.9 0.0 copy-done.2
  35.0 1.1 %lower.1 = (bf16[256,2048]{1,0:T(8,128)(2,1)S(1)}, bf16[2,2,64,128]{3,2,1,0:T(8,128)(2,1)S(1)}) custom-call(bf16[512,256]{1,0:T(8,128)(2,1)S(1)} %bitcast.22, s32[1,128]{1,0:T(1,128)S(1)} %bitcast.27, s32[1,128]{1,0:T(1,128)S(1)} %bitcast.25, f32[16,2048]{1,0:T(8,128)S(1)} %get-tuple-element.37.refs_3_, bf16[640,2048]{1,0:T(8,128)(2,1)S(1)} %copy-done), custom_call_target="tpu_custom_call" | custom-call | flops 134217728 | bytes 1048576 | tf_op jit(solution)/shard_map/lower/pallas_call | solution.py:51
  36.0 0.1 collective-permute-start.3
  36.1 0.7 %anterpolate.1.refs_0_ = f32[2,512,128]{2,1,0:T(8,128)S(1)} custom-call(bf16[640,2048]{1,0:T(8,128)(2,1)S(1)} %copy-done, bf16[256,2048]{1,0:T(8,128)(2,1)S(1)} %get-tuple-element.38.refs_1_, f32[2,512,128]{2,1,0:T(8,128)S(1)} %get-tuple-element.39.refs_2_), custom_call_target="tpu_custom_call" | custom-call | flops 536870912 | bytes 1048576 | tf_op jit(solution)/shard_map/anterpolate/pallas_call | solution.py:51
  36.9 0.5 %collective-permute-done.3.refs_1_ = bf16[2,2,64,128]{3,2,1,0:T(8,128)(2,1)S(1)} collective-permute-done((bf16[2,2,64,128]{3,2,1,0:T(8,128)(2,1)S(1)}, bf16[2,2,64,128]{3,2,1,0:T(8,128)(2,1)S(1)}, u32[]{:S(2)}, u32[]{:S(2)}) %collective-permute-start.3) | collective-permute-done | bytes 65568 | tf_op jit(solution)/shard_map/ppermute | solution.py:536
  37.4 0.7 %finish.1 = bf16[2,512,128]{2,1,0:T(8,128)(2,1)} custom-call(f32[2,512,128]{2,1,0:T(8,128)S(1)} %anterpolate.1.refs_0_, bf16[2,2,64,128]{3,2,1,0:T(8,128)(2,1)S(1)} %collective-permute-done.3.refs_1_), custom_call_target="tpu_custom_call" | custom-call | flops 1048576 | bytes 1048576 | tf_op jit(solution)/shard_map/finish/pallas_call | solution.py:51
Async XLA Ops:
  0.0 2.5 %collective-permute-start = (bf16[2,512,128]{2,1,0:T(8,128)(2,1)}, bf16[2,512,128]{2,1,0:T(8,128)(2,1)S(1)}, u32[]{:S(2)}, u32[]{:S(2)}) collective-permute-start(bf16[2,512,128]{2,1,0:T(8,128)(2,1)} %bitcast.30), channel_id=1, source_target_pairs={{0,1},{1,0},{2,3},{3,2},{4,5},{5,4},{6,7},{7,6},{8,9},{9,8},{10,11... | collective-permute-start | bytes 786440 | tf_op jit(solution)/shard_map/ppermute | solution.py:536
  2.5 10.8 %copy-start.4 = (bf16[2,32,512]{2,1,0:T(8,128)(2,1)S(1)}, bf16[2,32,512]{2,1,0:T(8,128)(2,1)}, u32[]{:S(2)}) copy-start(bf16[2,32,512]{2,1,0:T(8,128)(2,1)} %get-tuple-element.30) | copy-start | bytes 196612
  2.5 11.4 %copy-start.3 = (bf16[2,32,512]{2,1,0:T(8,128)(2,1)S(1)}, bf16[2,32,512]{2,1,0:T(8,128)(2,1)}, u32[]{:S(2)}) copy-start(bf16[2,32,512]{2,1,0:T(8,128)(2,1)} %get-tuple-element.31) | copy-start | bytes 196612
  4.9 15.9 %all-to-all-start = ((bf16[16,32,256]{2,1,0:T(8,128)(2,1)}), bf16[16,32,256]{2,1,0:T(8,128)(2,1)S(1)}, u32[]{:S(2)}, u32[]{:S(2)}) async-start(bf16[16,32,256]{2,1,0:T(8,128)(2,1)} %bitcast.28), calls=%async_computation | async-start | bytes 524288 | tf_op jit(solution)/shard_map/all_to_all | solution.py:529
  13.2 9.9 %collective-permute-start.1 = (bf16[2,32,512]{2,1,0:T(8,128)(2,1)S(1)}, bf16[2,32,512]{2,1,0:T(8,128)(2,1)}, u32[]{:S(2)}, u32[]{:S(2)}) collective-permute-start(bf16[2,32,512]{2,1,0:T(8,128)(2,1)S(1)} %copy-done.4), channel_id=1, source_target_pairs={{0,2},{4,6},{8,10},{12,14},{16,18},{20,22},{24,26},{28,30},{2,0},{... | collective-permute-start | bytes 196616 | tf_op jit(solution)/shard_map/ppermute | solution.py:542
  13.9 9.3 %collective-permute-start.2 = (bf16[2,32,512]{2,1,0:T(8,128)(2,1)S(1)}, bf16[2,32,512]{2,1,0:T(8,128)(2,1)}, u32[]{:S(2)}, u32[]{:S(2)}) collective-permute-start(bf16[2,32,512]{2,1,0:T(8,128)(2,1)S(1)} %copy-done.3), channel_id=1, source_target_pairs={{2,4},{6,8},{10,12},{14,16},{18,20},{22,24},{26,28},{4,2},{8,6},{1... | collective-permute-start | bytes 196616 | tf_op jit(solution)/shard_map/ppermute | solution.py:542
  23.1 11.8 %copy-start = (bf16[640,2048]{1,0:T(8,128)(2,1)S(1)}, bf16[640,2048]{1,0:T(8,128)(2,1)}, u32[]{:S(2)}) copy-start(bf16[640,2048]{1,0:T(8,128)(2,1)} %refs_0_.1) | copy-start | bytes 7864324
  23.1 11.8 %copy-start.1 = (s32[128]{0:T(128)S(1)}, s32[128]{0:T(128)}, u32[]{:S(2)}) copy-start(s32[128]{0:T(128)} %param.15) | copy-start | bytes 1540
  23.2 11.8 %copy-start.2 = (s32[128]{0:T(128)S(1)}, s32[128]{0:T(128)}, u32[]{:S(2)}) copy-start(s32[128]{0:T(128)} %param.14) | copy-start | bytes 1540
  23.2 11.7 %all-to-all-start.1 = ((bf16[16,32,256]{2,1,0:T(8,128)(2,1)}), bf16[16,32,256]{2,1,0:T(8,128)(2,1)S(1)}, u32[]{:S(2)}, u32[]{:S(2)}) async-start(bf16[16,32,256]{2,1,0:T(8,128)(2,1)} %bitcast.29), calls=%async_computation.1 | async-start | bytes 524288 | tf_op jit(solution)/shard_map/all_to_all | solution.py:529
  36.0 1.3 %collective-permute-start.3 = (bf16[2,2,64,128]{3,2,1,0:T(8,128)(2,1)S(1)}, bf16[2,2,64,128]{3,2,1,0:T(8,128)(2,1)S(1)}, u32[]{:S(2)}, u32[]{:S(2)}) collective-permute-start(bf16[2,2,64,128]{3,2,1,0:T(8,128)(2,1)S(1)} %get-tuple-element.40), channel_id=1, source_target_pairs={{0,1},{1,0},{2,3},{3,2},{4,5},{5,4},{6,7},{7,6},{8,9},{9,8},{10,11... | collective-permute-start | bytes 196616 | tf_op jit(solution)/shard_map/ppermute | solution.py:536

commit v7 on v6

--- a/solution.py
+++ b/solution.py
@@ -185,7 +185,7 @@
     boxes, kpg = cosine.shape
     rows = weights.shape[0]
     rim = spans[0][2] - spans[0][1]
-    width = 256
+    width = 512
     packed = order is not None
     shape = (kpg // LANES * parents, 2 * LANES) if packed else (2, parents, kpg)
 

time: 38.6 us -> 38.6 us (level)
  no operation moved by 1% of the time
where the time goes in v7:
time: 38.6 us; the launch traced here: 38.1 us
  starting transfers between devices  16.9 us (44%)
  Pallas kernels  16.4 us (42%)
  waiting for transfers between devices  4.63 us (12%)
    pallas_call x8, Pallas kernels, call(): pl.pallas_call(kernel, out_shape=[jax.ShapeDtypeStruct(shape, dtype) if p...  16.4 us
    all_to_all x2, starting transfers between devices, regroup(): lax.all_to_all(value, 'box', split_axis=0, concat_axis=0, tiled=True, axi...  14.5 us
    all_to_all x2, waiting for transfers between devices, regroup(): lax.all_to_all(value, 'box', split_axis=0, concat_axis=0, tiled=True, axi...  4.13 us
    ppermute x2, starting transfers between devices, exchange(): return lax.ppermute(value, axis, pairs + [(j, i) for i, j in pairs])  1.9 us
  transfers between devices with their start and end apart: 6, of which 3 were waited for; matrix products, arithmetic and copies ran while one was open for 0% of the time, Pallas kernels for 32%

profile of v7, /device:TPU:0, one launch (start us, length us, event | category | flops | bytes accessed | tf_op | source)
XLA Modules:
  0.0 38.1 jit_solution(9519606313566073559)
XLA Ops:
  0.0 0.5 %collective-permute-start = (bf16[2,512,128]{2,1,0:T(8,128)(2,1)}, bf16[2,512,128]{2,1,0:T(8,128)(2,1)S(1)}, u32[]{:S(2)}, u32[]{:S(2)}) collective-permute-start(bf16[2,512,128]{2,1,0:T(8,128)(2,1)} %bitcast.30), channel_id=1, source_target_pairs={{0,1},{1,0},{2,3},{3,2},{4,5},{5,4},{6,7},{7,6},{8,9},{9,8},{10,11... | collective-permute-start | bytes 786440 | tf_op jit(solution)/shard_map/ppermute | solution.py:536
  0.5 2.0 %prepare.1 = (f32[128,2048]{1,0:T(8,128)S(1)}, f32[128,2048]{1,0:T(8,128)S(1)}, bf16[256,512]{1,0:T(8,128)(2,1)S(1)}, bf16[32,256]{1,0:T(8,128)(2,1)S(1)}, bf16[...) custom-call(bf16[2,512,128]{2,1,0:T(8,128)(2,1)} %bitcast.31, ...), custom_call_target="tpu_custom_call" | custom-call | flops 1048576 | bytes 1048576 | tf_op jit(solution)/shard_map/prepare/pallas_call | solution.py:51
  2.5 0.0 collective-permute-done.refs_0_
  2.5 0.0 copy-start.4
  2.5 0.0 copy-start.3
  2.5 2.4 %rise.1 = bf16[512,256]{1,0:T(8,128)(2,1)} custom-call(bf16[2,512,128]{2,1,0:T(8,128)(2,1)S(1)} %collective-permute-done.refs_0_, bf16[32,256]{1,0:T(8,128)(2,1)S(1)} %get-tuple-element.23.refs_1_, f32[128,2048]{1,0:T(8,128)S(1)} %get-tuple-element.24.refs_2_, f32[128,2048]{1,0:T(8,128)S(1)} %get-tuple-element.25.refs_3_, ...), custom_call_target="tpu_custom_call" | custom-call | flops 671088640 | bytes 1048576 | tf_op jit(solution)/shard_map/rise/pallas_call | solution.py:51
  4.9 8.3 %all-to-all-start = ((bf16[16,32,256]{2,1,0:T(8,128)(2,1)}), bf16[16,32,256]{2,1,0:T(8,128)(2,1)S(1)}, u32[]{:S(2)}, u32[]{:S(2)}) async-start(bf16[16,32,256]{2,1,0:T(8,128)(2,1)} %bitcast.28), calls=%async_computation | async-start | bytes 524288 | tf_op jit(solution)/shard_map/all_to_all | solution.py:529
  13.2 0.0 copy-done.4
  13.2 0.6 %collective-permute-start.1 = (bf16[2,32,512]{2,1,0:T(8,128)(2,1)S(1)}, bf16[2,32,512]{2,1,0:T(8,128)(2,1)}, u32[]{:S(2)}, u32[]{:S(2)}) collective-permute-start(bf16[2,32,512]{2,1,0:T(8,128)(2,1)S(1)} %copy-done.4), channel_id=1, source_target_pairs={{0,2},{4,6},{8,10},{12,14},{16,18},{20,22},{24,26},{28,30},{2,0},{... | collective-permute-start | bytes 196616 | tf_op jit(solution)/shard_map/ppermute | solution.py:542
  13.9 0.0 copy-done.3
  13.9 1.3 %collective-permute-start.2 = (bf16[2,32,512]{2,1,0:T(8,128)(2,1)S(1)}, bf16[2,32,512]{2,1,0:T(8,128)(2,1)}, u32[]{:S(2)}, u32[]{:S(2)}) collective-permute-start(bf16[2,32,512]{2,1,0:T(8,128)(2,1)S(1)} %copy-done.3), channel_id=1, source_target_pairs={{2,4},{6,8},{10,12},{14,16},{18,20},{22,24},{26,28},{4,2},{8,6},{1... | collective-permute-start | bytes 196616 | tf_op jit(solution)/shard_map/ppermute | solution.py:542
  15.1 2.6 %operators_of_lists.1 = (bf16[4096,256]{1,0:T(8,128)(2,1)S(1)}, s16[4096,128]{1,0:T(8,128)(2,1)S(1)}) custom-call(s32[8,512]{1,0:T(8,128)} %bitcast.35, s32[8,512]{1,0:T(8,128)} %bitcast.36, s32[1,512]{1,0:T(1,128)} %bitcast.39, bf16[316,2,128]{2,1,0:T(2,128)(2,1)} %bitcast.34), custom_call_target="tpu_custom_call" | custom-call | flops 662700032 | bytes 1048576 | tf_op jit(solution)/shard_map/operators_of_lists/pallas_call | solution.py:51
  17.8 3.0 %all-to-all-done = bf16[16,32,256]{2,1,0:T(8,128)(2,1)S(1)} async-done(((bf16[16,32,256]{2,1,0:T(8,128)(2,1)}), bf16[16,32,256]{2,1,0:T(8,128)(2,1)S(1)}, u32[]{:S(2)}, u32[]{:S(2)}) %all-to-all-start) | async-done | bytes 262176 | tf_op jit(solution)/shard_map/all_to_all | solution.py:529
  20.8 2.3 %parent_sums.1 = bf16[512,256]{1,0:T(8,128)(2,1)} custom-call(bf16[512,256]{1,0:T(8,128)(2,1)S(1)} %bitcast.23, s16[4096,128]{1,0:T(8,128)(2,1)S(1)} %get-tuple-element.28.refs_1_, bf16[4096,256]{1,0:T(8,128)(2,1)S(1)} %get-tuple-element.29.refs_2_), custom_call_target="tpu_custom_call" | custom-call | flops 1073741824 | bytes 1048576 | tf_op jit(solution)/shard_map/parent_sums/pallas_call | solution.py:51
  23.1 0.0 copy-start
  23.1 0.0 copy-start.1
  23.2 0.0 copy-start.2
  23.2 0.0 collective-permute-done.1.refs_1_
  23.2 0.0 collective-permute-done.2.refs_2_
  23.2 6.2 %all-to-all-start.1 = ((bf16[16,32,256]{2,1,0:T(8,128)(2,1)}), bf16[16,32,256]{2,1,0:T(8,128)(2,1)S(1)}, u32[]{:S(2)}, u32[]{:S(2)}) async-start(bf16[16,32,256]{2,1,0:T(8,128)(2,1)} %bitcast.29), calls=%async_computation.1 | async-start | bytes 524288 | tf_op jit(solution)/shard_map/all_to_all | solution.py:529
  29.3 4.4 %near_sums.1 = (f32[2,512,128]{2,1,0:T(8,128)S(1)}, f32[16,2048]{1,0:T(8,128)S(1)}) custom-call(bf16[2,512,128]{2,1,0:T(8,128)(2,1)} %bitcast.32, bf16[2,32,512]{2,1,0:T(8,128)(2,1)} %collective-permute-done.1.refs_1_, bf16[2,32,512]{2,1,0:T(8,128)(2,1)} %collective-permute-done.2.refs_2_, s32[8,128]{1,0:T(8,128)} %bitcast.37, s32[8,128]{1,0:T(8,128)} %bitcast.38, ...), custom_call_target="tpu_custom_call" | custom-call | flops 1199570944 | bytes 1048576 | tf_op jit(solution)/shard_map/near_sums/pallas_call | solution.py:51
  33.8 1.1 %all-to-all-done.1 = bf16[16,32,256]{2,1,0:T(8,128)(2,1)S(1)} async-done(((bf16[16,32,256]{2,1,0:T(8,128)(2,1)}), bf16[16,32,256]{2,1,0:T(8,128)(2,1)S(1)}, u32[]{:S(2)}, u32[]{:S(2)}) %all-to-all-start.1) | async-done | bytes 262176 | tf_op jit(solution)/shard_map/all_to_all | solution.py:529
  34.9 0.0 copy-done
  34.9 0.0 copy-done.1
  34.9 0.0 copy-done.2
  34.9 1.1 %lower.1 = (bf16[256,2048]{1,0:T(8,128)(2,1)S(1)}, bf16[2,2,64,128]{3,2,1,0:T(8,128)(2,1)S(1)}) custom-call(bf16[512,256]{1,0:T(8,128)(2,1)S(1)} %bitcast.22, s32[1,128]{1,0:T(1,128)S(1)} %bitcast.27, s32[1,128]{1,0:T(1,128)S(1)} %bitcast.25, f32[16,2048]{1,0:T(8,128)S(1)} %get-tuple-element.37.refs_3_, bf16[640,2048]{1,0:T(8,128)(2,1)S(1)} %copy-done), custom_call_target="tpu_custom_call" | custom-call | flops 134217728 | bytes 1048576 | tf_op jit(solution)/shard_map/lower/pallas_call | solution.py:51
  36.0 0.1 collective-permute-start.3
  36.1 0.7 %anterpolate.1.refs_0_ = f32[2,512,128]{2,1,0:T(8,128)S(1)} custom-call(bf16[640,2048]{1,0:T(8,128)(2,1)S(1)} %copy-done, bf16[256,2048]{1,0:T(8,128)(2,1)S(1)} %get-tuple-element.38.refs_1_, f32[2,512,128]{2,1,0:T(8,128)S(1)} %get-tuple-element.39.refs_2_), custom_call_target="tpu_custom_call" | custom-call | flops 536870912 | bytes 1048576 | tf_op jit(solution)/shard_map/anterpolate/pallas_call | solution.py:51
  36.9 0.5 %collective-permute-done.3.refs_1_ = bf16[2,2,64,128]{3,2,1,0:T(8,128)(2,1)S(1)} collective-permute-done((bf16[2,2,64,128]{3,2,1,0:T(8,128)(2,1)S(1)}, bf16[2,2,64,128]{3,2,1,0:T(8,128)(2,1)S(1)}, u32[]{:S(2)}, u32[]{:S(2)}) %collective-permute-start.3) | collective-permute-done | bytes 65568 | tf_op jit(solution)/shard_map/ppermute | solution.py:536
  37.3 0.7 %finish.1 = bf16[2,512,128]{2,1,0:T(8,128)(2,1)} custom-call(f32[2,512,128]{2,1,0:T(8,128)S(1)} %anterpolate.1.refs_0_, bf16[2,2,64,128]{3,2,1,0:T(8,128)(2,1)S(1)} %collective-permute-done.3.refs_1_), custom_call_target="tpu_custom_call" | custom-call | flops 1048576 | bytes 1048576 | tf_op jit(solution)/shard_map/finish/pallas_call | solution.py:51
Async XLA Ops:
  0.0 2.5 %collective-permute-start = (bf16[2,512,128]{2,1,0:T(8,128)(2,1)}, bf16[2,512,128]{2,1,0:T(8,128)(2,1)S(1)}, u32[]{:S(2)}, u32[]{:S(2)}) collective-permute-start(bf16[2,512,128]{2,1,0:T(8,128)(2,1)} %bitcast.30), channel_id=1, source_target_pairs={{0,1},{1,0},{2,3},{3,2},{4,5},{5,4},{6,7},{7,6},{8,9},{9,8},{10,11... | collective-permute-start | bytes 786440 | tf_op jit(solution)/shard_map/ppermute | solution.py:536
  2.5 10.8 %copy-start.4 = (bf16[2,32,512]{2,1,0:T(8,128)(2,1)S(1)}, bf16[2,32,512]{2,1,0:T(8,128)(2,1)}, u32[]{:S(2)}) copy-start(bf16[2,32,512]{2,1,0:T(8,128)(2,1)} %get-tuple-element.30) | copy-start | bytes 196612
  2.5 11.4 %copy-start.3 = (bf16[2,32,512]{2,1,0:T(8,128)(2,1)S(1)}, bf16[2,32,512]{2,1,0:T(8,128)(2,1)}, u32[]{:S(2)}) copy-start(bf16[2,32,512]{2,1,0:T(8,128)(2,1)} %get-tuple-element.31) | copy-start | bytes 196612
  4.9 15.9 %all-to-all-start = ((bf16[16,32,256]{2,1,0:T(8,128)(2,1)}), bf16[16,32,256]{2,1,0:T(8,128)(2,1)S(1)}, u32[]{:S(2)}, u32[]{:S(2)}) async-start(bf16[16,32,256]{2,1,0:T(8,128)(2,1)} %bitcast.28), calls=%async_computation | async-start | bytes 524288 | tf_op jit(solution)/shard_map/all_to_all | solution.py:529
  13.2 9.9 %collective-permute-start.1 = (bf16[2,32,512]{2,1,0:T(8,128)(2,1)S(1)}, bf16[2,32,512]{2,1,0:T(8,128)(2,1)}, u32[]{:S(2)}, u32[]{:S(2)}) collective-permute-start(bf16[2,32,512]{2,1,0:T(8,128)(2,1)S(1)} %copy-done.4), channel_id=1, source_target_pairs={{0,2},{4,6},{8,10},{12,14},{16,18},{20,22},{24,26},{28,30},{2,0},{... | collective-permute-start | bytes 196616 | tf_op jit(solution)/shard_map/ppermute | solution.py:542
  13.9 9.3 %collective-permute-start.2 = (bf16[2,32,512]{2,1,0:T(8,128)(2,1)S(1)}, bf16[2,32,512]{2,1,0:T(8,128)(2,1)}, u32[]{:S(2)}, u32[]{:S(2)}) collective-permute-start(bf16[2,32,512]{2,1,0:T(8,128)(2,1)S(1)} %copy-done.3), channel_id=1, source_target_pairs={{2,4},{6,8},{10,12},{14,16},{18,20},{22,24},{26,28},{4,2},{8,6},{1... | collective-permute-start | bytes 196616 | tf_op jit(solution)/shard_map/ppermute | solution.py:542
  23.1 11.8 %copy-start = (bf16[640,2048]{1,0:T(8,128)(2,1)S(1)}, bf16[640,2048]{1,0:T(8,128)(2,1)}, u32[]{:S(2)}) copy-start(bf16[640,2048]{1,0:T(8,128)(2,1)} %refs_0_.1) | copy-start | bytes 7864324
  23.1 11.8 %copy-start.1 = (s32[128]{0:T(128)S(1)}, s32[128]{0:T(128)}, u32[]{:S(2)}) copy-start(s32[128]{0:T(128)} %param.15) | copy-start | bytes 1540
  23.2 11.8 %copy-start.2 = (s32[128]{0:T(128)S(1)}, s32[128]{0:T(128)}, u32[]{:S(2)}) copy-start(s32[128]{0:T(128)} %param.14) | copy-start | bytes 1540
  23.2 11.7 %all-to-all-start.1 = ((bf16[16,32,256]{2,1,0:T(8,128)(2,1)}), bf16[16,32,256]{2,1,0:T(8,128)(2,1)S(1)}, u32[]{:S(2)}, u32[]{:S(2)}) async-start(bf16[16,32,256]{2,1,0:T(8,128)(2,1)} %bitcast.29), calls=%async_computation.1 | async-start | bytes 524288 | tf_op jit(solution)/shard_map/all_to_all | solution.py:529
  36.0 1.3 %collective-permute-start.3 = (bf16[2,2,64,128]{3,2,1,0:T(8,128)(2,1)S(1)}, bf16[2,2,64,128]{3,2,1,0:T(8,128)(2,1)S(1)}, u32[]{:S(2)}, u32[]{:S(2)}) collective-permute-start(bf16[2,2,64,128]{3,2,1,0:T(8,128)(2,1)S(1)} %get-tuple-element.40), channel_id=1, source_target_pairs={{0,1},{1,0},{2,3},{3,2},{4,5},{5,4},{6,7},{7,6},{8,9},{9,8},{10,11... | collective-permute-start | bytes 196616 | tf_op jit(solution)/shard_map/ppermute | solution.py:536

commit v8 on v6

--- a/solution.py
+++ b/solution.py
@@ -416,17 +416,32 @@
     rim = start_terms[0].shape[-2]
     arrays = [start_terms[0]] if end_terms[0] is start_terms[0] else [start_terms[0], end_terms[0]]
 
+    spans = ((rim, kcg - 2 * rim), (0, rim), (kcg - rim, rim))
+
     def body(ins, outs, rest):
         sum_ref, start_ref, end_ref = ins[0], ins[1], ins[-1]
-        (out_ref,) = outs
+        (out_hbm,) = outs
+        out_ref, sems = rest
         start = start_ref[...] if start_terms[1] is None else start_ref[start_terms[1]]
         end = end_ref[...] if end_terms[1] is None else end_ref[end_terms[1]]
-        out_ref[:, rim : kcg - rim] = sum_ref[:, rim : kcg - rim].astype(bf16)
-        out_ref[:, :rim] = (sum_ref[:, :rim] + start.astype(f32)).astype(bf16)
-        out_ref[:, kcg - rim :] = (sum_ref[:, kcg - rim :] + end.astype(f32)).astype(bf16)
-
-    return call(
-        body, [partial, *arrays], [V] * (1 + len(arrays)), [(partial.shape, bf16, None)], "finish"
+        copies = []
+        for n, ((at, size), terms) in enumerate(zip(spans, (None, start, end))):
+            value = sum_ref[:, at : at + size]
+            value = value if terms is None else value + terms.astype(f32)
+            out_ref[:, at : at + size] = value.astype(bf16)
+            part = pl.ds(at, size)
+            copies.append(pltpu.make_async_copy(out_ref.at[:, part], out_hbm.at[:, part], sems.at[n]))
+            copies[-1].start()
+        for copy in copies:
+            copy.wait()
+
+    return call(
+        body,
+        [partial, *arrays],
+        [V] * (1 + len(arrays)),
+        [(partial.shape, bf16, H)],
+        "finish",
+        scratch=[pltpu.VMEM(partial.shape, bf16), pltpu.SemaphoreType.DMA((3,))],
     )[0]
 
 

time: 38.6 us -> 38.6 us (level)
  no operation moved by 1% of the time
where the time goes in v8:
time: 38.6 us; the launch traced here: 38.1 us
  starting transfers between devices  16.9 us (44%)
  Pallas kernels  16.4 us (42%)
  waiting for transfers between devices  4.63 us (12%)
    pallas_call x8, Pallas kernels, call(): pl.pallas_call(kernel, out_shape=[jax.ShapeDtypeStruct(shape, dtype) if p...  16.4 us
    all_to_all x2, starting transfers between devices, regroup(): lax.all_to_all(value, 'box', split_axis=0, concat_axis=0, tiled=True, axi...  14.5 us
    all_to_all x2, waiting for transfers between devices, regroup(): lax.all_to_all(value, 'box', split_axis=0, concat_axis=0, tiled=True, axi...  4.13 us
    ppermute x2, starting transfers between devices, exchange(): return lax.ppermute(value, axis, pairs + [(j, i) for i, j in pairs])  1.9 us
  transfers between devices with their start and end apart: 6, of which 3 were waited for; matrix products, arithmetic and copies ran while one was open for 0% of the time, Pallas kernels for 32%

profile of v8, /device:TPU:0, one launch (start us, length us, event | category | flops | bytes accessed | tf_op | source)
XLA Modules:
  0.0 38.1 jit_solution(5985059654734876366)
XLA Ops:
  0.0 0.5 %collective-permute-start = (bf16[2,512,128]{2,1,0:T(8,128)(2,1)}, bf16[2,512,128]{2,1,0:T(8,128)(2,1)S(1)}, u32[]{:S(2)}, u32[]{:S(2)}) collective-permute-start(bf16[2,512,128]{2,1,0:T(8,128)(2,1)} %bitcast.30), channel_id=1, source_target_pairs={{0,1},{1,0},{2,3},{3,2},{4,5},{5,4},{6,7},{7,6},{8,9},{9,8},{10,11... | collective-permute-start | bytes 786440 | tf_op jit(solution)/shard_map/ppermute | solution.py:551
  0.5 2.0 %prepare.1 = (f32[128,2048]{1,0:T(8,128)S(1)}, f32[128,2048]{1,0:T(8,128)S(1)}, bf16[256,512]{1,0:T(8,128)(2,1)S(1)}, bf16[32,256]{1,0:T(8,128)(2,1)S(1)}, bf16[...) custom-call(bf16[2,512,128]{2,1,0:T(8,128)(2,1)} %bitcast.31, ...), custom_call_target="tpu_custom_call" | custom-call | flops 1048576 | bytes 1048576 | tf_op jit(solution)/shard_map/prepare/pallas_call | solution.py:51
  2.5 0.0 collective-permute-done.refs_0_
  2.5 0.0 copy-start.4
  2.5 0.0 copy-start.3
  2.5 2.4 %rise.1 = bf16[512,256]{1,0:T(8,128)(2,1)} custom-call(bf16[2,512,128]{2,1,0:T(8,128)(2,1)S(1)} %collective-permute-done.refs_0_, bf16[32,256]{1,0:T(8,128)(2,1)S(1)} %get-tuple-element.23.refs_1_, f32[128,2048]{1,0:T(8,128)S(1)} %get-tuple-element.24.refs_2_, f32[128,2048]{1,0:T(8,128)S(1)} %get-tuple-element.25.refs_3_, ...), custom_call_target="tpu_custom_call" | custom-call | flops 671088640 | bytes 1048576 | tf_op jit(solution)/shard_map/rise/pallas_call | solution.py:51
  4.9 8.3 %all-to-all-start = ((bf16[16,32,256]{2,1,0:T(8,128)(2,1)}), bf16[16,32,256]{2,1,0:T(8,128)(2,1)S(1)}, u32[]{:S(2)}, u32[]{:S(2)}) async-start(bf16[16,32,256]{2,1,0:T(8,128)(2,1)} %bitcast.28), calls=%async_computation | async-start | bytes 524288 | tf_op jit(solution)/shard_map/all_to_all | solution.py:544
  13.2 0.0 copy-done.4
  13.2 0.6 %collective-permute-start.1 = (bf16[2,32,512]{2,1,0:T(8,128)(2,1)S(1)}, bf16[2,32,512]{2,1,0:T(8,128)(2,1)}, u32[]{:S(2)}, u32[]{:S(2)}) collective-permute-start(bf16[2,32,512]{2,1,0:T(8,128)(2,1)S(1)} %copy-done.4), channel_id=1, source_target_pairs={{0,2},{4,6},{8,10},{12,14},{16,18},{20,22},{24,26},{28,30},{2,0},{... | collective-permute-start | bytes 196616 | tf_op jit(solution)/shard_map/ppermute | solution.py:557
  13.9 0.0 copy-done.3
  13.9 1.3 %collective-permute-start.2 = (bf16[2,32,512]{2,1,0:T(8,128)(2,1)S(1)}, bf16[2,32,512]{2,1,0:T(8,128)(2,1)}, u32[]{:S(2)}, u32[]{:S(2)}) collective-permute-start(bf16[2,32,512]{2,1,0:T(8,128)(2,1)S(1)} %copy-done.3), channel_id=1, source_target_pairs={{2,4},{6,8},{10,12},{14,16},{18,20},{22,24},{26,28},{4,2},{8,6},{1... | collective-permute-start | bytes 196616 | tf_op jit(solution)/shard_map/ppermute | solution.py:557
  15.2 2.6 %operators_of_lists.1 = (bf16[4096,256]{1,0:T(8,128)(2,1)S(1)}, s16[4096,128]{1,0:T(8,128)(2,1)S(1)}) custom-call(s32[8,512]{1,0:T(8,128)} %bitcast.35, s32[8,512]{1,0:T(8,128)} %bitcast.36, s32[1,512]{1,0:T(1,128)} %bitcast.39, bf16[316,2,128]{2,1,0:T(2,128)(2,1)} %bitcast.34), custom_call_target="tpu_custom_call" | custom-call | flops 662700032 | bytes 1048576 | tf_op jit(solution)/shard_map/operators_of_lists/pallas_call | solution.py:51
  17.8 3.0 %all-to-all-done = bf16[16,32,256]{2,1,0:T(8,128)(2,1)S(1)} async-done(((bf16[16,32,256]{2,1,0:T(8,128)(2,1)}), bf16[16,32,256]{2,1,0:T(8,128)(2,1)S(1)}, u32[]{:S(2)}, u32[]{:S(2)}) %all-to-all-start) | async-done | bytes 262176 | tf_op jit(solution)/shard_map/all_to_all | solution.py:544
  20.8 2.3 %parent_sums.1 = bf16[512,256]{1,0:T(8,128)(2,1)} custom-call(bf16[512,256]{1,0:T(8,128)(2,1)S(1)} %bitcast.23, s16[4096,128]{1,0:T(8,128)(2,1)S(1)} %get-tuple-element.28.refs_1_, bf16[4096,256]{1,0:T(8,128)(2,1)S(1)} %get-tuple-element.29.refs_2_), custom_call_target="tpu_custom_call" | custom-call | flops 1073741824 | bytes 1048576 | tf_op jit(solution)/shard_map/parent_sums/pallas_call | solution.py:51
  23.1 0.0 copy-start
  23.1 0.0 copy-start.1
  23.2 0.0 copy-start.2
  23.2 0.0 collective-permute-done.1.refs_1_
  23.2 0.0 collective-permute-done.2.refs_2_
  23.2 6.2 %all-to-all-start.1 = ((bf16[16,32,256]{2,1,0:T(8,128)(2,1)}), bf16[16,32,256]{2,1,0:T(8,128)(2,1)S(1)}, u32[]{:S(2)}, u32[]{:S(2)}) async-start(bf16[16,32,256]{2,1,0:T(8,128)(2,1)} %bitcast.29), calls=%async_computation.1 | async-start | bytes 524288 | tf_op jit(solution)/shard_map/all_to_all | solution.py:544
  29.4 4.4 %near_sums.1 = (f32[2,512,128]{2,1,0:T(8,128)S(1)}, f32[16,2048]{1,0:T(8,128)S(1)}) custom-call(bf16[2,512,128]{2,1,0:T(8,128)(2,1)} %bitcast.32, bf16[2,32,512]{2,1,0:T(8,128)(2,1)} %collective-permute-done.1.refs_1_, bf16[2,32,512]{2,1,0:T(8,128)(2,1)} %collective-permute-done.2.refs_2_, s32[8,128]{1,0:T(8,128)} %bitcast.37, s32[8,128]{1,0:T(8,128)} %bitcast.38, ...), custom_call_target="tpu_custom_call" | custom-call | flops 1199570944 | bytes 1048576 | tf_op jit(solution)/shard_map/near_sums/pallas_call | solution.py:51
  33.8 1.1 %all-to-all-done.1 = bf16[16,32,256]{2,1,0:T(8,128)(2,1)S(1)} async-done(((bf16[16,32,256]{2,1,0:T(8,128)(2,1)}), bf16[16,32,256]{2,1,0:T(8,128)(2,1)S(1)}, u32[]{:S(2)}, u32[]{:S(2)}) %all-to-all-start.1) | async-done | bytes 262176 | tf_op jit(solution)/shard_map/all_to_all | solution.py:544
  34.9 0.0 copy-done
  34.9 0.0 copy-done.1
  34.9 0.0 copy-done.2
  35.0 1.1 %lower.1 = (bf16[256,2048]{1,0:T(8,128)(2,1)S(1)}, bf16[2,2,64,128]{3,2,1,0:T(8,128)(2,1)S(1)}) custom-call(bf16[512,256]{1,0:T(8,128)(2,1)S(1)} %bitcast.22, s32[1,128]{1,0:T(1,128)S(1)} %bitcast.27, s32[1,128]{1,0:T(1,128)S(1)} %bitcast.25, f32[16,2048]{1,0:T(8,128)S(1)} %get-tuple-element.37.refs_3_, bf16[640,2048]{1,0:T(8,128)(2,1)S(1)} %copy-done), custom_call_target="tpu_custom_call" | custom-call | flops 134217728 | bytes 1048576 | tf_op jit(solution)/shard_map/lower/pallas_call | solution.py:51
  36.0 0.1 collective-permute-start.3
  36.1 0.7 %anterpolate.1.refs_0_ = f32[2,512,128]{2,1,0:T(8,128)S(1)} custom-call(bf16[640,2048]{1,0:T(8,128)(2,1)S(1)} %copy-done, bf16[256,2048]{1,0:T(8,128)(2,1)S(1)} %get-tuple-element.38.refs_1_, f32[2,512,128]{2,1,0:T(8,128)S(1)} %get-tuple-element.39.refs_2_), custom_call_target="tpu_custom_call" | custom-call | flops 536870912 | bytes 1048576 | tf_op jit(solution)/shard_map/anterpolate/pallas_call | solution.py:51
  36.9 0.5 %collective-permute-done.3.refs_1_ = bf16[2,2,64,128]{3,2,1,0:T(8,128)(2,1)S(1)} collective-permute-done((bf16[2,2,64,128]{3,2,1,0:T(8,128)(2,1)S(1)}, bf16[2,2,64,128]{3,2,1,0:T(8,128)(2,1)S(1)}, u32[]{:S(2)}, u32[]{:S(2)}) %collective-permute-start.3) | collective-permute-done | bytes 65568 | tf_op jit(solution)/shard_map/ppermute | solution.py:551
  37.4 0.7 %finish.1 = bf16[2,512,128]{2,1,0:T(8,128)(2,1)} custom-call(f32[2,512,128]{2,1,0:T(8,128)S(1)} %anterpolate.1.refs_0_, bf16[2,2,64,128]{3,2,1,0:T(8,128)(2,1)S(1)} %collective-permute-done.3.refs_1_), custom_call_target="tpu_custom_call" | custom-call | flops 1048576 | bytes 1048576 | tf_op jit(solution)/shard_map/finish/pallas_call | solution.py:51
Async XLA Ops:
  0.0 2.5 %collective-permute-start = (bf16[2,512,128]{2,1,0:T(8,128)(2,1)}, bf16[2,512,128]{2,1,0:T(8,128)(2,1)S(1)}, u32[]{:S(2)}, u32[]{:S(2)}) collective-permute-start(bf16[2,512,128]{2,1,0:T(8,128)(2,1)} %bitcast.30), channel_id=1, source_target_pairs={{0,1},{1,0},{2,3},{3,2},{4,5},{5,4},{6,7},{7,6},{8,9},{9,8},{10,11... | collective-permute-start | bytes 786440 | tf_op jit(solution)/shard_map/ppermute | solution.py:551
  2.5 10.8 %copy-start.4 = (bf16[2,32,512]{2,1,0:T(8,128)(2,1)S(1)}, bf16[2,32,512]{2,1,0:T(8,128)(2,1)}, u32[]{:S(2)}) copy-start(bf16[2,32,512]{2,1,0:T(8,128)(2,1)} %get-tuple-element.30) | copy-start | bytes 196612
  2.5 11.4 %copy-start.3 = (bf16[2,32,512]{2,1,0:T(8,128)(2,1)S(1)}, bf16[2,32,512]{2,1,0:T(8,128)(2,1)}, u32[]{:S(2)}) copy-start(bf16[2,32,512]{2,1,0:T(8,128)(2,1)} %get-tuple-element.31) | copy-start | bytes 196612
  4.9 15.9 %all-to-all-start = ((bf16[16,32,256]{2,1,0:T(8,128)(2,1)}), bf16[16,32,256]{2,1,0:T(8,128)(2,1)S(1)}, u32[]{:S(2)}, u32[]{:S(2)}) async-start(bf16[16,32,256]{2,1,0:T(8,128)(2,1)} %bitcast.28), calls=%async_computation | async-start | bytes 524288 | tf_op jit(solution)/shard_map/all_to_all | solution.py:544
  13.2 9.9 %collective-permute-start.1 = (bf16[2,32,512]{2,1,0:T(8,128)(2,1)S(1)}, bf16[2,32,512]{2,1,0:T(8,128)(2,1)}, u32[]{:S(2)}, u32[]{:S(2)}) collective-permute-start(bf16[2,32,512]{2,1,0:T(8,128)(2,1)S(1)} %copy-done.4), channel_id=1, source_target_pairs={{0,2},{4,6},{8,10},{12,14},{16,18},{20,22},{24,26},{28,30},{2,0},{... | collective-permute-start | bytes 196616 | tf_op jit(solution)/shard_map/ppermute | solution.py:557
  13.9 9.3 %collective-permute-start.2 = (bf16[2,32,512]{2,1,0:T(8,128)(2,1)S(1)}, bf16[2,32,512]{2,1,0:T(8,128)(2,1)}, u32[]{:S(2)}, u32[]{:S(2)}) collective-permute-start(bf16[2,32,512]{2,1,0:T(8,128)(2,1)S(1)} %copy-done.3), channel_id=1, source_target_pairs={{2,4},{6,8},{10,12},{14,16},{18,20},{22,24},{26,28},{4,2},{8,6},{1... | collective-permute-start | bytes 196616 | tf_op jit(solution)/shard_map/ppermute | solution.py:557
  23.1 11.8 %copy-start = (bf16[640,2048]{1,0:T(8,128)(2,1)S(1)}, bf16[640,2048]{1,0:T(8,128)(2,1)}, u32[]{:S(2)}) copy-start(bf16[640,2048]{1,0:T(8,128)(2,1)} %refs_0_.1) | copy-start | bytes 7864324
  23.1 11.8 %copy-start.1 = (s32[128]{0:T(128)S(1)}, s32[128]{0:T(128)}, u32[]{:S(2)}) copy-start(s32[128]{0:T(128)} %param.15) | copy-start | bytes 1540
  23.2 11.8 %copy-start.2 = (s32[128]{0:T(128)S(1)}, s32[128]{0:T(128)}, u32[]{:S(2)}) copy-start(s32[128]{0:T(128)} %param.14) | copy-start | bytes 1540
  23.2 11.7 %all-to-all-start.1 = ((bf16[16,32,256]{2,1,0:T(8,128)(2,1)}), bf16[16,32,256]{2,1,0:T(8,128)(2,1)S(1)}, u32[]{:S(2)}, u32[]{:S(2)}) async-start(bf16[16,32,256]{2,1,0:T(8,128)(2,1)} %bitcast.29), calls=%async_computation.1 | async-start | bytes 524288 | tf_op jit(solution)/shard_map/all_to_all | solution.py:544
  36.0 1.3 %collective-permute-start.3 = (bf16[2,2,64,128]{3,2,1,0:T(8,128)(2,1)S(1)}, bf16[2,2,64,128]{3,2,1,0:T(8,128)(2,1)S(1)}, u32[]{:S(2)}, u32[]{:S(2)}) collective-permute-start(bf16[2,2,64,128]{3,2,1,0:T(8,128)(2,1)S(1)} %get-tuple-element.40), channel_id=1, source_target_pairs={{0,1},{1,0},{2,3},{3,2},{4,5},{5,4},{6,7},{7,6},{8,9},{9,8},{10,11... | collective-permute-start | bytes 196616 | tf_op jit(solution)/shard_map/ppermute | solution.py:551
